TPU v7x, 32 devices: a whole 2x2x4 slice. The times are simulated.
32 devices in a mesh: wide: 8 (over z, x), narrow: 4 (over y, core).
Axes of the slice: x: 2, y: 2, z: 4, core: 2. Of those that a mesh axis runs over, the one named last changes fastest.
Arguments:
- inputs: bfloat16 [64, 512, 512], P(('wide', 'narrow')), may hold values from -6 to 6
- segment_ids: int32 [64, 512], P(('wide', 'narrow')), may hold values from 0 to 7, never falling along the last dimension, each value on 1 to 256 neighbouring positions
- cotangent: bfloat16 [64, 512, 512], P(('wide', 'narrow')), may hold values from -6 to 6
- w_query: bfloat16 [512, 512], P('wide', 'narrow'), may hold values from -0.25 to 0.25
- w_key: bfloat16 [512, 512], P('wide', 'narrow'), may hold values from -0.25 to 0.25
- w_value: bfloat16 [512, 512], P('wide', 'narrow'), may hold values from -0.25 to 0.25
- w_out: bfloat16 [512, 512], P('wide', 'narrow'), may hold values from -0.75 to 0.75
- w_in: bfloat16 [512, 2048], P('wide', 'narrow'), may hold values from -0.25 to 0.25
- w_back: bfloat16 [2048, 512], P('wide', 'narrow'), may hold values from -0.125 to 0.125
- position_table: bfloat16 [512, 512], P('wide', 'narrow'), may hold values from -3 to 3
- vectors: bfloat16 [8, 512], P('narrow', 'wide'), may hold values from -1.25 to 1.625, as said below
- in_bias: bfloat16 [2048], P(('wide', 'narrow')), may hold values from -3 to 3
Outputs:
- layer_output: bfloat16 [64, 512, 512], P(('wide', 'narrow'))
- input_grad: bfloat16 [64, 512, 512], P(('wide', 'narrow'))
- grad_query: float32 [512, 512], P('wide', 'narrow')
- grad_key: float32 [512, 512], P('wide', 'narrow')
- grad_value: float32 [512, 512], P('wide', 'narrow')
- grad_out: float32 [512, 512], P('wide', 'narrow')
- grad_in: float32 [512, 2048], P('wide', 'narrow')
- grad_back: float32 [2048, 512], P('wide', 'narrow')
- grad_table: float32 [512, 512], P('wide', 'narrow')
- grad_vectors: float32 [8, 512], P('narrow', 'wide')
- grad_in_bias: float32 [2048], P(('wide', 'narrow'))
Inputs may be any that keep to these rules, and one draw needn't show every extreme that they name: `segment_ids`: within each window of 512 characters the ids never fall; a document spans 1 to 256 characters, and document lengths are heavy-tailed. `vectors`: rows 4 and 6 (the norms' gains) lie from 0.375 to 1.625, the other rows from -1.25 to 1.25.
All inputs are finite; a program needn't handle non-finite values.
Results may differ from a plain program's by a relative error of at most 0.015.
The roundings to bfloat16 on the way count: a program that leaves them out, or rounds other values in their place, can miss the bound.
Values may be sent and summed in bfloat16 or wider, within the bound.
No kernel may reach another device: no remote copies, remote signals or barrier semaphores. Data moves between devices by JAX's collectives and lax.ppermute only.
A program may use at most 128 MiB of HBM per device.

v0:
```python
from functools import partial
import math

import jax
import jax.numpy as jnp
from jax import lax
from jax.sharding import PartitionSpec as P

HEADS = 8


EPSILON = 1e-05


def product(left, right):
    return jnp.dot(left, right, preferred_element_type=jnp.float32)


def cross_product(left, right):
    return lax.dot_general(
        left, right, (((0,), (0,)), ((), ())), preferred_element_type=jnp.float32
    )


def product_back(left, right):
    return lax.dot_general(
        left, right, (((1,), (1,)), ((), ())), preferred_element_type=jnp.float32
    )


def norm_apply(values, gains, offset):
    average = jnp.mean(values, axis=-1, keepdims=True)
    centred = values - average
    variance = jnp.mean(centred * centred, axis=-1, keepdims=True)
    return centred * lax.rsqrt(variance + EPSILON) * gains + offset


def window_mask(segments):
    places = lax.iota(jnp.int32, segments.shape[0])
    return (places[:, None] >= places[None, :]) & (segments[:, None] == segments[None, :])


def attend(window_item, scaling):
    queries, key_rows, value_rows, segments = window_item
    allowed = window_mask(segments)[None]
    scores = (
        jnp.einsum("qhe,khe->hqk", queries, key_rows, preferred_element_type=jnp.float32) * scaling
    )
    scores = jnp.where(allowed, scores, -1e30)
    row_peak = jnp.max(scores, axis=-1, keepdims=True)
    weight = jnp.exp(scores - row_peak)
    totals = jnp.sum(weight, axis=-1, keepdims=True)
    shares = (weight / totals).astype(jnp.bfloat16)
    attended = jnp.einsum("hqk,khe->qhe", shares, value_rows, preferred_element_type=jnp.float32)
    return (attended.astype(jnp.bfloat16), row_peak + jnp.log(totals))


def attend_back(window_item, scaling):
    queries, key_rows, value_rows, segments, log_total, grad_attended = window_item
    allowed = window_mask(segments)[None]
    scores = (
        jnp.einsum("qhe,khe->hqk", queries, key_rows, preferred_element_type=jnp.float32) * scaling
    )
    scores = jnp.where(allowed, scores, -1e30)
    shares_f = jnp.exp(scores - log_total)
    shares = shares_f.astype(jnp.bfloat16)
    grad_values = jnp.einsum(
        "hqk,qhe->khe", shares, grad_attended, preferred_element_type=jnp.float32
    )
    grad_shares = jnp.einsum(
        "qhe,khe->hqk", grad_attended, value_rows, preferred_element_type=jnp.float32
    )
    grad_scores = shares_f * (grad_shares - jnp.sum(shares_f * grad_shares, axis=-1, keepdims=True))
    grad_scores = grad_scores.astype(jnp.bfloat16)
    grad_queries = (
        jnp.einsum("hqk,khe->qhe", grad_scores, key_rows, preferred_element_type=jnp.float32)
        * scaling
    )
    grad_keys = (
        jnp.einsum("hqk,qhe->khe", grad_scores, queries, preferred_element_type=jnp.float32)
        * scaling
    )
    return (
        grad_queries.astype(jnp.bfloat16),
        grad_keys.astype(jnp.bfloat16),
        grad_values.astype(jnp.bfloat16),
    )


def forward_local(inputs, segment_ids, parameters):
    w_query, w_key, w_value, w_out, w_in, w_back, position_table, vectors, in_bias = parameters
    vectors_f = vectors.astype(jnp.float32)
    windows, positions, features = inputs.shape
    head_shape = (windows, positions, HEADS, features // HEADS)
    scaling = 1.0 / math.sqrt(features // HEADS)
    passed = (inputs.astype(jnp.float32) + position_table.astype(jnp.float32)[None]).reshape(
        windows * positions, features
    )
    mixed_low = passed.astype(jnp.bfloat16)
    queries = (product(mixed_low, w_query) + vectors_f[0]).astype(jnp.bfloat16)
    key_rows = product(mixed_low, w_key).astype(jnp.bfloat16)
    value_rows = (product(mixed_low, w_value) + vectors_f[1]).astype(jnp.bfloat16)
    attended, log_total = lax.map(
        partial(attend, scaling=scaling),
        (
            queries.reshape(head_shape),
            key_rows.reshape(head_shape),
            value_rows.reshape(head_shape),
            segment_ids,
        ),
    )
    attended = attended.reshape(windows * positions, features)
    first_sum = passed + product(attended, w_out) + vectors_f[2]
    hidden = norm_apply(first_sum, vectors_f[4], vectors_f[5])
    hidden_low = hidden.astype(jnp.bfloat16)
    pre_act = product(hidden_low, w_in) + in_bias.astype(jnp.float32)
    active = jax.nn.gelu(pre_act).astype(jnp.bfloat16)
    second_sum = hidden + product(active, w_back) + vectors_f[3]
    result = norm_apply(second_sum, vectors_f[6], vectors_f[7])
    saved = (
        mixed_low,
        queries,
        key_rows,
        value_rows,
        attended,
        log_total,
        first_sum,
        hidden_low,
        pre_act,
        active,
        second_sum,
    )
    return (result.reshape(windows, positions, features), saved)


def backward_local(cotangent, segment_ids, parameters, saved):
    w_query, w_key, w_value, w_out, w_in, w_back, position_table, vectors, in_bias = parameters
    (
        mixed_low,
        queries,
        key_rows,
        value_rows,
        attended,
        log_total,
        first_sum,
        hidden_low,
        pre_act,
        active,
        second_sum,
    ) = saved
    vectors_f = vectors.astype(jnp.float32)
    windows, positions, features = cotangent.shape
    head_shape = (windows, positions, HEADS, features // HEADS)
    scaling = 1.0 / math.sqrt(features // HEADS)
    grad_output = cotangent.astype(jnp.float32).reshape(windows * positions, features)
    unused_second, pull_second = jax.vjp(norm_apply, second_sum, vectors_f[6], vectors_f[7])
    grad_second, grad_gain_two, grad_offset_two = pull_second(grad_output)
    grad_ffn = grad_second.astype(jnp.bfloat16)
    grad_back = cross_product(active, grad_ffn)
    grad_bias_two = jnp.sum(grad_ffn.astype(jnp.float32), axis=0)
    grad_active = product_back(grad_ffn, w_back)
    unused_gelu, pull_gelu = jax.vjp(jax.nn.gelu, pre_act)
    grad_pre = pull_gelu(grad_active)[0].astype(jnp.bfloat16)
    grad_in = cross_product(hidden_low, grad_pre)
    grad_in_bias = jnp.sum(grad_pre.astype(jnp.float32), axis=0)
    grad_hidden = grad_second + product_back(grad_pre, w_in)
    unused_first, pull_first = jax.vjp(norm_apply, first_sum, vectors_f[4], vectors_f[5])
    grad_first, grad_gain_one, grad_offset_one = pull_first(grad_hidden)
    grad_branch = grad_first.astype(jnp.bfloat16)
    grad_out = cross_product(attended, grad_branch)
    grad_bias_out = jnp.sum(grad_branch.astype(jnp.float32), axis=0)
    grad_attended = product_back(grad_branch, w_out).astype(jnp.bfloat16)
    grad_queries, grad_keys, grad_values = lax.map(
        partial(attend_back, scaling=scaling),
        (
            queries.reshape(head_shape),
            key_rows.reshape(head_shape),
            value_rows.reshape(head_shape),
            segment_ids,
            log_total,
            grad_attended.reshape(head_shape),
        ),
    )
    grad_queries = grad_queries.reshape(windows * positions, features)
    grad_keys = grad_keys.reshape(windows * positions, features)
    grad_values = grad_values.reshape(windows * positions, features)
    grad_query = cross_product(mixed_low, grad_queries)
    grad_key = cross_product(mixed_low, grad_keys)
    grad_value = cross_product(mixed_low, grad_values)
    grad_stream = (
        grad_first
        + product_back(grad_queries, w_query)
        + product_back(grad_keys, w_key)
        + product_back(grad_values, w_value)
    )
    grad_stream = grad_stream.reshape(windows, positions, features)
    grad_table = jnp.sum(grad_stream, axis=0)
    grad_vectors = jnp.stack(
        [
            jnp.sum(grad_queries.astype(jnp.float32), axis=0),
            jnp.sum(grad_values.astype(jnp.float32), axis=0),
            grad_bias_out,
            grad_bias_two,
            grad_gain_one,
            grad_offset_one,
            grad_gain_two,
            grad_offset_two,
        ]
    )
    gradients = (
        grad_query,
        grad_key,
        grad_value,
        grad_out,
        grad_in,
        grad_back,
        grad_table,
        grad_vectors,
        grad_in_bias,
    )
    return (gradients, grad_stream)


def per_device(
    inputs,
    segment_ids,
    cotangent,
    w_query,
    w_key,
    w_value,
    w_out,
    w_in,
    w_back,
    position_table,
    vectors,
    in_bias,
):
    narrow_parts = (
        lax.all_gather(w_query, "narrow", axis=1, tiled=True),
        lax.all_gather(w_key, "narrow", axis=1, tiled=True),
        lax.all_gather(w_value, "narrow", axis=1, tiled=True),
        lax.all_gather(w_out, "narrow", axis=1, tiled=True),
        lax.all_gather(w_in, "narrow", axis=1, tiled=True),
        lax.all_gather(w_back, "narrow", axis=1, tiled=True),
        lax.all_gather(position_table, "narrow", axis=1, tiled=True),
        lax.all_gather(vectors, "narrow", axis=0, tiled=True),
        lax.all_gather(in_bias, "narrow", axis=0, tiled=True),
    )
    gathered = (
        lax.all_gather(narrow_parts[0], "wide", axis=0, tiled=True),
        lax.all_gather(narrow_parts[1], "wide", axis=0, tiled=True),
        lax.all_gather(narrow_parts[2], "wide", axis=0, tiled=True),
        lax.all_gather(narrow_parts[3], "wide", axis=0, tiled=True),
        lax.all_gather(narrow_parts[4], "wide", axis=0, tiled=True),
        lax.all_gather(narrow_parts[5], "wide", axis=0, tiled=True),
        lax.all_gather(narrow_parts[6], "wide", axis=0, tiled=True),
        lax.all_gather(narrow_parts[7], "wide", axis=1, tiled=True),
        lax.all_gather(narrow_parts[8], "wide", axis=0, tiled=True),
    )
    layer_output, saved = forward_local(inputs, segment_ids, gathered)
    narrow_again = (
        lax.all_gather(w_query, "narrow", axis=1, tiled=True),
        lax.all_gather(w_key, "narrow", axis=1, tiled=True),
        lax.all_gather(w_value, "narrow", axis=1, tiled=True),
        lax.all_gather(w_out, "narrow", axis=1, tiled=True),
        lax.all_gather(w_in, "narrow", axis=1, tiled=True),
        lax.all_gather(w_back, "narrow", axis=1, tiled=True),
        lax.all_gather(position_table, "narrow", axis=1, tiled=True),
        lax.all_gather(vectors, "narrow", axis=0, tiled=True),
        lax.all_gather(in_bias, "narrow", axis=0, tiled=True),
    )
    gathered_again = (
        lax.all_gather(narrow_again[0], "wide", axis=0, tiled=True),
        lax.all_gather(narrow_again[1], "wide", axis=0, tiled=True),
        lax.all_gather(narrow_again[2], "wide", axis=0, tiled=True),
        lax.all_gather(narrow_again[3], "wide", axis=0, tiled=True),
        lax.all_gather(narrow_again[4], "wide", axis=0, tiled=True),
        lax.all_gather(narrow_again[5], "wide", axis=0, tiled=True),
        lax.all_gather(narrow_again[6], "wide", axis=0, tiled=True),
        lax.all_gather(narrow_again[7], "wide", axis=1, tiled=True),
        lax.all_gather(narrow_again[8], "wide", axis=0, tiled=True),
    )
    unused_output, saved_again = forward_local(inputs, segment_ids, gathered_again)
    gradients, grad_stream = backward_local(cotangent, segment_ids, gathered_again, saved_again)
    wide_sums = (
        lax.psum_scatter(gradients[0], "wide", scatter_dimension=0, tiled=True),
        lax.psum_scatter(gradients[1], "wide", scatter_dimension=0, tiled=True),
        lax.psum_scatter(gradients[2], "wide", scatter_dimension=0, tiled=True),
        lax.psum_scatter(gradients[3], "wide", scatter_dimension=0, tiled=True),
        lax.psum_scatter(gradients[4], "wide", scatter_dimension=0, tiled=True),
        lax.psum_scatter(gradients[5], "wide", scatter_dimension=0, tiled=True),
        lax.psum_scatter(gradients[6], "wide", scatter_dimension=0, tiled=True),
        lax.psum_scatter(gradients[7], "wide", scatter_dimension=1, tiled=True),
        lax.psum_scatter(gradients[8], "wide", scatter_dimension=0, tiled=True),
    )
    owned = (
        lax.psum_scatter(
            wide_sums[0].astype(jnp.bfloat16), "narrow", scatter_dimension=1, tiled=True
        ).astype(jnp.float32),
        lax.psum_scatter(
            wide_sums[1].astype(jnp.bfloat16), "narrow", scatter_dimension=1, tiled=True
        ).astype(jnp.float32),
        lax.psum_scatter(
            wide_sums[2].astype(jnp.bfloat16), "narrow", scatter_dimension=1, tiled=True
        ).astype(jnp.float32),
        lax.psum_scatter(
            wide_sums[3].astype(jnp.bfloat16), "narrow", scatter_dimension=1, tiled=True
        ).astype(jnp.float32),
        lax.psum_scatter(
            wide_sums[4].astype(jnp.bfloat16), "narrow", scatter_dimension=1, tiled=True
        ).astype(jnp.float32),
        lax.psum_scatter(
            wide_sums[5].astype(jnp.bfloat16), "narrow", scatter_dimension=1, tiled=True
        ).astype(jnp.float32),
        lax.psum_scatter(
            wide_sums[6].astype(jnp.bfloat16), "narrow", scatter_dimension=1, tiled=True
        ).astype(jnp.float32),
        lax.psum_scatter(
            wide_sums[7].astype(jnp.bfloat16), "narrow", scatter_dimension=0, tiled=True
        ).astype(jnp.float32),
        lax.psum_scatter(
            wide_sums[8].astype(jnp.bfloat16), "narrow", scatter_dimension=0, tiled=True
        ).astype(jnp.float32),
    )
    return (
        layer_output.astype(jnp.bfloat16),
        grad_stream.astype(jnp.bfloat16),
        owned[0],
        owned[1],
        owned[2],
        owned[3],
        owned[4],
        owned[5],
        owned[6],
        owned[7],
        owned[8],
    )


def solution(mesh):
    placed = (
        P(("wide", "narrow"), None, None),
        P(("wide", "narrow"), None),
        P(("wide", "narrow"), None, None),
        P("wide", "narrow"),
        P("wide", "narrow"),
        P("wide", "narrow"),
        P("wide", "narrow"),
        P("wide", "narrow"),
        P("wide", "narrow"),
        P("wide", "narrow"),
        P("narrow", "wide"),
        P(("wide", "narrow")),
    )
    return jax.shard_map(
        per_device,
        mesh=mesh,
        in_specs=placed,
        out_specs=(
            P(("wide", "narrow"), None, None),
            P(("wide", "narrow"), None, None),
            P("wide", "narrow"),
            P("wide", "narrow"),
            P("wide", "narrow"),
            P("wide", "narrow"),
            P("wide", "narrow"),
            P("wide", "narrow"),
            P("wide", "narrow"),
            P("narrow", "wide"),
            P(("wide", "narrow")),
        ),
        check_vma=False,
    )
```

profile of v0, /device:TPU:0, one launch (start us, length us, event | category | flops | bytes accessed | tf_op | source)
XLA Modules:
  0.0 1122.1 jit_solution(6946857589563898973)
XLA Ops:
  28.3 26.7 %all-gather.1 = bf16[8,64,8]{1,2,0:T(8,128)(2,1)S(1)} all-gather(bf16[1,64,8]{1,2,0:T(8,128)(2,1)S(1)} %bitcast.335), channel_id=1, replica_groups=mesh['wide'=8,'narrow'=4] {'wide'}, dimensions={0}, use_global_device_ids=true | all-gather | bytes 9216 | tf_op jit(solution)/shard_map/all_gather | solution.py:257
  77.6 34.6 %all_gather.75 = bf16[512,512]{1,0:T(8,128)(2,1)} all-gather(bf16[64,512]{1,0:T(8,128)(2,1)S(1)} %all_gather.74), channel_id=1, replica_groups=mesh['wide'=8,'narrow'=4] {'wide'}, dimensions={0}, use_global_device_ids=true | all-gather | bytes 589824 | tf_op jit(solution)/shard_map/all_gather | solution.py:252
  112.2 32.2 %all_gather.81 = bf16[512,512]{1,0:T(8,128)(2,1)S(1)} all-gather(bf16[64,512]{1,0:T(8,128)(2,1)S(1)} %all_gather.80), channel_id=1, replica_groups=mesh['wide'=8,'narrow'=4] {'wide'}, dimensions={0}, use_global_device_ids=true | all-gather | bytes 589824 | tf_op jit(solution)/shard_map/all_gather | solution.py:251
  144.3 33.4 %all_gather.79 = bf16[512,512]{1,0:T(8,128)(2,1)} all-gather(bf16[64,512]{1,0:T(8,128)(2,1)S(1)} %all_gather.78), channel_id=1, replica_groups=mesh['wide'=8,'narrow'=4] {'wide'}, dimensions={0}, use_global_device_ids=true | all-gather | bytes 589824 | tf_op jit(solution)/shard_map/all_gather | solution.py:250
  177.7 31.2 %all_gather.73 = bf16[512,512]{1,0:T(8,128)(2,1)S(1)} all-gather(bf16[64,512]{1,0:T(8,128)(2,1)S(1)} %all_gather.72), channel_id=1, replica_groups=mesh['wide'=8,'narrow'=4] {'wide'}, dimensions={0}, use_global_device_ids=true | all-gather | bytes 589824 | tf_op jit(solution)/shard_map/all_gather | solution.py:256
  233.6 13.9 %while.37 = (s32[]{:T(128)}, bf16[2,512,8,64]{1,3,2,0:T(8,128)(2,1)}, f32[2,8,512,1]{2,1,3,0:T(8,128)S(1)}, bf16[2,512,8,64]{1,3,2,0:T(8,128)(2,1)S(1)}, s32[2,5...) while((s32[]{:T(128)}, ...), condition=%wide.region_11.12_spmd, body=%wide.region_8.11_spmd.sunk | while | flops 563081216 | bytes 36839580 | solution.py:103
  248.6 21.4 %while.36 = (s32[]{:T(128)}, bf16[2,512,8,64]{1,3,2,0:T(8,128)(2,1)}, bf16[2,512,8,64]{1,3,2,0:T(8,128)(2,1)S(1)}, s32[2,512]{1,0:T(2,128)S(1)}, bf16[2,512,8,64...) while((s32[]{:T(128)}, bf16[2,512,8,64]{1,3,2,0:T(8,128)(2,1)}, ...), condition=%wide.region_3.4_spmd, body=%wide.region_0.3_spmd.sunk | while | flops 550502912 | bytes 19439704 | solution.py:103
  277.7 18.7 %all-gather.2 = bf16[8,1,256]{2,1,0:T(2,128)(2,1)S(1)} all-gather(bf16[1,1,256]{2,1,0:T(2,128)(2,1)S(1)} %reshape.349), channel_id=1, replica_groups=mesh['wide'=8,'narrow'=4] {'wide'}, dimensions={0}, use_global_device_ids=true | all-gather | bytes 4608 | tf_op jit(solution)/shard_map/all_gather | solution.py:258
  305.8 31.3 %all_gather.83 = bf16[512,512]{1,0:T(8,128)(2,1)S(1)} all-gather(bf16[64,512]{1,0:T(8,128)(2,1)S(1)} %all_gather.82), channel_id=1, replica_groups=mesh['wide'=8,'narrow'=4] {'wide'}, dimensions={0}, use_global_device_ids=true | all-gather | bytes 589824 | tf_op jit(solution)/shard_map/all_gather | solution.py:253
  397.6 26.6 %while.38 = (s32[]{:T(128)}, bf16[2,512,8,64]{1,3,2,0:T(8,128)(2,1)}, bf16[2,512,8,64]{1,3,2,0:T(8,128)(2,1)}, bf16[2,512,8,64]{1,3,2,0:T(8,128)(2,1)}, bf16[2,5...) while((s32[]{:T(128)}, ...), condition=%wide.region_22.23_spmd, body=%wide.region_20.22_spmd.sunk | while | flops 1375727616 | bytes 98692424 | solution.py:173
  463.6 50.4 %reduce-scatter.30.cloned.1.call-done = f32[64,512]{1,0:T(8,128)} async-done(((f32[512,512]{1,0:T(8,128)}), f32[64,512]{1,0:T(8,128)}) %reduce-scatter.30.cloned.1.call-update) | async-done | bytes 131088 | tf_op jit(solution)/shard_map/reduce_scatter | solution.py:286
  515.8 63.9 %reduce-scatter.34.cloned.1.call-done = f32[64,512]{1,0:T(8,128)} async-done(((f32[512,512]{1,0:T(8,128)}), f32[64,512]{1,0:T(8,128)}) %reduce-scatter.34.cloned.1.call-update) | async-done | bytes 131088 | tf_op jit(solution)/shard_map/reduce_scatter | solution.py:288
  581.5 64.3 %reduce-scatter.32.cloned.1.call-done = f32[64,512]{1,0:T(8,128)} async-done(((f32[512,512]{1,0:T(8,128)}), f32[64,512]{1,0:T(8,128)}) %reduce-scatter.32.cloned.1.call-update) | async-done | bytes 131088 | tf_op jit(solution)/shard_map/reduce_scatter | solution.py:287
  647.5 64.1 %reduce-scatter.44.cloned.1.call-done = f32[64,512]{1,0:T(8,128)} async-done(((f32[512,512]{1,0:T(8,128)}), f32[64,512]{1,0:T(8,128)}) %reduce-scatter.44.cloned.1.call-update) | async-done | bytes 131088 | tf_op jit(solution)/shard_map/reduce_scatter | solution.py:292
  713.4 89.3 %reduce-scatter.42.cloned.1.call-done = f32[256,512]{1,0:T(8,128)} async-done(((f32[2048,512]{1,0:T(8,128)}), f32[256,512]{1,0:T(8,128)}) %reduce-scatter.42.cloned.1.call-update) | async-done | bytes 524304 | tf_op jit(solution)/shard_map/reduce_scatter | solution.py:291
  804.7 89.3 %reduce-scatter.38.cloned.1.call-done = f32[64,2048]{1,0:T(8,128)} async-done(((f32[512,2048]{1,0:T(8,128)}), f32[64,2048]{1,0:T(8,128)}) %reduce-scatter.38.cloned.1.call-update) | async-done | bytes 524304 | tf_op jit(solution)/shard_map/reduce_scatter | solution.py:290
  898.4 20.4 %all-reduce.2 = bf16[2048]{0:T(1024)(128)(2,1)S(1)} all-reduce(f32[2048]{0:T(1024)S(1)} %get-tuple-element.326), channel_id=18, replica_groups=mesh['wide'=8,'narrow'=4] {'wide'}, use_global_device_ids=true, to_apply=%region_49.50.clone | all-reduce | flops 2048 | bytes 12288
  918.9 39.7 %reduce-scatter.58.cloned.1.call-done = f32[64,8]{1,0:T(8,128)} async-done(((f32[512,8]{1,0:T(8,128)}), f32[64,8]{1,0:T(8,128)}) %reduce-scatter.58.cloned.1.call-update) | async-done | bytes 2064
  981.3 21.0 %reduce-scatter.46.cloned.1.call-done = bf16[128,64]{1,0:T(8,128)(2,1)} async-done(((bf16[512,64]{1,0:T(8,128)(2,1)}), bf16[128,64]{1,0:T(8,128)(2,1)}) %reduce-scatter.46.cloned.1.call-update) | async-done | bytes 16400
  1003.8 20.7 %reduce-scatter.50.cloned.1.call-done = bf16[128,64]{1,0:T(8,128)(2,1)} async-done(((bf16[512,64]{1,0:T(8,128)(2,1)}), bf16[128,64]{1,0:T(8,128)(2,1)}) %reduce-scatter.50.cloned.1.call-update) | async-done | bytes 16400
  1026.0 21.0 %reduce-scatter.48.cloned.1.call-done = bf16[128,64]{1,0:T(8,128)(2,1)} async-done(((bf16[512,64]{1,0:T(8,128)(2,1)}), bf16[128,64]{1,0:T(8,128)(2,1)}) %reduce-scatter.48.cloned.1.call-update) | async-done | bytes 16400
  1048.4 20.5 %reduce-scatter.56.cloned.1.call-done = bf16[128,64]{1,0:T(8,128)(2,1)} async-done(((bf16[512,64]{1,0:T(8,128)(2,1)}), bf16[128,64]{1,0:T(8,128)(2,1)}) %reduce-scatter.56.cloned.1.call-update) | async-done | bytes 16400
  1070.4 20.9 %reduce-scatter.54.cloned.1.call-done = bf16[128,256]{1,0:T(8,128)(2,1)} async-done(((bf16[512,256]{1,0:T(8,128)(2,1)}), bf16[128,256]{1,0:T(8,128)(2,1)}) %reduce-scatter.54.cloned.1.call-update) | async-done | bytes 65552
  1093.0 20.9 %reduce-scatter.40.cloned.1.call-done = bf16[64,512]{1,0:T(8,128)(2,1)} async-done(((bf16[64,2048]{1,0:T(8,128)(2,1)}), bf16[64,512]{1,0:T(8,128)(2,1)}) %reduce-scatter.40.cloned.1.call-update) | async-done | bytes 65552 | tf_op jit(solution)/shard_map/reduce_scatter | solution.py:309
  (332 shorter events, 289.2 us)
Async XLA Ops:
  7.2 333.9 %all-gather.6.cloned.1.call-start = ((), (), s32[]{:S(2)}) async-start(), calls=%async_computation.15 | async-start | bytes 2359296 | tf_op jit(solution)/shard_map/all_gather | solution.py:254
  16.1 325.0 %all-gather.8.cloned.1.call-start = ((), (), s32[]{:S(2)}) async-start(), calls=%async_computation.16 | async-start | bytes 2359296 | tf_op jit(solution)/shard_map/all_gather | solution.py:255
  23.0 438.8 %reduce-scatter.36.cloned.1.call-start = ((), (), s32[]{:S(2)}) async-start(), calls=%async_computation.20 | async-start | bytes 1179648 | tf_op jit(solution)/shard_map/reduce_scatter | solution.py:289
  61.1 147.9 %copy-start.33 = (bf16[2,512,512]{2,1,0:T(8,128)(2,1)S(1)}, bf16[2,512,512]{2,1,0:T(8,128)(2,1)}, u32[]{:S(2)}) copy-start(bf16[2,512,512]{2,1,0:T(8,128)(2,1)} %param.18) | copy-start | bytes 3145732
  144.3 67.5 %copy-start.30 = (bf16[512,512]{1,0:T(8,128)(2,1)}, bf16[512,512]{1,0:T(8,128)(2,1)S(1)}, u32[]{:S(2)}) copy-start(bf16[512,512]{1,0:T(8,128)(2,1)S(1)} %all_gather.81) | copy-start | bytes 1572868
  248.6 22.6 %copy-start.54 = (bf16[64]{0:T(256)(128)(2,1)S(1)}, bf16[64]{0:T(256)(128)(2,1)}, u32[]{:S(2)}) copy-start(bf16[64]{0:T(256)(128)(2,1)} %param.29) | copy-start | bytes 388
  299.1 37.9 %copy-start.4 = (f32[2,512,512]{2,1,0:T(8,128)S(1)}, f32[2,512,512]{2,1,0:T(8,128)}, u32[]{:S(2)}) copy-start(f32[2,512,512]{2,1,0:T(8,128)} %copy-done.3) | copy-start | bytes 6291460
  299.1 37.9 %copy-start.45 = (f32[1,512]{1,0:T(1,128)S(1)}, f32[1,512]{1,0:T(1,128)}, u32[]{:S(2)}) copy-start(f32[1,512]{1,0:T(1,128)} %get-tuple-element.307) | copy-start | bytes 6148
  300.5 37.4 %copy-start.27 = (bf16[64,8,2,512]{3,1,2,0:T(8,128)(2,1)}, bf16[64,8,2,512]{3,1,2,0:T(8,128)(2,1)S(1)}, u32[]{:S(2)}) copy-start(bf16[64,8,2,512]{3,1,2,0:T(8,128)(2,1)S(1)} %copy.140) | copy-start | bytes 3145732
  386.9 127.1 %reduce-scatter.30.cloned.1.call-start = ((), (), s32[]{:S(2)}) async-start(), calls=%async_computation.17 | async-start | bytes 1179648 | tf_op jit(solution)/shard_map/reduce_scatter | solution.py:286
  428.7 151.0 %reduce-scatter.34.cloned.1.call-start = ((), (), s32[]{:S(2)}) async-start(), calls=%async_computation.19 | async-start | bytes 1179648 | tf_op jit(solution)/shard_map/reduce_scatter | solution.py:288
  431.9 213.9 %reduce-scatter.32.cloned.1.call-start = ((), (), s32[]{:S(2)}) async-start(), calls=%async_computation.18 | async-start | bytes 1179648 | tf_op jit(solution)/shard_map/reduce_scatter | solution.py:287
  436.4 275.3 %reduce-scatter.44.cloned.1.call-start = ((), (), s32[]{:S(2)}) async-start(), calls=%async_computation.24 | async-start | bytes 1179648 | tf_op jit(solution)/shard_map/reduce_scatter | solution.py:292
  443.7 359.0 %reduce-scatter.42.cloned.1.call-start = ((), (), s32[]{:S(2)}) async-start(), calls=%async_computation.23 | async-start | bytes 4718592 | tf_op jit(solution)/shard_map/reduce_scatter | solution.py:291
  450.6 443.4 %reduce-scatter.38.cloned.1.call-start = ((), (), s32[]{:S(2)}) async-start(), calls=%async_computation.21 | async-start | bytes 4718592 | tf_op jit(solution)/shard_map/reduce_scatter | solution.py:290
  458.9 499.7 %reduce-scatter.58.cloned.1.call-start = ((), (), s32[]{:S(2)}) async-start(), calls=%async_computation.31 | async-start | bytes 294912
  461.8 518.0 %reduce-scatter.52.cloned.1.call-start = ((), (), s32[]{:S(2)}) async-start(), calls=%async_computation.28 | async-start | bytes 163840
  463.6 538.7 %reduce-scatter.46.cloned.1.call-start = ((), (), s32[]{:S(2)}) async-start(), calls=%async_computation.25 | async-start | bytes 163840
  515.7 380.2 %copy-start.55 = (u32[32]{0:T(128)S(1)}, u32[32]{0:T(128)}, u32[]{:S(2)}) copy-start(u32[32]{0:T(128)} %constant.116) | copy-start | bytes 388
  515.7 508.7 %reduce-scatter.50.cloned.1.call-start = ((), (), s32[]{:S(2)}) async-start(), calls=%async_computation.27 | async-start | bytes 163840
  581.4 465.5 %reduce-scatter.48.cloned.1.call-start = ((), (), s32[]{:S(2)}) async-start(), calls=%async_computation.26 | async-start | bytes 163840
  647.5 421.5 %reduce-scatter.56.cloned.1.call-start = ((), (), s32[]{:S(2)}) async-start(), calls=%async_computation.30 | async-start | bytes 163840
  713.4 378.0 %reduce-scatter.54.cloned.1.call-start = ((), (), s32[]{:S(2)}) async-start(), calls=%async_computation.29 | async-start | bytes 327680
  804.7 309.2 %reduce-scatter.40.cloned.1.call-start = ((), (), s32[]{:S(2)}) async-start(), calls=%async_computation.22 | async-start | bytes 327680 | tf_op jit(solution)/shard_map/reduce_scatter | solution.py:309
  (59 other events, 148.2 us)
Sparse Core Ops, SparseCore 0:
  16.2 49.7 all-gather.5
  68.2 54.1 all-gather.7
  387.0 60.8 reduce-scatter.35
  451.5 62.4 reduce-scatter.29
  517.3 62.3 reduce-scatter.33
  583.3 62.3 reduce-scatter.31
  649.2 62.4 reduce-scatter.43
  715.7 86.9 reduce-scatter.41
  806.4 87.6 reduce-scatter.37
  897.6 60.9 reduce-scatter.57
  961.2 18.5 reduce-scatter.51
  982.7 19.6 reduce-scatter.45
  1004.9 19.5 reduce-scatter.49
  1027.3 19.5 reduce-scatter.47
  1049.4 19.5 reduce-scatter.55
  1071.3 20.0 reduce-scatter.53
  1093.8 20.0 reduce-scatter.39
where the time goes:
time: 1130 us; the launch traced here: 1120 us
  waiting for transfers between devices  600 us (53%)
  blocking collectives  288 us (25%)
  matrix products  113 us (10%)
  local copies, waits for them, and re-layouts  66.9 us (6%)
  other arithmetic  34.8 us (3%)
  between operations  17.6 us (2%)
    unnamed x24, waiting for transfers between devices  158 us
    reduce_scatter x1, waiting for transfers between devices, per_device(): lax.psum_scatter(gradients[4], 'wide', scatter_dimension=0, tiled=True)  89.3 us
    reduce_scatter x1, waiting for transfers between devices, per_device(): lax.psum_scatter(gradients[5], 'wide', scatter_dimension=0, tiled=True)  89.3 us
    reduce_scatter x1, waiting for transfers between devices, per_device(): lax.psum_scatter(gradients[1], 'wide', scatter_dimension=0, tiled=True)  64.3 us
    reduce_scatter x1, waiting for transfers between devices, per_device(): lax.psum_scatter(gradients[6], 'wide', scatter_dimension=0, tiled=True)  64.1 us
    reduce_scatter x1, waiting for transfers between devices, per_device(): lax.psum_scatter(gradients[2], 'wide', scatter_dimension=0, tiled=True)  63.9 us
    reduce_scatter x1, waiting for transfers between devices, per_device(): lax.psum_scatter(gradients[0], 'wide', scatter_dimension=0, tiled=True)  50.4 us
    all_gather x1, blocking collectives, per_device(): lax.all_gather(narrow_parts[2], 'wide', axis=0, tiled=True)  34.6 us
  transfers between devices with their start and end apart: 17, of which 14 were waited for; matrix products, arithmetic and copies ran while one was open for 14% of the time, Pallas kernels for 0%

commit v1 on v0

v1 whole, which is shorter than its diff:
```python
from functools import partial
import math

import jax
import jax.numpy as jnp
from jax import lax
from jax.experimental import pallas as pl
from jax.experimental.pallas import tpu as pltpu
from jax.sharding import PartitionSpec as P

HEADS = 8
EPSILON = 1e-05
AXES = ("wide", "narrow")
F32 = jnp.float32
BF16 = jnp.bfloat16
NEG = -1e30
VMEM_LIMIT = 60 * 1024 * 1024

WIDE = 8
NARROW = 4
PLACES = WIDE * NARROW
HALF = PLACES // 2

Z1, Z0, X, Y = 16, 8, 4, 2
ORDER_FIRST = ((Z1, Z0, X, Y), (Y, Z1, Z0, X))
ORDER_SECOND = ((Z1, Z0, X, Y), (Y, Z1, Z0, X))


def nn(left, right):
    return lax.dot_general(left, right, (((1,), (0,)), ((), ())), preferred_element_type=F32)


def nt(left, right):
    return lax.dot_general(left, right, (((1,), (1,)), ((), ())), preferred_element_type=F32)


def step_mask(order, step, core):
    return jnp.where(core == 0, order[0][step], order[1][step])


def relative_mask(order, block, core):
    masks = []
    for own in order:
        total = 0
        for step in range(4):
            if block >> step & 1:
                total ^= own[step]
        masks.append(total)
    return jnp.where(core == 0, masks[0], masks[1])


def place_of(order, direct, me, half, block):
    if not direct:
        where = half * HALF + block
        return where // NARROW, where % NARROW
    core = me & 1
    if half == 0:
        where = me ^ relative_mask(order, block, core)
    else:
        where = me ^ 1 ^ relative_mask(order, block, 1 - core)
    return where >> 2, where & 3


def pairs(order, step):
    found = []
    for place in range(PLACES):
        mask = 1 if step == 4 else order[place & 1][step]
        found.append((place, place ^ mask))
    return found


def my_place():
    return lax.axis_index("wide") * NARROW + lax.axis_index("narrow")


def head_masks(rows):
    lane = lax.broadcasted_iota(jnp.int32, (rows, 128), 1)
    return lane < 64


def stack_heads(pair_rows, low):
    zero = jnp.zeros_like(pair_rows)
    return jnp.concatenate(
        [jnp.where(low, pair_rows, zero), jnp.where(low, zero, pair_rows)], axis=0
    )


def fill_bias(segments_ref, bias_ref, windows):
    length = segments_ref.shape[1]
    for window in range(windows):
        row = segments_ref[window : window + 1, :].astype(F32)
        column = jnp.transpose(jnp.broadcast_to(row, (128, length)))
        for block in range(length // 128):
            start = max(0, block * 128 - 256)
            stop = block * 128 + 128
            span = stop - start
            key_at = start + lax.broadcasted_iota(jnp.int32, (span, 128), 0)
            query_at = block * 128 + lax.broadcasted_iota(jnp.int32, (span, 128), 1)
            same = column[start:stop, :] == row[:, block * 128 : block * 128 + 128]
            bias_ref[window, block, 0:span, :] = jnp.where(
                (key_at <= query_at) & same, 0.0, NEG
            )


def wait_whole(ref, sem):
    pltpu.make_async_copy(ref, ref, sem).wait()


def attend_kernel(
    direct,
    segments_ref,
    x_ref,
    p0_ref,
    p1_ref,
    p2_ref,
    p3_ref,
    qkv_ref,
    attended_ref,
    lse_ref,
    passed_ref,
    mixed_ref,
    vec_ref,
    bin_ref,
    weights,
    table,
    small,
    bias,
    sems,
):
    windows, length = segments_ref.shape
    me = my_place() if direct else 0
    for block in range(HALF):
        for half in range(2):
            source = ((p0_ref, p1_ref), (p2_ref, p3_ref))[half][block // 8].at[block % 8]
            wide, narrow = place_of(ORDER_FIRST, direct, me, half, block)
            rows = pl.ds(pl.multiple_of(wide * 64, 64), 64)
            pltpu.make_async_copy(
                source.at[pl.ds(192, 64)],
                table.at[rows, pl.ds(pl.multiple_of(narrow * 128, 128), 128)],
                sems.at[0],
            ).start()
            pltpu.make_async_copy(
                source.at[pl.ds(256, 16)], small.at[half * HALF + block], sems.at[1]
            ).start()
            for part in range(3):
                pltpu.make_async_copy(
                    source.at[pl.ds(part * 64, 64)],
                    weights.at[narrow, rows, pl.ds(part * 128, 128)],
                    sems.at[2],
                ).start()
    fill_bias(segments_ref, bias, windows)
    wait_whole(table, sems.at[0])
    for window in range(windows):
        rows = slice(window * length, (window + 1) * length)
        passed = x_ref[rows, :].astype(F32) + table[...].astype(F32)
        passed_ref[rows, :] = passed
        mixed_ref[rows, :] = passed.astype(BF16)
    wait_whole(small, sems.at[1])
    vec_ref[...] = jnp.zeros_like(vec_ref)
    bin_ref[...] = jnp.zeros_like(bin_ref)
    for half in range(2):
        for block in range(HALF):
            wide, narrow = place_of(ORDER_FIRST, direct, me, half, block)
            piece = small[half * HALF + block].astype(F32)
            vec_ref[wide // 2] += piece[0:8]
            bin_ref[wide // 4] += piece[8:16]
    wait_whole(weights, sems.at[2])
    low = head_masks(128)

    def per_pair(pair, unused):
        projected = nn(mixed_ref[...], weights[pair])
        vec = vec_ref[pair]
        queries = (projected[:, 0:128] + vec[0:1]).astype(BF16) * BF16(0.125)
        qkv_ref[pair, :, 0:128] = queries
        qkv_ref[pair, :, 128:256] = projected[:, 128:256].astype(BF16)
        qkv_ref[pair, :, 256:384] = (projected[:, 256:384] + vec[1:2]).astype(BF16)
        for window in range(windows):
            base = window * length
            values_t = jnp.transpose(qkv_ref[pair, base : base + length, 256:384])
            for block in range(length // 128):
                start = max(0, block * 128 - 256)
                stop = block * 128 + 128
                span = stop - start
                query = stack_heads(
                    qkv_ref[pair, base + block * 128 : base + block * 128 + 128, 0:128], low
                )
                keys = qkv_ref[pair, base + start : base + stop, 128:256]
                mask = bias[window, block, 0:span, :]
                scores = nt(keys, query) + jnp.concatenate([mask, mask], axis=1)
                peak = jnp.max(scores, axis=0, keepdims=True)
                weight = jnp.exp(scores - peak)
                total = jnp.sum(weight, axis=0, keepdims=True)
                shares = (weight * (1.0 / total)).astype(BF16)
                lse_ref[pair, window, block : block + 1, :] = peak + jnp.log(total)
                joined = nn(values_t[:, start:stop], shares)
                both = jnp.concatenate([joined[0:64, 0:128], joined[64:128, 128:256]], axis=0)
                attended_ref[
                    base + block * 128 : base + block * 128 + 128,
                    pl.ds(pl.multiple_of(pair * 128, 128), 128),
                ] = jnp.transpose(both).astype(BF16)
        return unused

    lax.fori_loop(0, NARROW, per_pair, 0)


def norm_parts(values):
    average = jnp.mean(values, axis=-1, keepdims=True)
    centred = values - average
    variance = jnp.mean(centred * centred, axis=-1, keepdims=True)
    scale = lax.rsqrt(variance + EPSILON)
    return centred * scale, scale


def norm_back(hat, scale, gains, grad):
    scaled = grad * gains
    first = jnp.mean(scaled, axis=-1, keepdims=True)
    second = jnp.mean(scaled * hat, axis=-1, keepdims=True)
    return scale * (scaled - first - hat * second)


def vec_row(vec_ref, row):
    return jnp.concatenate([vec_ref[tile, row : row + 1, :] for tile in range(4)], axis=1)


def column_sum(values):
    return jnp.sum(values, axis=0, keepdims=True)


GELU_SCALE = math.sqrt(2.0 / math.pi)


def gelu_both(pre):
    square = pre * pre
    curve = jnp.tanh(pre * (GELU_SCALE + (GELU_SCALE * 0.044715) * square))
    half = 0.5 + 0.5 * curve
    slope = (0.5 * pre) * (1.0 - curve * curve) * (
        GELU_SCALE + (3.0 * GELU_SCALE * 0.044715) * square
    )
    return pre * half, half + slope


def load_second(direct, blocks, w_out, w_in, w_back, sems):
    me = my_place() if direct else 0
    for block in range(HALF):
        for half in range(2):
            source = blocks[half * 2 + block // 8].at[block % 8]
            wide, narrow = place_of(ORDER_SECOND, direct, me, half, block)
            rows = pl.ds(pl.multiple_of(wide * 64, 64), 64)
            columns = pl.ds(pl.multiple_of(narrow * 128, 128), 128)
            pltpu.make_async_copy(source.at[0], w_out.at[rows, columns], sems.at[0]).start()
            pltpu.make_async_copy(
                source.at[pl.ds(1, 4)], w_in.at[pl.ds(narrow * 4, 4), rows, :], sems.at[1]
            ).start()
            pltpu.make_async_copy(
                source.at[pl.ds(5, 4)], w_back.at[pl.ds(wide * 4, 4), :, columns], sems.at[2]
            ).start()


def w_in_columns(w_in, chunk):
    return jnp.concatenate([w_in[chunk * 2], w_in[chunk * 2 + 1]], axis=1)


def forward_kernel(
    direct,
    attended_ref,
    passed_ref,
    cotangent_ref,
    vec_ref,
    bin_ref,
    p0_ref,
    p1_ref,
    p2_ref,
    p3_ref,
    output_ref,
    slope_ref,
    grad_second_ref,
    first_ref,
    low_ref,
    keep_ref,
    send_ref,
    sums_ref,
    w_out,
    w_in,
    w_back,
    active,
    grad_t,
    sems,
):
    step = pl.program_id(0)
    rows = attended_ref.shape[0]

    @pl.when(step == 0)
    def _():
        load_second(direct, (p0_ref, p1_ref, p2_ref, p3_ref), w_out, w_in, w_back, sems)
        sums_ref[...] = jnp.zeros_like(sums_ref)
        wait_whole(w_out, sems.at[0])

    first_sum = passed_ref[...] + nn(attended_ref[...], w_out[...]) + vec_row(vec_ref, 2)
    first_ref[...] = first_sum
    hat, unused_scale = norm_parts(first_sum)
    hidden = hat * vec_row(vec_ref, 4) + vec_row(vec_ref, 5)
    low = hidden.astype(BF16)
    low_ref[...] = low

    @pl.when(step == 0)
    def _():
        wait_whole(w_in, sems.at[1])
        wait_whole(w_back, sems.at[2])

    total = hidden + vec_row(vec_ref, 3)
    for chunk in range(8):
        offset = jnp.concatenate(
            [bin_ref[chunk // 4, 2 * (chunk % 4) + part : 2 * (chunk % 4) + part + 1, :] for part in range(2)],
            axis=1,
        )
        value, slope = gelu_both(nn(low, w_in_columns(w_in, chunk)) + offset)
        value = value.astype(BF16)
        active[pl.ds(pl.multiple_of(step * rows, rows), rows), chunk * 256 : chunk * 256 + 256] = value
        slope_ref[:, chunk * 256 : chunk * 256 + 256] = slope
        weight = w_back[chunk * 4 : chunk * 4 + 4].reshape(256, 512)
        total += nn(value, weight)
    hat, scale = norm_parts(total)
    gains = vec_row(vec_ref, 6)
    output_ref[...] = (hat * gains + vec_row(vec_ref, 7)).astype(BF16)
    cotangent = cotangent_ref[...].astype(F32)
    grad_second = norm_back(hat, scale, gains, cotangent)
    grad_second_ref[...] = grad_second
    grad_low = grad_second.astype(BF16)
    grad_t[:, pl.ds(pl.multiple_of(step * rows, rows), rows)] = jnp.transpose(grad_low)
    sums_ref[0:1, :] += column_sum(grad_low.astype(F32))
    sums_ref[1:2, :] += column_sum(cotangent * hat)
    sums_ref[2:3, :] += column_sum(cotangent)

    @pl.when(step == pl.num_programs(0) - 1)
    def _():
        me = my_place() if direct else 0
        for half, target in ((0, keep_ref), (1, send_ref)):
            for block in range(HALF):
                wide, narrow = place_of(ORDER_SECOND, direct, me, half, block)
                piece = nn(
                    grad_t[pl.ds(pl.multiple_of(narrow * 128, 128), 128), :],
                    active[:, pl.ds(pl.multiple_of(wide * 256, 256), 256)],
                )
                target[block, 0:128, :] = piece[:, 0:128].astype(target.dtype)
                target[block, 128:256, :] = piece[:, 128:256].astype(target.dtype)


def backward_kernel(
    direct,
    slope_ref,
    grad_second_ref,
    first_ref,
    low_ref,
    attended_ref,
    vec_ref,
    p0_ref,
    p1_ref,
    p2_ref,
    p3_ref,
    grad_first_ref,
    grad_attended_ref,
    keep_ref,
    send_ref,
    sums_ref,
    bin_sums_ref,
    w_out,
    w_in,
    w_back,
    grad_pre,
    grad_branch,
    low_t,
    attended_t,
    sems,
):
    step = pl.program_id(0)
    rows = attended_ref.shape[0]
    here = pl.ds(pl.multiple_of(step * rows, rows), rows)

    @pl.when(step == 0)
    def _():
        load_second(direct, (p0_ref, p1_ref, p2_ref, p3_ref), w_out, w_in, w_back, sems)
        sums_ref[...] = jnp.zeros_like(sums_ref)
        bin_sums_ref[...] = jnp.zeros_like(bin_sums_ref)

    low_t[:, here] = jnp.transpose(low_ref[...])
    attended_t[:, here] = jnp.transpose(attended_ref[...])

    @pl.when(step == 0)
    def _():
        wait_whole(w_out, sems.at[0])
        wait_whole(w_in, sems.at[1])
        wait_whole(w_back, sems.at[2])

    grad_hidden = grad_second_ref[...]
    grad_low = grad_hidden.astype(BF16)
    for chunk in range(8):
        weight = w_back[chunk * 4 : chunk * 4 + 4].reshape(256, 512)
        grad = nt(grad_low, weight) * slope_ref[:, chunk * 256 : chunk * 256 + 256]
        grad = grad.astype(BF16)
        grad_pre[here, chunk * 256 : chunk * 256 + 256] = grad
        grad_hidden += nt(grad, w_in_columns(w_in, chunk))
        sums = column_sum(grad.astype(F32))
        for part in range(2):
            row = 2 * (chunk % 4) + part
            bin_sums_ref[chunk // 4, row : row + 1, :] += sums[:, part * 128 : part * 128 + 128]
    hat, scale = norm_parts(first_ref[...])
    gains = vec_row(vec_ref, 4)
    grad_first = norm_back(hat, scale, gains, grad_hidden)
    grad_first_ref[...] = grad_first
    branch = grad_first.astype(BF16)
    grad_branch[here, :] = branch
    sums_ref[0:1, :] += column_sum(branch.astype(F32))
    sums_ref[1:2, :] += column_sum(grad_hidden * hat)
    sums_ref[2:3, :] += column_sum(grad_hidden)
    grad_attended_ref[...] = nt(branch, w_out[...]).astype(BF16)

    @pl.when(step == pl.num_programs(0) - 1)
    def _():
        me = my_place() if direct else 0
        for half, target in ((0, keep_ref), (1, send_ref)):
            for block in range(HALF):
                wide, narrow = place_of(ORDER_SECOND, direct, me, half, block)
                own = pl.ds(pl.multiple_of(wide * 64, 64), 64)
                piece = nn(
                    low_t[own, :], grad_pre[:, pl.ds(pl.multiple_of(narrow * 512, 512), 512)]
                )
                for part in range(4):
                    target[block, part] = piece[:, part * 128 : part * 128 + 128].astype(target.dtype)
                piece = nn(
                    attended_t[own, :],
                    grad_branch[:, pl.ds(pl.multiple_of(narrow * 128, 128), 128)],
                )
                target[block, 4] = piece.astype(target.dtype)


def attend_back_kernel(
    direct,
    segments_ref,
    qkv_ref,
    grad_attended_ref,
    lse_ref,
    mixed_ref,
    grad_first_ref,
    sums_a_ref,
    sums_b_ref,
    bin_sums_ref,
    p0_ref,
    p1_ref,
    p2_ref,
    p3_ref,
    stream_ref,
    keep_ref,
    send_ref,
    weights,
    bias,
    mixed_t,
    grads,
    accumulate,
    stream,
    vec_sums,
    sems,
):
    windows, length = segments_ref.shape
    me = my_place() if direct else 0
    for block in range(HALF):
        for half in range(2):
            source = ((p0_ref, p1_ref), (p2_ref, p3_ref))[half][block // 8].at[block % 8]
            wide, narrow = place_of(ORDER_FIRST, direct, me, half, block)
            rows = pl.ds(pl.multiple_of(wide * 64, 64), 64)
            for part in range(3):
                pltpu.make_async_copy(
                    source.at[pl.ds(part * 64, 64)],
                    weights.at[narrow, rows, pl.ds(part * 128, 128)],
                    sems.at[0],
                ).start()
    fill_bias(segments_ref, bias, windows)
    mixed_t[...] = jnp.transpose(mixed_ref[...])
    stream[...] = grad_first_ref[...]
    for tile in range(4):
        lanes = slice(tile * 128, tile * 128 + 128)
        vec_sums[tile, 2:3, :] = sums_b_ref[0:1, lanes]
        vec_sums[tile, 3:4, :] = sums_a_ref[0:1, lanes]
        vec_sums[tile, 4:6, :] = sums_b_ref[1:3, lanes]
        vec_sums[tile, 6:8, :] = sums_a_ref[1:3, lanes]
    wait_whole(weights, sems.at[0])
    low = head_masks(128)

    def per_pair(pair, unused):
        for window in range(windows):
            base = window * length
            keys_t = jnp.transpose(qkv_ref[pair, base : base + length, 128:256])
            accumulate[...] = jnp.zeros_like(accumulate)
            for block in range(length // 128):
                start = max(0, block * 128 - 256)
                stop = block * 128 + 128
                span = stop - start
                here = slice(base + block * 128, base + block * 128 + 128)
                query = stack_heads(qkv_ref[pair, here, 0:128], low)
                above = stack_heads(
                    grad_attended_ref[here, pl.ds(pl.multiple_of(pair * 128, 128), 128)], low
                )
                keys = qkv_ref[pair, base + start : base + stop, 128:256]
                values = qkv_ref[pair, base + start : base + stop, 256:384]
                mask = bias[window, block, 0:span, :]
                mask = jnp.concatenate([mask, mask], axis=1)
                shares = jnp.exp(
                    nt(keys, query) + mask - lse_ref[pair, window, block : block + 1, :]
                )
                grad_shares = nt(values, above)
                inner = jnp.sum(shares * grad_shares, axis=0, keepdims=True)
                grad_scores = (shares * (grad_shares - inner)).astype(BF16)
                accumulate[start:stop, 0:128] += nn(grad_scores, query)
                accumulate[start:stop, 128:256] += nn(shares.astype(BF16), above)
                joined = nn(keys_t[:, start:stop], grad_scores)
                both = jnp.concatenate([joined[0:64, 0:128], joined[64:128, 128:256]], axis=0)
                grads[here, 0:128] = (jnp.transpose(both) * 0.125).astype(BF16)
            grads[base : base + length, 128:384] = accumulate[...].astype(BF16)
        grad = grads[...]
        vec_sums[pair, 0:1, :] = column_sum(grad[:, 0:128].astype(F32))
        vec_sums[pair, 1:2, :] = column_sum(grad[:, 256:384].astype(F32))
        stream[...] += nt(grad, weights[pair])
        weight_grads = nn(mixed_t[...], grad)
        for wide in range(WIDE):
            half, block = index_of(ORDER_FIRST, direct, me, wide, pair)
            piece = weight_grads[wide * 64 : wide * 64 + 64, :]

            for which, target in ((0, keep_ref), (1, send_ref)):

                @pl.when(half == which)
                def _(target=target, piece=piece, block=block):
                    for part in range(3):
                        target[block, part * 64 : part * 64 + 64, :] = piece[
                            :, part * 128 : part * 128 + 128
                        ].astype(target.dtype)

        return unused

    lax.fori_loop(0, NARROW, per_pair, 0)
    total = jnp.zeros((length, stream.shape[1]), F32)
    for window in range(windows):
        rows = slice(window * length, (window + 1) * length)
        stream_ref[rows, :] = stream[rows, :].astype(BF16)
        total += stream[rows, :]
    stream[0:length, :] = total
    for half, target in ((0, keep_ref), (1, send_ref)):
        for block in range(HALF):
            wide, narrow = place_of(ORDER_FIRST, direct, me, half, block)
            target[block, 192:256, :] = stream[
                pl.ds(pl.multiple_of(wide * 64, 64), 64),
                pl.ds(pl.multiple_of(narrow * 128, 128), 128),
            ].astype(target.dtype)
            target[block, 256:264, :] = vec_sums[wide // 2].astype(target.dtype)
            target[block, 264:272, :] = bin_sums_ref[wide // 4].astype(target.dtype)


def index_of(order, direct, me, wide, narrow):
    where = wide * NARROW + narrow
    if not direct:
        return where // HALF, where % HALF
    core = where & 1
    apart = me ^ where
    half = apart & 1
    apart = apart ^ half
    block = 0
    for step in range(4):
        bit = jnp.where((apart & step_mask(order, step, core)) != 0, 1 << step, 0)
        block = block + bit
    return half, block


def vmem():
    return pl.BlockSpec(memory_space=pltpu.VMEM)


def hbm():
    return pl.BlockSpec(memory_space=pl.ANY)


def params(**more):
    return pltpu.CompilerParams(vmem_limit_bytes=VMEM_LIMIT, **more)


def shape(dims, dtype):
    return jax.ShapeDtypeStruct(dims, dtype)


def attend_call(direct, segments, x, blocks):
    windows, length = segments.shape
    total = windows * length
    return pl.pallas_call(
        partial(attend_kernel, direct),
        out_shape=(
            shape((NARROW, total, 384), BF16),
            shape((total, 512), BF16),
            shape((NARROW, windows, length // 128, 256), F32),
            shape((total, 512), F32),
            shape((total, 512), BF16),
            shape((4, 8, 128), F32),
            shape((2, 8, 128), F32),
        ),
        in_specs=[vmem(), vmem()] + [hbm()] * 4,
        out_specs=tuple([vmem()] * 7),
        scratch_shapes=[
            pltpu.VMEM((NARROW, 512, 384), BF16),
            pltpu.VMEM((512, 512), BF16),
            pltpu.VMEM((PLACES, 16, 128), BF16),
            pltpu.VMEM((windows, length // 128, 384, 128), F32),
            pltpu.SemaphoreType.DMA((3,)),
        ],
        compiler_params=params(),
        name="attend",
    )(segments, x, *blocks)


ROWS = 256


def second_scratch():
    return [
        pltpu.VMEM((512, 512), BF16),
        pltpu.VMEM((16, 512, 128), BF16),
        pltpu.VMEM((32, 64, 512), BF16),
    ]


def row_block(columns):
    return pl.BlockSpec((ROWS, columns), lambda step: (step, 0))


def forward_call(direct, attended, passed, cotangent, vec, bins, blocks):
    total = attended.shape[0]
    return pl.pallas_call(
        partial(forward_kernel, direct),
        grid=(total // ROWS,),
        out_shape=(
            shape((total, 512), BF16),
            shape((total, 2048), F32),
            shape((total, 512), F32),
            shape((total, 512), F32),
            shape((total, 512), BF16),
            shape((HALF, 256, 128), F32),
            shape((HALF, 256, 128), BF16),
            shape((8, 512), F32),
        ),
        in_specs=[row_block(512)] * 3 + [vmem()] * 2 + [hbm()] * 4,
        out_specs=(
            row_block(512),
            row_block(2048),
            row_block(512),
            row_block(512),
            row_block(512),
            vmem(),
            vmem(),
            vmem(),
        ),
        scratch_shapes=second_scratch()
        + [
            pltpu.VMEM((total, 2048), BF16),
            pltpu.VMEM((512, total), BF16),
            pltpu.SemaphoreType.DMA((3,)),
        ],
        compiler_params=params(),
        name="forward",
    )(attended, passed, cotangent, vec, bins, *blocks)


def backward_call(direct, slope, grad_second, first_sum, low, attended, vec, blocks):
    total = attended.shape[0]
    return pl.pallas_call(
        partial(backward_kernel, direct),
        grid=(total // ROWS,),
        out_shape=(
            shape((total, 512), F32),
            shape((total, 512), BF16),
            shape((HALF, 5, 64, 128), F32),
            shape((HALF, 5, 64, 128), BF16),
            shape((8, 512), F32),
            shape((2, 8, 128), F32),
        ),
        in_specs=[row_block(2048)] + [row_block(512)] * 4 + [vmem()] + [hbm()] * 4,
        out_specs=(row_block(512), row_block(512), vmem(), vmem(), vmem(), vmem()),
        scratch_shapes=second_scratch()
        + [
            pltpu.VMEM((total, 2048), BF16),
            pltpu.VMEM((total, 512), BF16),
            pltpu.VMEM((512, total), BF16),
            pltpu.VMEM((512, total), BF16),
            pltpu.SemaphoreType.DMA((3,)),
        ],
        compiler_params=params(),
        name="backward",
    )(slope, grad_second, first_sum, low, attended, vec, *blocks)


def attend_back_call(direct, segments, qkv, grad_attended, lse, mixed, grad_first, sums, blocks):
    windows, length = segments.shape
    total = windows * length
    return pl.pallas_call(
        partial(attend_back_kernel, direct),
        out_shape=(
            shape((total, 512), BF16),
            shape((HALF, 272, 128), F32),
            shape((HALF, 272, 128), BF16),
        ),
        in_specs=[vmem()] * 9 + [hbm()] * 4,
        out_specs=(vmem(), vmem(), vmem()),
        scratch_shapes=[
            pltpu.VMEM((NARROW, 512, 384), BF16),
            pltpu.VMEM((windows, length // 128, 384, 128), F32),
            pltpu.VMEM((512, total), BF16),
            pltpu.VMEM((total, 384), BF16),
            pltpu.VMEM((length, 256), F32),
            pltpu.VMEM((total, 512), F32),
            pltpu.VMEM((4, 8, 128), F32),
            pltpu.SemaphoreType.DMA((1,)),
        ],
        compiler_params=params(),
        name="attend_back",
    )(segments, qkv, grad_attended, lse, mixed, grad_first, *sums, *blocks)


def gather_blocks(own, order):
    held = own[None]
    for step in range(3):
        held = jnp.concatenate([held, lax.ppermute(held, AXES, pairs(order, step))], axis=0)
    far = lax.ppermute(held, AXES, pairs(order, 3))
    return (
        held,
        far,
        lax.ppermute(held, AXES, pairs(order, 4)),
        lax.ppermute(far, AXES, pairs(order, 4)),
    )


def scatter_sum(keep, send, order):
    total = keep + lax.ppermute(send, AXES, pairs(order, 4)).astype(F32)
    for step in (3, 2, 1, 0):
        size = 1 << step
        total = total[:size] + lax.ppermute(
            total[size:].astype(BF16), AXES, pairs(order, step)
        ).astype(F32)
    return total[0]


def small_block(vectors, in_bias, wide, narrow):
    row = lax.broadcasted_iota(jnp.int32, (8, 128), 0)
    side = lax.broadcasted_iota(jnp.int32, (8, 128), 1) // 64
    spread = jnp.tile(vectors, (4, 2))
    first = jnp.where((row // 2 == narrow) & (side == wide % 2), spread, 0)
    spread = jnp.tile(in_bias[None], (8, 2))
    second = jnp.where((row == 2 * (wide % 4) + narrow // 2) & (side == narrow % 2), spread, 0)
    return jnp.concatenate([first, second], axis=0).astype(BF16)


def first_block(w_query, w_key, w_value, table, small):
    return jnp.concatenate([w_query, w_key, w_value, table, small], axis=0)


def second_block(w_out, w_in, w_back):
    return jnp.concatenate(
        [w_out[None]]
        + [w_in[None, :, part * 128 : part * 128 + 128] for part in range(4)]
        + [w_back.reshape(4, 64, 128)],
        axis=0,
    )


def turned(total):
    return jnp.concatenate([total[0:128].T, total[128:256].T], axis=0)


def layer(direct, inputs, segment_ids, cotangent, first, second):
    windows, length, features = inputs.shape
    rows = windows * length
    x = inputs.reshape(rows, features)
    qkv, attended, lse, passed, mixed, vec, bins = attend_call(direct, segment_ids, x, first)
    output, slope, grad_second, first_sum, low, keep_back, send_back, sums_a = forward_call(
        direct, attended, passed, cotangent.reshape(rows, features), vec, bins, second
    )
    grad_first, grad_attended, keep_in, send_in, sums_b, bin_sums = backward_call(
        direct, slope, grad_second, first_sum, low, attended, vec, second
    )
    stream, keep_first, send_first = attend_back_call(
        direct,
        segment_ids,
        qkv,
        grad_attended,
        lse,
        mixed,
        grad_first,
        (sums_a, sums_b, bin_sums),
        first,
    )
    return (
        output.reshape(inputs.shape),
        stream.reshape(inputs.shape),
        (keep_back, send_back),
        (keep_in, send_in),
        (keep_first, send_first),
    )


def per_device(
    inputs,
    segment_ids,
    cotangent,
    w_query,
    w_key,
    w_value,
    w_out,
    w_in,
    w_back,
    position_table,
    vectors,
    in_bias,
):
    wide, narrow = lax.axis_index("wide"), lax.axis_index("narrow")
    small = small_block(vectors, in_bias, wide, narrow)
    first = gather_blocks(
        first_block(w_query, w_key, w_value, position_table, small), ORDER_FIRST
    )
    second = gather_blocks(second_block(w_out, w_in, w_back), ORDER_SECOND)
    output, stream, back, inner, outer = layer(
        True, inputs, segment_ids, cotangent, first, second
    )
    back = scatter_sum(*back, ORDER_SECOND)
    inner = scatter_sum(*inner, ORDER_SECOND)
    outer = scatter_sum(*outer, ORDER_FIRST)
    grad_in = jnp.concatenate([inner[part] for part in range(4)], axis=1)
    vec = outer[256:264]
    vec = jnp.where(wide % 2 == 0, vec[:, 0:64], vec[:, 64:128])
    vec = lax.dynamic_slice_in_dim(vec, narrow * 2, 2, 0)
    bins = lax.dynamic_slice_in_dim(outer[264:272], 2 * (wide % 4) + narrow // 2, 1, 0)[0]
    bins = jnp.where(narrow % 2 == 0, bins[0:64], bins[64:128])
    return (
        output,
        stream,
        outer[0:64],
        outer[64:128],
        outer[128:192],
        inner[4],
        grad_in,
        turned(back),
        outer[192:256],
        vec,
        bins,
    )


def canonical(array, axis_tiles):
    rows, columns = array.shape
    across, along = axis_tiles
    return (
        array.reshape(across, rows // across, along, columns // along)
        .transpose(0, 2, 1, 3)
        .reshape(PLACES, rows // across, columns // along)
    )


def uncanonical(blocks, rows, columns):
    return (
        blocks.reshape(WIDE, NARROW, rows // WIDE, columns // NARROW)
        .transpose(0, 2, 1, 3)
        .reshape(rows, columns)
    )


def per_device_any(
    inputs,
    segment_ids,
    cotangent,
    w_query,
    w_key,
    w_value,
    w_out,
    w_in,
    w_back,
    position_table,
    vectors,
    in_bias,
):
    def whole(array):
        array = lax.all_gather(array, "narrow", axis=1, tiled=True)
        return lax.all_gather(array, "wide", axis=0, tiled=True)

    def fours(blocks):
        return tuple(blocks[at * 8 : at * 8 + 8] for at in range(4))

    vectors = lax.all_gather(vectors, "narrow", axis=0, tiled=True)
    vectors = lax.all_gather(vectors, "wide", axis=1, tiled=True)
    in_bias = lax.all_gather(in_bias, AXES, axis=0, tiled=True)
    places = jnp.arange(PLACES)
    pieces = vectors.reshape(NARROW, 2, WIDE, 64).transpose(2, 0, 1, 3).reshape(PLACES, 2, 64)
    small = jax.vmap(small_block)(
        pieces, in_bias.reshape(PLACES, 64), places // NARROW, places % NARROW
    )
    tiles = (WIDE, NARROW)
    first = jax.vmap(first_block)(
        canonical(whole(w_query), tiles),
        canonical(whole(w_key), tiles),
        canonical(whole(w_value), tiles),
        canonical(whole(position_table), tiles),
        small,
    )
    second = jax.vmap(second_block)(
        canonical(whole(w_out), tiles),
        canonical(whole(w_in), tiles),
        canonical(whole(w_back), tiles),
    )
    output, stream, back, inner, outer = layer(
        False, inputs, segment_ids, cotangent, fours(first), fours(second)
    )

    def joined(pair):
        return jnp.concatenate([pair[0], pair[1].astype(F32)], axis=0)

    def summed(array):
        array = lax.psum_scatter(array, "wide", scatter_dimension=0, tiled=True)
        return lax.psum_scatter(array, "narrow", scatter_dimension=1, tiled=True)

    back, inner, outer = joined(back), joined(inner), joined(outer)
    back = jax.vmap(turned)(back)
    grad_in = inner[:, 0:4].transpose(0, 2, 1, 3).reshape(PLACES, 64, 512)
    vec = outer.reshape(WIDE, NARROW, 272, 128)[::2, 0, 256:264]
    vec = vec.transpose(1, 0, 2).reshape(8, 512)
    vec = lax.psum_scatter(vec, "wide", scatter_dimension=1, tiled=True)
    vec = lax.psum_scatter(vec, "narrow", scatter_dimension=0, tiled=True)
    bins = outer.reshape(WIDE, NARROW, 272, 128)[::4, 0, 264:272].reshape(2048)
    bins = lax.psum_scatter(bins, AXES, scatter_dimension=0, tiled=True)
    return (
        output,
        stream,
        summed(uncanonical(outer[:, 0:64], 512, 512)),
        summed(uncanonical(outer[:, 64:128], 512, 512)),
        summed(uncanonical(outer[:, 128:192], 512, 512)),
        summed(uncanonical(inner[:, 4], 512, 512)),
        summed(uncanonical(grad_in, 512, 2048)),
        summed(uncanonical(back, 2048, 512)),
        summed(uncanonical(outer[:, 192:256], 512, 512)),
        vec,
        bins,
    )


def solution(mesh):
    matrix = P("wide", "narrow")
    rows = P(AXES, None, None)
    direct = mesh.shape["wide"] == WIDE and mesh.shape["narrow"] == NARROW
    return jax.shard_map(
        per_device if direct else per_device_any,
        mesh=mesh,
        in_specs=(
            rows,
            P(AXES, None),
            rows,
            matrix,
            matrix,
            matrix,
            matrix,
            matrix,
            matrix,
            matrix,
            P("narrow", "wide"),
            P(AXES),
        ),
        out_specs=(
            rows,
            rows,
            matrix,
            matrix,
            matrix,
            matrix,
            matrix,
            matrix,
            matrix,
            P("narrow", "wide"),
            P(AXES),
        ),
        check_vma=False,
    )
```

time: 1130 us -> 214 us (0.19)
  waiting for transfers between devices: 600 us -> 65.3 us
  blocking collectives: 288 us -> 0 us
  matrix products: 113 us -> 0 us
  Pallas kernels: 0 us -> 85.5 us
  local copies, waits for them, and re-layouts: 66.9 us -> 12.2 us
  starting transfers between devices: 0.88 us -> 40.7 us
  other arithmetic: 34.8 us -> 8.17 us
  between operations: 17.6 us -> 1.13 us
    reduce_scatter x8 -> x0, waiting for transfers between devices: 442 us -> none  [the longest x1 89.3 us: per_device(): lax.psum_scatter(gradients[4], 'wide', scatter_dimension=0, tiled=True)]
    all_gather x15 -> x0, blocking collectives: 256 us -> none  [the longest x1 34.6 us: per_device(): lax.all_gather(narrow_parts[2], 'wide', axis=0, tiled=True)]
    unnamed x24 -> x0, waiting for transfers between devices: 158 us -> none
    dot_general x36 -> x0, matrix products: 102 us -> none  [the longest x8 27 us: product(): return jnp.dot(left, right, preferred_element_type=jnp.float32)]
    pallas_call x0 -> x4, Pallas kernels: none -> 85.5 us  [the longest x1 24.1 us: attend_back_call(): pl.pallas_call(partial(attend_back_kernel, direct), out_shape=(shape((tot...]
    ppermute x0 -> x27, waiting for transfers between devices: none -> 65.3 us  [the longest x6 30.9 us: gather_blocks(): lax.ppermute(held, AXES, pairs(order, step))]
    ppermute x0 -> x27, starting transfers between devices: none -> 40.7 us  [the longest x12 19.6 us: scatter_sum(): lax.ppermute(total[size:].astype(BF16), AXES, pairs(order, step))]
    unnamed x3 -> x0, blocking collectives: 32.2 us -> none
  transfers between devices with their start and end apart: 17 -> 27, of which waited for: 14 -> 16; matrix products, arithmetic and copies ran while one was open for 14% -> 5% of each run, Pallas kernels for 0% -> 31%
where the time goes in v1:
time: 214 us; the launch traced here: 213 us
  Pallas kernels  85.5 us (40%)
  waiting for transfers between devices  65.3 us (31%)
  starting transfers between devices  40.7 us (19%)
  local copies, waits for them, and re-layouts  12.2 us (6%)
  other arithmetic  8.17 us (4%)
    ppermute x6, waiting for transfers between devices, gather_blocks(): lax.ppermute(held, AXES, pairs(order, step))  30.9 us
    ppermute x12, waiting for transfers between devices, scatter_sum(): lax.ppermute(total[size:].astype(BF16), AXES, pairs(order, step))  25.2 us
    pallas_call x1, Pallas kernels, attend_back_call(): pl.pallas_call(partial(attend_back_kernel, direct), out_shape=(shape((tot...  24.1 us
    pallas_call x1, Pallas kernels, backward_call(): pl.pallas_call(partial(backward_kernel, direct), grid=(total // ROWS,), o...  23.1 us
    pallas_call x1, Pallas kernels, forward_call(): pl.pallas_call(partial(forward_kernel, direct), grid=(total // ROWS,), ou...  19.8 us
    ppermute x12, starting transfers between devices, scatter_sum(): lax.ppermute(total[size:].astype(BF16), AXES, pairs(order, step))  19.6 us
    pallas_call x1, Pallas kernels, attend_call(): pl.pallas_call(partial(attend_kernel, direct), out_shape=(shape((NARROW,...  18.5 us
    ppermute x6, starting transfers between devices, gather_blocks(): lax.ppermute(held, AXES, pairs(order, step))  15.8 us
  transfers between devices with their start and end apart: 27, of which 16 were waited for; matrix products, arithmetic and copies ran while one was open for 5% of the time, Pallas kernels for 31%

profile of v1, /device:TPU:0, one launch (start us, length us, event | category | flops | bytes accessed | tf_op | source)
XLA Modules:
  0.0 213.1 jit_solution(8908311408744418289)
XLA Ops:
  5.2 4.1 %collective-permute-start.6 = (bf16[1,9,64,128]{3,2,1,0:T(8,128)(2,1)S(1)}, bf16[1,9,64,128]{3,2,1,0:T(8,128)(2,1)S(1)}, u32[]{:S(2)}, u32[]{:S(2)}) collective-permute-start(bf16[1,9,64,128]{3,2,1,0:T(8,128)(2,1)S(1)} %bitcast.47), channel_id=1, source_target_pairs={{0,16},{1,3},{2,18},{3,1},{4,20},{5,7},{6,22},{7,5},{8,24},{9,11},... | collective-permute-start | bytes 442376 | tf_op jit(solution)/shard_map/ppermute | solution.py:725
  9.3 4.7 %collective-permute-done.6 = bf16[1,9,64,128]{3,2,1,0:T(8,128)(2,1)S(1)} collective-permute-done((bf16[1,9,64,128]{3,2,1,0:T(8,128)(2,1)S(1)}, bf16[1,9,64,128]{3,2,1,0:T(8,128)(2,1)S(1)}, u32[]{:S(2)}, u32[]{:S(2)}) %collective-permute-start.6) | collective-permute-done | bytes 147488 | tf_op jit(solution)/shard_map/ppermute | solution.py:725
  15.1 7.7 %collective-permute-done.7 = bf16[2,9,64,128]{3,2,1,0:T(8,128)(2,1)S(1)} collective-permute-done((bf16[2,9,64,128]{3,2,1,0:T(8,128)(2,1)S(1)}, bf16[2,9,64,128]{3,2,1,0:T(8,128)(2,1)S(1)}, u32[]{:S(2)}, u32[]{:S(2)}) %collective-permute-start.7) | collective-permute-done | bytes 294944 | tf_op jit(solution)/shard_map/ppermute | solution.py:725
  22.9 2.4 %collective-permute-start.8 = (bf16[4,9,64,128]{3,2,1,0:T(8,128)(2,1)S(1)}, bf16[4,9,64,128]{3,2,1,0:T(8,128)(2,1)S(1)}, u32[]{:S(2)}, u32[]{:S(2)}) collective-permute-start(bf16[4,9,64,128]{3,2,1,0:T(8,128)(2,1)S(1)} %pad_maximum_fusion.1), channel_id=1, source_target_pairs={{0,4},{1,9},{2,6},{3,11},{4,0},{5,13},{6,2},{7,15},{8,12},{9,1},{1... | collective-permute-start | bytes 1769480 | tf_op jit(solution)/shard_map/ppermute | solution.py:725
  25.4 8.4 %collective-permute-done.8 = bf16[4,9,64,128]{3,2,1,0:T(8,128)(2,1)S(1)} collective-permute-done((bf16[4,9,64,128]{3,2,1,0:T(8,128)(2,1)S(1)}, bf16[4,9,64,128]{3,2,1,0:T(8,128)(2,1)S(1)}, u32[]{:S(2)}, u32[]{:S(2)}) %collective-permute-start.8) | collective-permute-done | bytes 589856 | tf_op jit(solution)/shard_map/ppermute | solution.py:725
  33.9 2.4 %collective-permute-start.9 = (bf16[8,9,64,128]{3,2,1,0:T(8,128)(2,1)S(1)}, bf16[8,9,64,128]{3,2,1,0:T(8,128)(2,1)S(1)}, u32[]{:S(2)}, u32[]{:S(2)}) collective-permute-start(bf16[8,9,64,128]{3,2,1,0:T(8,128)(2,1)S(1)} %pad_maximum_fusion.p0_ref), channel_id=1, source_target_pairs={{0,2},{1,5},{2,0},{3,7},{4,6},{5,1},{6,4},{7,3},{8,10},{9,13},{10,... | collective-permute-start | bytes 3538952 | tf_op jit(solution)/shard_map/ppermute | solution.py:726
  36.7 4.0 %collective-permute-start = (bf16[1,272,128]{2,1,0:T(8,128)(2,1)S(1)}, bf16[1,272,128]{2,1,0:T(8,128)(2,1)S(1)}, u32[]{:S(2)}, u32[]{:S(2)}) collective-permute-start(bf16[1,272,128]{2,1,0:T(8,128)(2,1)S(1)} %bitcast.53), channel_id=1, source_target_pairs={{0,16},{1,3},{2,18},{3,1},{4,20},{5,7},{6,22},{7,5},{8,24},{9,11},... | collective-permute-start | bytes 208904 | tf_op jit(solution)/shard_map/ppermute | solution.py:725
  40.6 2.3 %collective-permute-done = bf16[1,272,128]{2,1,0:T(8,128)(2,1)S(1)} collective-permute-done((bf16[1,272,128]{2,1,0:T(8,128)(2,1)S(1)}, bf16[1,272,128]{2,1,0:T(8,128)(2,1)S(1)}, u32[]{:S(2)}, u32[]{:S(2)}) %collective-permute-start) | collective-permute-done | bytes 69664 | tf_op jit(solution)/shard_map/ppermute | solution.py:725
  42.9 2.6 %collective-permute-start.1 = (bf16[2,272,128]{2,1,0:T(8,128)(2,1)S(1)}, bf16[2,272,128]{2,1,0:T(8,128)(2,1)S(1)}, u32[]{:S(2)}, u32[]{:S(2)}) collective-permute-start(bf16[2,272,128]{2,1,0:T(8,128)(2,1)S(1)} %pad_maximum_fusion.5), channel_id=1, source_target_pairs={{0,8},{1,17},{2,10},{3,19},{4,12},{5,21},{6,14},{7,23},{8,0},{9,25... | collective-permute-start | bytes 417800 | tf_op jit(solution)/shard_map/ppermute | solution.py:725
  45.6 3.0 %collective-permute-done.1 = bf16[2,272,128]{2,1,0:T(8,128)(2,1)S(1)} collective-permute-done((bf16[2,272,128]{2,1,0:T(8,128)(2,1)S(1)}, bf16[2,272,128]{2,1,0:T(8,128)(2,1)S(1)}, u32[]{:S(2)}, u32[]{:S(2)}) %collective-permute-start.1) | collective-permute-done | bytes 139296 | tf_op jit(solution)/shard_map/ppermute | solution.py:725
  50.7 4.9 %collective-permute-done.2 = bf16[4,272,128]{2,1,0:T(8,128)(2,1)S(1)} collective-permute-done((bf16[4,272,128]{2,1,0:T(8,128)(2,1)S(1)}, bf16[4,272,128]{2,1,0:T(8,128)(2,1)S(1)}, u32[]{:S(2)}, u32[]{:S(2)}) %collective-permute-start.2) | collective-permute-done | bytes 278560 | tf_op jit(solution)/shard_map/ppermute | solution.py:725
  56.6 1.9 collective-permute-start.3
  58.5 7.7 %collective-permute-done.3.p1_ref = bf16[8,272,128]{2,1,0:T(8,128)(2,1)S(1)} collective-permute-done((bf16[8,272,128]{2,1,0:T(8,128)(2,1)S(1)}, bf16[8,272,128]{2,1,0:T(8,128)(2,1)S(1)}, u32[]{:S(2)}, u32[]{:S(2)}) %collective-permute-start.3) | collective-permute-done | bytes 557088 | tf_op jit(solution)/shard_map/ppermute | solution.py:726
  68.9 18.5 %attend.1 = (bf16[4,1024,384]{2,1,0:T(8,128)(2,1)}, bf16[1024,512]{1,0:T(8,128)(2,1)}, f32[4,2,4,256]{3,2,1,0:T(4,128)}, f32[1024,512]{1,0:T(8,128)}, bf16[1024,...) custom-call(s32[2,512]{1,0:T(2,128)} %segments_ref.3, bf16[1024,512]{1,0:T(8,128)(2,1)} %bitcast.52, ...), custom_call_target="tpu_custom_call" | custom-call | tf_op jit(solution)/shard_map/attend/pallas_call | solution.py:590
  88.5 19.8 %forward.1 = (bf16[1024,512]{1,0:T(8,128)(2,1)}, f32[1024,2048]{1,0:T(8,128)}, f32[1024,512]{1,0:T(8,128)}, f32[1024,512]{1,0:T(8,128)}, bf16[1024,512]{1,0:T(8,...) custom-call(bf16[1024,512]{1,0:T(8,128)(2,1)} %get-tuple-element.35.attended_ref, ...), custom_call_target="tpu_custom_call" | custom-call | tf_op jit(solution)/shard_map/forward/pallas_call | solution.py:632
  108.5 23.1 %backward.1 = (f32[1024,512]{1,0:T(8,128)}, bf16[1024,512]{1,0:T(8,128)(2,1)}, f32[16,5,64,128]{3,2,1,0:T(8,128)}, bf16[16,5,64,128]{3,2,1,0:T(8,128)(2,1)}, f32[8,512]{1,0:T(8,128)}, /*index=5*/f32[2,8,128]{2,1,0:T(8,128)}) custom-call(f32[1024,2048]{1,0:T(8,128)} %get-tuple-element.41.slope_ref, f32[1024,512]{1,0:T(8,128)} %get-tuple-element.42.grad_second_ref, ...), custom_call_target="tpu_custom_call" | custom-call | tf_op jit(solution)/shard_map/backward/pallas_call | solution.py:669
  131.7 24.1 %attend_back.1 = (bf16[1024,512]{1,0:T(8,128)(2,1)}, f32[16,272,128]{2,1,0:T(8,128)}, bf16[16,272,128]{2,1,0:T(8,128)(2,1)}) custom-call(s32[2,512]{1,0:T(2,128)} %segments_ref.3, bf16[4,1024,384]{2,1,0:T(8,128)(2,1)} %get-tuple-element.40.qkv_ref, bf16[1024,512]{1,0:T(8,128)(2,1)} %get-tuple-element.45.grad_attended_ref, ...), custom_call_target="tpu_custom_call" | custom-call | tf_op jit(solution)/shard_map/attend_back/pallas_call | solution.py:698
  162.4 6.0 %collective-permute-done.23 = bf16[8,256,128]{2,1,0:T(8,128)(2,1)} collective-permute-done((bf16[8,256,128]{2,1,0:T(8,128)(2,1)}, bf16[8,256,128]{2,1,0:T(8,128)(2,1)}, u32[]{:S(2)}, u32[]{:S(2)}) %collective-permute-start.23) | collective-permute-done | bytes 524320 | tf_op jit(solution)/shard_map/ppermute | solution.py:739
  171.2 3.2 %collective-permute-done.13 = bf16[8,272,128]{2,1,0:T(8,128)(2,1)} collective-permute-done((bf16[8,272,128]{2,1,0:T(8,128)(2,1)}, bf16[8,272,128]{2,1,0:T(8,128)(2,1)}, u32[]{:S(2)}, u32[]{:S(2)}) %collective-permute-start.13) | collective-permute-done | bytes 557088 | tf_op jit(solution)/shard_map/ppermute | solution.py:739
  178.5 3.2 %collective-permute-start.25 = (bf16[2,256,128]{2,1,0:T(8,128)(2,1)S(1)}, bf16[2,256,128]{2,1,0:T(8,128)(2,1)S(1)}, u32[]{:S(2)}, u32[]{:S(2)}) collective-permute-start(bf16[2,256,128]{2,1,0:T(8,128)(2,1)S(1)} %slice.317), channel_id=1, source_target_pairs={{0,8},{1,17},{2,10},{3,19},{4,12},{5,21},{6,14},{7,23},{8,0},{9,25... | collective-permute-start | bytes 393224 | tf_op jit(solution)/shard_map/ppermute | solution.py:739
  183.1 5.2 %collective-permute-start.15 = (bf16[2,272,128]{2,1,0:T(8,128)(2,1)S(1)}, bf16[2,272,128]{2,1,0:T(8,128)(2,1)S(1)}, u32[]{:S(2)}, u32[]{:S(2)}) collective-permute-start(bf16[2,272,128]{2,1,0:T(8,128)(2,1)S(1)} %slice.316), channel_id=1, source_target_pairs={{0,8},{1,17},{2,10},{3,19},{4,12},{5,21},{6,14},{7,23},{8,0},{9,25... | collective-permute-start | bytes 417800 | tf_op jit(solution)/shard_map/ppermute | solution.py:739
  196.1 3.3 %collective-permute-done.16 = bf16[1,272,128]{2,1,0:T(8,128)(2,1)S(1)} collective-permute-done((bf16[1,272,128]{2,1,0:T(8,128)(2,1)S(1)}, bf16[1,272,128]{2,1,0:T(8,128)(2,1)S(1)}, u32[]{:S(2)}, u32[]{:S(2)}) %collective-permute-start.16) | collective-permute-done | bytes 69664 | tf_op jit(solution)/shard_map/ppermute | solution.py:739
  200.9 5.3 %collective-permute-done.20 = bf16[2,5,64,128]{3,2,1,0:T(8,128)(2,1)S(1)} collective-permute-done((bf16[2,5,64,128]{3,2,1,0:T(8,128)(2,1)S(1)}, bf16[2,5,64,128]{3,2,1,0:T(8,128)(2,1)S(1)}, u32[]{:S(2)}, u32[]{:S(2)}) %collective-permute-start.20) | collective-permute-done | bytes 163872 | tf_op jit(solution)/shard_map/ppermute | solution.py:739
  207.5 4.2 %collective-permute-done.21 = bf16[1,5,64,128]{3,2,1,0:T(8,128)(2,1)S(1)} collective-permute-done((bf16[1,5,64,128]{3,2,1,0:T(8,128)(2,1)S(1)}, bf16[1,5,64,128]{3,2,1,0:T(8,128)(2,1)S(1)}, u32[]{:S(2)}, u32[]{:S(2)}) %collective-permute-start.21) | collective-permute-done | bytes 81952 | tf_op jit(solution)/shard_map/ppermute | solution.py:739
  (135 shorter events, 39.9 us)
Async XLA Ops:
  5.2 8.8 %collective-permute-start.6 = (bf16[1,9,64,128]{3,2,1,0:T(8,128)(2,1)S(1)}, bf16[1,9,64,128]{3,2,1,0:T(8,128)(2,1)S(1)}, u32[]{:S(2)}, u32[]{:S(2)}) collective-permute-start(bf16[1,9,64,128]{3,2,1,0:T(8,128)(2,1)S(1)} %bitcast.47), channel_id=1, source_target_pairs={{0,16},{1,3},{2,18},{3,1},{4,20},{5,7},{6,22},{7,5},{8,24},{9,11},... | collective-permute-start | bytes 442376 | tf_op jit(solution)/shard_map/ppermute | solution.py:725
  14.0 8.8 %collective-permute-start.7 = (bf16[2,9,64,128]{3,2,1,0:T(8,128)(2,1)S(1)}, bf16[2,9,64,128]{3,2,1,0:T(8,128)(2,1)S(1)}, u32[]{:S(2)}, u32[]{:S(2)}) collective-permute-start(bf16[2,9,64,128]{3,2,1,0:T(8,128)(2,1)S(1)} %pad_maximum_fusion.3), channel_id=1, source_target_pairs={{0,8},{1,17},{2,10},{3,19},{4,12},{5,21},{6,14},{7,23},{8,0},{9,25... | collective-permute-start | bytes 884744 | tf_op jit(solution)/shard_map/ppermute | solution.py:725
  22.9 10.9 %collective-permute-start.8 = (bf16[4,9,64,128]{3,2,1,0:T(8,128)(2,1)S(1)}, bf16[4,9,64,128]{3,2,1,0:T(8,128)(2,1)S(1)}, u32[]{:S(2)}, u32[]{:S(2)}) collective-permute-start(bf16[4,9,64,128]{3,2,1,0:T(8,128)(2,1)S(1)} %pad_maximum_fusion.1), channel_id=1, source_target_pairs={{0,4},{1,9},{2,6},{3,11},{4,0},{5,13},{6,2},{7,15},{8,12},{9,1},{1... | collective-permute-start | bytes 1769480 | tf_op jit(solution)/shard_map/ppermute | solution.py:725
  33.9 16.6 %collective-permute-start.9 = (bf16[8,9,64,128]{3,2,1,0:T(8,128)(2,1)S(1)}, bf16[8,9,64,128]{3,2,1,0:T(8,128)(2,1)S(1)}, u32[]{:S(2)}, u32[]{:S(2)}) collective-permute-start(bf16[8,9,64,128]{3,2,1,0:T(8,128)(2,1)S(1)} %pad_maximum_fusion.p0_ref), channel_id=1, source_target_pairs={{0,2},{1,5},{2,0},{3,7},{4,6},{5,1},{6,4},{7,3},{8,10},{9,13},{10,... | collective-permute-start | bytes 3538952 | tf_op jit(solution)/shard_map/ppermute | solution.py:726
  36.7 6.3 %collective-permute-start = (bf16[1,272,128]{2,1,0:T(8,128)(2,1)S(1)}, bf16[1,272,128]{2,1,0:T(8,128)(2,1)S(1)}, u32[]{:S(2)}, u32[]{:S(2)}) collective-permute-start(bf16[1,272,128]{2,1,0:T(8,128)(2,1)S(1)} %bitcast.53), channel_id=1, source_target_pairs={{0,16},{1,3},{2,18},{3,1},{4,20},{5,7},{6,22},{7,5},{8,24},{9,11},... | collective-permute-start | bytes 208904 | tf_op jit(solution)/shard_map/ppermute | solution.py:725
  42.9 5.7 %collective-permute-start.1 = (bf16[2,272,128]{2,1,0:T(8,128)(2,1)S(1)}, bf16[2,272,128]{2,1,0:T(8,128)(2,1)S(1)}, u32[]{:S(2)}, u32[]{:S(2)}) collective-permute-start(bf16[2,272,128]{2,1,0:T(8,128)(2,1)S(1)} %pad_maximum_fusion.5), channel_id=1, source_target_pairs={{0,8},{1,17},{2,10},{3,19},{4,12},{5,21},{6,14},{7,23},{8,0},{9,25... | collective-permute-start | bytes 417800 | tf_op jit(solution)/shard_map/ppermute | solution.py:725
  48.7 6.9 %collective-permute-start.2 = (bf16[4,272,128]{2,1,0:T(8,128)(2,1)S(1)}, bf16[4,272,128]{2,1,0:T(8,128)(2,1)S(1)}, u32[]{:S(2)}, u32[]{:S(2)}) collective-permute-start(bf16[4,272,128]{2,1,0:T(8,128)(2,1)S(1)} %pad_maximum_fusion.4), channel_id=1, source_target_pairs={{0,4},{1,9},{2,6},{3,11},{4,0},{5,13},{6,2},{7,15},{8,12},{9,1},{1... | collective-permute-start | bytes 835592 | tf_op jit(solution)/shard_map/ppermute | solution.py:725
  50.2 37.2 %collective-permute-start.10 = (bf16[8,9,64,128]{3,2,1,0:T(8,128)(2,1)S(1)}, bf16[8,9,64,128]{3,2,1,0:T(8,128)(2,1)S(1)}, u32[]{:S(2)}, u32[]{:S(2)}) collective-permute-start(bf16[8,9,64,128]{3,2,1,0:T(8,128)(2,1)S(1)} %pad_maximum_fusion.p0_ref), channel_id=1, source_target_pairs={{0,1},{1,0},{2,3},{3,2},{4,5},{5,4},{6,7},{7,6},{8,9},{9,8},{10,11... | collective-permute-start | bytes 3538952 | tf_op jit(solution)/shard_map/ppermute | solution.py:730
  50.5 36.9 %collective-permute-start.11 = (bf16[8,9,64,128]{3,2,1,0:T(8,128)(2,1)S(1)}, bf16[8,9,64,128]{3,2,1,0:T(8,128)(2,1)}, u32[]{:S(2)}, u32[]{:S(2)}) collective-permute-start(bf16[8,9,64,128]{3,2,1,0:T(8,128)(2,1)S(1)} %collective-permute-done.9.p1_ref), channel_id=1, source_target_pairs={{0,1},{1,0},{2,3},{3,2},{4,5},{5,4},{6,7},{7,6},{8,9},{9,8},{10,11... | collective-permute-start | bytes 3538952 | tf_op jit(solution)/shard_map/ppermute | solution.py:731
  56.6 9.6 %collective-permute-start.3 = (bf16[8,272,128]{2,1,0:T(8,128)(2,1)S(1)}, bf16[8,272,128]{2,1,0:T(8,128)(2,1)S(1)}, u32[]{:S(2)}, u32[]{:S(2)}) collective-permute-start(bf16[8,272,128]{2,1,0:T(8,128)(2,1)S(1)} %pad_maximum_fusion.2.p0_ref), channel_id=1, source_target_pairs={{0,2},{1,5},{2,0},{3,7},{4,6},{5,1},{6,4},{7,3},{8,10},{9,13},{10,... | collective-permute-start | bytes 1671176 | tf_op jit(solution)/shard_map/ppermute | solution.py:726
  58.5 7.7 %collective-permute-start.4 = (bf16[8,272,128]{2,1,0:T(8,128)(2,1)S(1)}, bf16[8,272,128]{2,1,0:T(8,128)(2,1)S(1)}, u32[]{:S(2)}, u32[]{:S(2)}) collective-permute-start(bf16[8,272,128]{2,1,0:T(8,128)(2,1)S(1)} %pad_maximum_fusion.2.p0_ref), channel_id=1, source_target_pairs={{0,1},{1,0},{2,3},{3,2},{4,5},{5,4},{6,7},{7,6},{8,9},{9,8},{10,11... | collective-permute-start | bytes 1671176 | tf_op jit(solution)/shard_map/ppermute | solution.py:730
  108.3 48.1 %collective-permute-start.22 = (bf16[16,256,128]{2,1,0:T(8,128)(2,1)}, bf16[16,256,128]{2,1,0:T(8,128)(2,1)}, u32[]{:S(2)}, u32[]{:S(2)}) collective-permute-start(bf16[16,256,128]{2,1,0:T(8,128)(2,1)} %get-tuple-element.58), channel_id=1, source_target_pairs={{0,1},{1,0},{2,3},{3,2},{4,5},{5,4},{6,7},{7,6},{8,9},{9,8},{10,11... | collective-permute-start | bytes 3145736 | tf_op jit(solution)/shard_map/ppermute | solution.py:736
  156.1 20.8 %collective-permute-start.17 = (bf16[16,5,64,128]{3,2,1,0:T(8,128)(2,1)}, bf16[16,5,64,128]{3,2,1,0:T(8,128)(2,1)S(1)}, u32[]{:S(2)}, u32[]{:S(2)}) collective-permute-start(bf16[16,5,64,128]{3,2,1,0:T(8,128)(2,1)} %get-tuple-element.56), channel_id=1, source_target_pairs={{0,1},{1,0},{2,3},{3,2},{4,5},{5,4},{6,7},{7,6},{8,9},{9,8},{10,11... | collective-permute-start | bytes 3932168 | tf_op jit(solution)/shard_map/ppermute | solution.py:736
  159.0 9.5 %collective-permute-start.23 = (bf16[8,256,128]{2,1,0:T(8,128)(2,1)}, bf16[8,256,128]{2,1,0:T(8,128)(2,1)}, u32[]{:S(2)}, u32[]{:S(2)}) collective-permute-start(bf16[8,256,128]{2,1,0:T(8,128)(2,1)} %slice.311), channel_id=1, source_target_pairs={{0,2},{1,5},{2,0},{3,7},{4,6},{5,1},{6,4},{7,3},{8,10},{9,13},{10,... | collective-permute-start | bytes 1572872 | tf_op jit(solution)/shard_map/ppermute | solution.py:739
  161.9 12.5 %collective-permute-start.13 = (bf16[8,272,128]{2,1,0:T(8,128)(2,1)}, bf16[8,272,128]{2,1,0:T(8,128)(2,1)}, u32[]{:S(2)}, u32[]{:S(2)}) collective-permute-start(bf16[8,272,128]{2,1,0:T(8,128)(2,1)} %slice.310), channel_id=1, source_target_pairs={{0,2},{1,5},{2,0},{3,7},{4,6},{5,1},{6,4},{7,3},{8,10},{9,13},{10,... | collective-permute-start | bytes 1671176 | tf_op jit(solution)/shard_map/ppermute | solution.py:739
  170.0 8.4 %collective-permute-start.24 = (bf16[4,256,128]{2,1,0:T(8,128)(2,1)S(1)}, bf16[4,256,128]{2,1,0:T(8,128)(2,1)S(1)}, u32[]{:S(2)}, u32[]{:S(2)}) collective-permute-start(bf16[4,256,128]{2,1,0:T(8,128)(2,1)S(1)} %slice.314), channel_id=1, source_target_pairs={{0,4},{1,9},{2,6},{3,11},{4,0},{5,13},{6,2},{7,15},{8,12},{9,1},{1... | collective-permute-start | bytes 786440 | tf_op jit(solution)/shard_map/ppermute | solution.py:739
  175.6 7.4 %collective-permute-start.14 = (bf16[4,272,128]{2,1,0:T(8,128)(2,1)S(1)}, bf16[4,272,128]{2,1,0:T(8,128)(2,1)S(1)}, u32[]{:S(2)}, u32[]{:S(2)}) collective-permute-start(bf16[4,272,128]{2,1,0:T(8,128)(2,1)S(1)} %slice.313), channel_id=1, source_target_pairs={{0,4},{1,9},{2,6},{3,11},{4,0},{5,13},{6,2},{7,15},{8,12},{9,1},{1... | collective-permute-start | bytes 835592 | tf_op jit(solution)/shard_map/ppermute | solution.py:739
  177.7 12.4 %collective-permute-start.18 = (bf16[8,5,64,128]{3,2,1,0:T(8,128)(2,1)S(1)}, bf16[8,5,64,128]{3,2,1,0:T(8,128)(2,1)S(1)}, u32[]{:S(2)}, u32[]{:S(2)}) collective-permute-start(bf16[8,5,64,128]{3,2,1,0:T(8,128)(2,1)S(1)} %slice.309), channel_id=1, source_target_pairs={{0,2},{1,5},{2,0},{3,7},{4,6},{5,1},{6,4},{7,3},{8,10},{9,13},{10,... | collective-permute-start | bytes 1966088 | tf_op jit(solution)/shard_map/ppermute | solution.py:739
  178.5 9.8 %collective-permute-start.25 = (bf16[2,256,128]{2,1,0:T(8,128)(2,1)S(1)}, bf16[2,256,128]{2,1,0:T(8,128)(2,1)S(1)}, u32[]{:S(2)}, u32[]{:S(2)}) collective-permute-start(bf16[2,256,128]{2,1,0:T(8,128)(2,1)S(1)} %slice.317), channel_id=1, source_target_pairs={{0,8},{1,17},{2,10},{3,19},{4,12},{5,21},{6,14},{7,23},{8,0},{9,25... | collective-permute-start | bytes 393224 | tf_op jit(solution)/shard_map/ppermute | solution.py:739
  183.1 10.9 %collective-permute-start.15 = (bf16[2,272,128]{2,1,0:T(8,128)(2,1)S(1)}, bf16[2,272,128]{2,1,0:T(8,128)(2,1)S(1)}, u32[]{:S(2)}, u32[]{:S(2)}) collective-permute-start(bf16[2,272,128]{2,1,0:T(8,128)(2,1)S(1)} %slice.316), channel_id=1, source_target_pairs={{0,8},{1,17},{2,10},{3,19},{4,12},{5,21},{6,14},{7,23},{8,0},{9,25... | collective-permute-start | bytes 417800 | tf_op jit(solution)/shard_map/ppermute | solution.py:739
  188.3 5.6 %collective-permute-start.26 = (bf16[1,256,128]{2,1,0:T(8,128)(2,1)S(1)}, bf16[1,256,128]{2,1,0:T(8,128)(2,1)S(1)}, u32[]{:S(2)}, u32[]{:S(2)}) collective-permute-start(bf16[1,256,128]{2,1,0:T(8,128)(2,1)S(1)} %slice.320), channel_id=1, source_target_pairs={{0,16},{1,3},{2,18},{3,1},{4,20},{5,7},{6,22},{7,5},{8,24},{9,11},... | collective-permute-start | bytes 196616 | tf_op jit(solution)/shard_map/ppermute | solution.py:739
  190.3 9.9 %collective-permute-start.19 = (bf16[4,5,64,128]{3,2,1,0:T(8,128)(2,1)S(1)}, bf16[4,5,64,128]{3,2,1,0:T(8,128)(2,1)S(1)}, u32[]{:S(2)}, u32[]{:S(2)}) collective-permute-start(bf16[4,5,64,128]{3,2,1,0:T(8,128)(2,1)S(1)} %slice.312), channel_id=1, source_target_pairs={{0,4},{1,9},{2,6},{3,11},{4,0},{5,13},{6,2},{7,15},{8,12},{9,1},{1... | collective-permute-start | bytes 983048 | tf_op jit(solution)/shard_map/ppermute | solution.py:739
  200.3 6.0 %collective-permute-start.20 = (bf16[2,5,64,128]{3,2,1,0:T(8,128)(2,1)S(1)}, bf16[2,5,64,128]{3,2,1,0:T(8,128)(2,1)S(1)}, u32[]{:S(2)}, u32[]{:S(2)}) collective-permute-start(bf16[2,5,64,128]{3,2,1,0:T(8,128)(2,1)S(1)} %slice.315), channel_id=1, source_target_pairs={{0,8},{1,17},{2,10},{3,19},{4,12},{5,21},{6,14},{7,23},{8,0},{9,25... | collective-permute-start | bytes 491528 | tf_op jit(solution)/shard_map/ppermute | solution.py:739
  206.3 5.4 %collective-permute-start.21 = (bf16[1,5,64,128]{3,2,1,0:T(8,128)(2,1)S(1)}, bf16[1,5,64,128]{3,2,1,0:T(8,128)(2,1)S(1)}, u32[]{:S(2)}, u32[]{:S(2)}) collective-permute-start(bf16[1,5,64,128]{3,2,1,0:T(8,128)(2,1)S(1)} %slice.318), channel_id=1, source_target_pairs={{0,16},{1,3},{2,18},{3,1},{4,20},{5,7},{6,22},{7,5},{8,24},{9,11},... | collective-permute-start | bytes 245768 | tf_op jit(solution)/shard_map/ppermute | solution.py:739
  (21 other events, 295.8 us)

commit v2 on v1

v2 whole, which is shorter than its diff:
```python
from functools import partial
import math

import jax
import jax.numpy as jnp
from jax import lax
from jax.experimental import pallas as pl
from jax.experimental.pallas import tpu as pltpu
from jax.sharding import PartitionSpec as P

HEADS = 8
EPSILON = 1e-05
AXES = ("wide", "narrow")
F32 = jnp.float32
BF16 = jnp.bfloat16
NEG = -1e30
VMEM_LIMIT = 60 * 1024 * 1024

WIDE = 8
NARROW = 4
PLACES = WIDE * NARROW
HALF = PLACES // 2

Z1, Z0, X, Y = 16, 8, 4, 2
ORDER_FIRST = ((Z1, X, Y, Z0), (Z0, Y, X, Z1))
ORDER_SECOND = ((Z1, Z0, X, Y), (Z0, Z1, Y, X))


def nn(left, right):
    return lax.dot_general(left, right, (((1,), (0,)), ((), ())), preferred_element_type=F32)


def nt(left, right):
    return lax.dot_general(left, right, (((1,), (1,)), ((), ())), preferred_element_type=F32)


def block_masks(order, core):
    masks = []
    for block in range(HALF):
        total = 0
        for step in range(4):
            if block >> step & 1:
                total ^= order[core][step]
        masks.append(total)
    return masks


def place_of(order, me, half, block):
    core = (me & 1) ^ half
    apart = jnp.where(core == 0, block_masks(order, 0)[block], block_masks(order, 1)[block])
    where = me ^ half ^ apart
    return where >> 2, where & 3


def block_at(order, me, apart):
    half = apart & 1
    core = (me & 1) ^ half
    first, second = (block_masks(order, of).index(apart ^ half) for of in range(2))
    return jnp.where(core == 0, first, second)


def pairs(order, step):
    found = []
    for place in range(PLACES):
        mask = 1 if step == 4 else order[place & 1][step]
        found.append((place, place ^ mask))
    return found


def my_place():
    return lax.axis_index("wide") * NARROW + lax.axis_index("narrow")


def head_masks(rows):
    lane = lax.broadcasted_iota(jnp.int32, (rows, 128), 1)
    return lane < 64


def stack_heads(pair_rows, low):
    zero = jnp.zeros_like(pair_rows)
    return jnp.concatenate(
        [jnp.where(low, pair_rows, zero), jnp.where(low, zero, pair_rows)], axis=0
    )


def fill_bias(segments_ref, bias_ref, windows):
    length = segments_ref.shape[1]
    for window in range(windows):
        row = segments_ref[window : window + 1, :].astype(F32)
        column = jnp.transpose(jnp.broadcast_to(row, (128, length)))
        for block in range(length // 128):
            start = max(0, block * 128 - 256)
            stop = block * 128 + 128
            span = stop - start
            key_at = start + lax.broadcasted_iota(jnp.int32, (span, 128), 0)
            query_at = block * 128 + lax.broadcasted_iota(jnp.int32, (span, 128), 1)
            same = column[start:stop, :] == row[:, block * 128 : block * 128 + 128]
            bias_ref[window, block, 0:span, :] = jnp.where(
                (key_at <= query_at) & same, 0.0, NEG
            )


def block_spans(windows, length):
    spans = []
    for window in range(windows):
        for block in range(length // 128):
            stop = block * 128 + 128
            start = max(0, stop - 384)
            base = window * length
            spans.append(
                (
                    window,
                    block,
                    slice(base + stop - 128, base + stop),
                    slice(base + start, base + stop),
                    stop - start,
                )
            )
    return spans


def part_lanes(pair, part):
    return pl.ds(pl.multiple_of(pair * 384 + part * 128, 128), 128)


def wait_whole(ref, sem):
    pltpu.make_async_copy(ref, ref, sem).wait()


def attend_kernel(
    direct,
    segments_ref,
    x_ref,
    p0_ref,
    p1_ref,
    p2_ref,
    p3_ref,
    qkv_ref,
    attended_ref,
    lse_ref,
    passed_ref,
    mixed_ref,
    vec_ref,
    bin_ref,
    weights,
    bias,
    table,
    small,
    sems,
):
    windows, length = segments_ref.shape
    me = my_place() if direct else jnp.int32(0)
    for block in range(HALF):
        for half in range(2):
            source = ((p0_ref, p1_ref), (p2_ref, p3_ref))[half][block // 8].at[block % 8]
            wide, narrow = place_of(ORDER_FIRST, me, half, block)
            rows = pl.ds(pl.multiple_of(wide * 64, 64), 64)
            pltpu.make_async_copy(
                source.at[pl.ds(192, 64)],
                table.at[rows, pl.ds(pl.multiple_of(narrow * 128, 128), 128)],
                sems.at[0],
            ).start()
            pltpu.make_async_copy(
                source.at[pl.ds(256, 16)], small.at[half * HALF + block], sems.at[1]
            ).start()
            for part in range(3):
                pltpu.make_async_copy(
                    source.at[pl.ds(part * 64, 64)],
                    weights.at[
                        rows, pl.ds(pl.multiple_of(narrow * 384 + part * 128, 128), 128)
                    ],
                    sems.at[2],
                ).start()
    fill_bias(segments_ref, bias, windows)
    wait_whole(table, sems.at[0])
    for window in range(windows):
        rows = slice(window * length, (window + 1) * length)
        passed = x_ref[rows, :].astype(F32) + table[...].astype(F32)
        passed_ref[rows, :] = passed
        mixed_ref[rows, :] = passed.astype(BF16)
    wait_whole(small, sems.at[1])
    vec_ref[...] = jnp.zeros_like(vec_ref)
    bin_ref[...] = jnp.zeros_like(bin_ref)
    for half in range(2):
        for block in range(HALF):
            wide, narrow = place_of(ORDER_FIRST, me, half, block)
            piece = small[half * HALF + block].astype(F32)
            vec_ref[wide // 2] += piece[0:8]
            bin_ref[wide // 4] += piece[8:16]
    wait_whole(weights, sems.at[2])
    low = head_masks(128)

    for chunk in range(6):
        projected = nn(mixed_ref[...], weights[:, chunk * 256 : chunk * 256 + 256])
        for side in range(2):
            pair, part = divmod(chunk * 2 + side, 3)
            own = projected[:, side * 128 : side * 128 + 128]
            if part != 1:
                own = own + vec_ref[pair, part // 2 : part // 2 + 1, :]
            own = own.astype(BF16)
            if part == 0:
                own = own * BF16(0.125)
            qkv_ref[:, (chunk * 2 + side) * 128 : (chunk * 2 + side) * 128 + 128] = own

    def per_pair(pair, unused):
        spans = block_spans(windows, length)
        turned_values = [
            jnp.transpose(
                qkv_ref[window * length : (window + 1) * length, part_lanes(pair, 2)]
            )
            for window in range(windows)
        ]
        scores = []
        for window, block, here, there, span in spans:
            query = stack_heads(qkv_ref[here, part_lanes(pair, 0)], low)
            mask = bias[window, block, 0:span, :]
            scores.append(
                nt(qkv_ref[there, part_lanes(pair, 1)], query)
                + jnp.concatenate([mask, mask], axis=1)
            )
        shares = []
        for (window, block, here, there, span), score in zip(spans, scores):
            peak = jnp.max(score, axis=0, keepdims=True)
            weight = jnp.exp(score - peak)
            total = jnp.sum(weight, axis=0, keepdims=True)
            shares.append((weight * (1.0 / total)).astype(BF16))
            lse_ref[pair, window, block : block + 1, :] = peak + jnp.log(total)
        for (window, block, here, there, span), share in zip(spans, shares):
            stop = block * 128 + 128
            joined = nn(turned_values[window][:, stop - span : stop], share)
            both = jnp.concatenate([joined[0:64, 0:128], joined[64:128, 128:256]], axis=0)
            attended_ref[here, pl.ds(pl.multiple_of(pair * 128, 128), 128)] = jnp.transpose(
                both
            ).astype(BF16)
        return unused

    lax.fori_loop(0, NARROW, per_pair, 0)


def norm_parts(values):
    average = jnp.mean(values, axis=-1, keepdims=True)
    centred = values - average
    variance = jnp.mean(centred * centred, axis=-1, keepdims=True)
    scale = lax.rsqrt(variance + EPSILON)
    return centred * scale, scale


def norm_back(hat, scale, gains, grad):
    scaled = grad * gains
    first = jnp.mean(scaled, axis=-1, keepdims=True)
    second = jnp.mean(scaled * hat, axis=-1, keepdims=True)
    return scale * (scaled - first - hat * second)


def vec_row(vec_ref, row):
    return jnp.concatenate([vec_ref[tile, row : row + 1, :] for tile in range(4)], axis=1)


def column_sum(values):
    return jnp.sum(values, axis=0, keepdims=True)


GELU_SCALE = math.sqrt(2.0 / math.pi)


def gelu_both(pre):
    square = pre * pre
    curve = jnp.tanh(pre * (GELU_SCALE + (GELU_SCALE * 0.044715) * square))
    half = 0.5 + 0.5 * curve
    slope = (0.5 * pre) * (1.0 - curve * curve) * (
        GELU_SCALE + (3.0 * GELU_SCALE * 0.044715) * square
    )
    return pre * half, half + slope


def load_second(me, blocks, w_out, w_in, w_back, sems):
    for block in range(HALF):
        for half in range(2):
            source = blocks[half * 2 + block // 8].at[block % 8]
            wide, narrow = place_of(ORDER_SECOND, me, half, block)
            rows = pl.ds(pl.multiple_of(wide * 64, 64), 64)
            columns = pl.ds(pl.multiple_of(narrow * 128, 128), 128)
            pltpu.make_async_copy(source.at[0], w_out.at[rows, columns], sems.at[0]).start()
            pltpu.make_async_copy(
                source.at[pl.ds(1, 4)], w_in.at[pl.ds(narrow * 4, 4), rows, :], sems.at[1]
            ).start()
            pltpu.make_async_copy(
                source.at[pl.ds(5, 4)], w_back.at[pl.ds(wide * 4, 4), :, columns], sems.at[2]
            ).start()


def w_in_columns(w_in, chunk):
    return jnp.concatenate([w_in[chunk * 2], w_in[chunk * 2 + 1]], axis=1)


def rows_at(step, rows):
    return pl.ds(pl.multiple_of(step * rows, rows), rows)


def forward_kernel(
    direct,
    attended_ref,
    passed_ref,
    cotangent_ref,
    vec_ref,
    bin_ref,
    p0_ref,
    p1_ref,
    p2_ref,
    p3_ref,
    output_ref,
    slope_ref,
    grad_second_ref,
    first_ref,
    low_t,
    keep_ref,
    send_ref,
    sums_ref,
    w_out,
    w_in,
    w_back,
    active,
    grad_t,
    sems,
):
    rows = ROWS
    me = my_place() if direct else jnp.int32(0)
    load_second(me, (p0_ref, p1_ref, p2_ref, p3_ref), w_out, w_in, w_back, sems)
    sums_ref[...] = jnp.zeros_like(sums_ref)
    wait_whole(w_out, sems.at[0])
    wait_whole(w_in, sems.at[1])
    wait_whole(w_back, sems.at[2])

    def per_rows(step, unused):
        here = rows_at(step, rows)
        first_sum = passed_ref[here, :] + nn(attended_ref[here, :], w_out[...]) + vec_row(vec_ref, 2)
        first_ref[here, :] = first_sum
        hat, unused_scale = norm_parts(first_sum)
        hidden = hat * vec_row(vec_ref, 4) + vec_row(vec_ref, 5)
        low = hidden.astype(BF16)
        turned_low = jnp.transpose(low)
        for wide in range(WIDE):
            low_t[wide ^ (me >> 2), :, here] = turned_low[wide * 64 : wide * 64 + 64, :]
        total = hidden + vec_row(vec_ref, 3)
        for chunk in range(8):
            offset = jnp.concatenate(
                [
                    bin_ref[chunk // 4, 2 * (chunk % 4) + part : 2 * (chunk % 4) + part + 1, :]
                    for part in range(2)
                ],
                axis=1,
            )
            columns = slice(chunk * 256, chunk * 256 + 256)
            value, slope = gelu_both(nn(low, w_in_columns(w_in, chunk)) + offset)
            value = value.astype(BF16)
            active[here, columns] = value
            slope_ref[here, columns] = slope
            total += nn(value, w_back[chunk * 4 : chunk * 4 + 4].reshape(256, 512))
        hat, scale = norm_parts(total)
        gains = vec_row(vec_ref, 6)
        output_ref[here, :] = (hat * gains + vec_row(vec_ref, 7)).astype(BF16)
        cotangent = cotangent_ref[here, :].astype(F32)
        grad_second = norm_back(hat, scale, gains, cotangent)
        grad_second_ref[here, :] = grad_second
        grad_low = grad_second.astype(BF16)
        turned_low = jnp.transpose(grad_low)
        for narrow in range(NARROW):
            grad_t[narrow ^ (me & 3), :, here] = turned_low[narrow * 128 : narrow * 128 + 128, :]
        sums_ref[0:1, :] += column_sum(grad_low.astype(F32))
        sums_ref[1:2, :] += column_sum(cotangent * hat)
        sums_ref[2:3, :] += column_sum(cotangent)
        return unused

    total_rows = attended_ref.shape[0]
    lax.fori_loop(0, total_rows // rows, per_rows, 0)
    grads = grad_t[...].reshape(512, total_rows)
    for wide in range(WIDE):
        columns = pl.ds(pl.multiple_of((wide ^ (me >> 2)) * 256, 256), 256)
        piece = nn(grads, active[:, columns])
        for narrow in range(NARROW):
            target = (keep_ref, send_ref)[narrow & 1]
            block = block_at(ORDER_SECOND, me, wide * NARROW + narrow)
            own = piece[narrow * 128 : narrow * 128 + 128]
            target[block, 0:128, :] = own[:, 0:128].astype(target.dtype)
            target[block, 128:256, :] = own[:, 128:256].astype(target.dtype)


def backward_kernel(
    direct,
    slope_ref,
    grad_second_ref,
    first_ref,
    low_t,
    attended_ref,
    vec_ref,
    w_out,
    w_in,
    w_back,
    grad_first_ref,
    grad_attended_ref,
    keep_ref,
    send_ref,
    sums_ref,
    bin_sums_ref,
    grad_pre,
    grad_branch,
    attended_t,
):
    rows = ROWS
    me = my_place() if direct else jnp.int32(0)
    sums_ref[...] = jnp.zeros_like(sums_ref)
    bin_sums_ref[...] = jnp.zeros_like(bin_sums_ref)

    def per_rows(step, unused):
        here = rows_at(step, rows)
        turned_low = jnp.transpose(attended_ref[here, :])
        for wide in range(WIDE):
            attended_t[wide ^ (me >> 2), :, here] = turned_low[wide * 64 : wide * 64 + 64, :]
        grad_hidden = grad_second_ref[here, :]
        grad_low = grad_hidden.astype(BF16)
        for chunk in range(8):
            columns = slice(chunk * 256, chunk * 256 + 256)
            weight = w_back[chunk * 4 : chunk * 4 + 4].reshape(256, 512)
            grad = (nt(grad_low, weight) * slope_ref[here, columns]).astype(BF16)
            grad_pre[here, columns] = grad
            grad_hidden += nt(grad, w_in_columns(w_in, chunk))
            sums = column_sum(grad.astype(F32))
            for part in range(2):
                row = 2 * (chunk % 4) + part
                bin_sums_ref[chunk // 4, row : row + 1, :] += sums[:, part * 128 : part * 128 + 128]
        hat, scale = norm_parts(first_ref[here, :])
        gains = vec_row(vec_ref, 4)
        grad_first = norm_back(hat, scale, gains, grad_hidden)
        grad_first_ref[here, :] = grad_first
        branch = grad_first.astype(BF16)
        grad_branch[here, :] = branch
        sums_ref[0:1, :] += column_sum(branch.astype(F32))
        sums_ref[1:2, :] += column_sum(grad_hidden * hat)
        sums_ref[2:3, :] += column_sum(grad_hidden)
        grad_attended_ref[here, :] = nt(branch, w_out[...]).astype(BF16)
        return unused

    total_rows = attended_ref.shape[0]
    lax.fori_loop(0, total_rows // rows, per_rows, 0)
    lows = low_t[...].reshape(512, total_rows)
    joined = attended_t[...].reshape(512, total_rows)
    for narrow in range(NARROW):
        target = (keep_ref, send_ref)[narrow & 1]
        at = narrow ^ (me & 3)
        for part in range(2):
            columns = pl.ds(pl.multiple_of(at * 512 + part * 256, 256), 256)
            piece = nn(lows, grad_pre[:, columns])
            for wide in range(WIDE):
                block = block_at(ORDER_SECOND, me, wide * NARROW + narrow)
                own = piece[wide * 64 : wide * 64 + 64]
                target[block, part * 2] = own[:, 0:128].astype(target.dtype)
                target[block, part * 2 + 1] = own[:, 128:256].astype(target.dtype)
        piece = nn(joined, grad_branch[:, pl.ds(pl.multiple_of(at * 128, 128), 128)])
        for wide in range(WIDE):
            block = block_at(ORDER_SECOND, me, wide * NARROW + narrow)
            target[block, 4] = piece[wide * 64 : wide * 64 + 64].astype(target.dtype)


def attend_back_kernel(
    direct,
    qkv_ref,
    grad_attended_ref,
    lse_ref,
    mixed_ref,
    grad_first_ref,
    sums_a_ref,
    sums_b_ref,
    bin_sums_ref,
    weights,
    bias,
    stream_ref,
    keep_ref,
    send_ref,
    mixed_t,
    grads,
    stream,
    vec_sums,
):
    windows, blocks = lse_ref.shape[1:3]
    length = blocks * 128
    me = my_place() if direct else jnp.int32(0)
    turned_low = jnp.transpose(mixed_ref[...])
    for wide in range(WIDE):
        mixed_t[wide ^ (me >> 2), :, :] = turned_low[wide * 64 : wide * 64 + 64, :]
    vec_sums[...] = jnp.zeros_like(vec_sums)
    for tile in range(4):
        lanes = slice(tile * 128, tile * 128 + 128)
        vec_sums[tile, 2:3, :] = sums_b_ref[0:1, lanes]
        vec_sums[tile, 3:4, :] = sums_a_ref[0:1, lanes]
        vec_sums[tile, 4:6, :] = sums_b_ref[1:3, lanes]
        vec_sums[tile, 6:8, :] = sums_a_ref[1:3, lanes]
    low = head_masks(128)

    def per_pair(core, upper, unused):
        apart = 2 * upper + core
        pair = (me & 3) ^ apart
        spans = block_spans(windows, length)
        lanes = pl.ds(pl.multiple_of(pair * 128, 128), 128)
        turned_keys = [
            jnp.transpose(
                qkv_ref[window * length : (window + 1) * length, part_lanes(pair, 1)]
            )
            for window in range(windows)
        ]
        queries, aboves, scores, grad_shares = [], [], [], []
        for window, block, here, there, span in spans:
            queries.append(stack_heads(qkv_ref[here, part_lanes(pair, 0)], low))
            aboves.append(stack_heads(grad_attended_ref[here, lanes], low))
            mask = bias[window, block, 0:span, :]
            mask = jnp.concatenate([mask, mask], axis=1)
            scores.append(
                nt(qkv_ref[there, part_lanes(pair, 1)], queries[-1])
                + (mask - lse_ref[pair, window, block : block + 1, :])
            )
            grad_shares.append(nt(qkv_ref[there, part_lanes(pair, 2)], aboves[-1]))
        shares, grad_scores = [], []
        for score, grad_share in zip(scores, grad_shares):
            share = jnp.exp(score)
            inner = jnp.sum(share * grad_share, axis=0, keepdims=True)
            shares.append(share.astype(BF16))
            grad_scores.append((share * (grad_share - inner)).astype(BF16))
        grad_keys = [[None] * (length // 128) for window in range(windows)]
        grad_values = [[None] * (length // 128) for window in range(windows)]
        for at, (window, block, here, there, span) in enumerate(spans):
            stop = block * 128 + 128
            for found, sums in (
                (nn(grad_scores[at], queries[at]), grad_keys[window]),
                (nn(shares[at], aboves[at]), grad_values[window]),
            ):
                for part in range(span // 128):
                    of = block - span // 128 + 1 + part
                    piece = found[part * 128 : part * 128 + 128]
                    sums[of] = piece if sums[of] is None else sums[of] + piece
            joined = nn(turned_keys[window][:, stop - span : stop], grad_scores[at])
            both = jnp.concatenate([joined[0:64, 0:128], joined[64:128, 128:256]], axis=0)
            grad = (jnp.transpose(both) * 0.125).astype(BF16)
            grads[here, part_lanes(apart, 0)] = grad
            vec_sums[pair, 0:1, :] += column_sum(grad.astype(F32))
        for window, block, here, there, span in spans:
            grads[here, part_lanes(apart, 1)] = grad_keys[window][block].astype(BF16)
            grad = grad_values[window][block].astype(BF16)
            grads[here, part_lanes(apart, 2)] = grad
            vec_sums[pair, 1:2, :] += column_sum(grad.astype(F32))
        return unused

    lax.fori_loop(0, 2, partial(per_pair, 0), 0)
    lax.fori_loop(0, 2, partial(per_pair, 1), 0)
    turned_mixed = mixed_t[...].reshape(512, windows * length)
    for chunk in range(6):
        weight_grads = nn(turned_mixed, grads[:, chunk * 256 : chunk * 256 + 256])
        for side in range(2):
            apart, part = divmod(chunk * 2 + side, 3)
            target = (keep_ref, send_ref)[apart & 1]
            for wide in range(WIDE):
                block = block_at(ORDER_FIRST, me, wide * NARROW + apart)
                target[block, part * 64 : part * 64 + 64, :] = weight_grads[
                    wide * 64 : wide * 64 + 64, side * 128 : side * 128 + 128
                ].astype(target.dtype)
    for row in range(0, length, 256):
        total = None
        for window in range(windows):
            rows = slice(window * length + row, window * length + row + 256)
            sums = grad_first_ref[rows, :]
            for apart in range(NARROW):
                lanes = pl.ds(pl.multiple_of(((me & 3) ^ apart) * 384, 128), 384)
                sums += nt(grads[rows, apart * 384 : apart * 384 + 384], weights[:, lanes])
            stream_ref[rows, :] = sums.astype(BF16)
            total = sums if total is None else total + sums
        stream[row : row + 256, :] = total
    for half, target in ((0, keep_ref), (1, send_ref)):
        for block in range(HALF):
            wide, narrow = place_of(ORDER_FIRST, me, half, block)
            target[block, 192:256, :] = stream[
                pl.ds(pl.multiple_of(wide * 64, 64), 64),
                pl.ds(pl.multiple_of(narrow * 128, 128), 128),
            ].astype(target.dtype)
            target[block, 256:264, :] = vec_sums[wide // 2].astype(target.dtype)
            target[block, 264:272, :] = bin_sums_ref[wide // 4].astype(target.dtype)


def doubled(row):
    return jnp.concatenate([row, row], axis=1)


def pack_kernel(
    w_query_ref,
    w_key_ref,
    w_value_ref,
    w_out_ref,
    w_in_ref,
    w_back_ref,
    table_ref,
    vectors_ref,
    in_bias_ref,
    first_ref,
    second_ref,
):
    wide, narrow = lax.axis_index("wide"), lax.axis_index("narrow")
    first_ref[0:64, :] = w_query_ref[...]
    first_ref[64:128, :] = w_key_ref[...]
    first_ref[128:192, :] = w_value_ref[...]
    first_ref[192:256, :] = table_ref[...]
    row = lax.broadcasted_iota(jnp.int32, (8, 128), 0)
    side = lax.broadcasted_iota(jnp.int32, (8, 128), 1) // 64
    vectors = doubled(vectors_ref[...].astype(F32))
    spread = jnp.where(row % 2 == 0, vectors[0:1], vectors[1:2])
    upper = jnp.where((row // 2 == narrow) & (side == wide % 2), spread, 0.0)
    spread = doubled(in_bias_ref[...].astype(F32))
    lower = jnp.where(
        (row == 2 * (wide % 4) + narrow // 2) & (side == narrow % 2), spread, 0.0
    )
    first_ref[256:272, :] = jnp.concatenate([upper, lower], axis=0).astype(BF16)
    second_ref[0] = w_out_ref[...]
    for part in range(4):
        second_ref[1 + part] = w_in_ref[:, part * 128 : part * 128 + 128]
        second_ref[5 + part] = w_back_ref[part * 64 : part * 64 + 64, :]


def finish_kernel(
    held_ref, came_ref, query_ref, key_ref, value_ref, table_ref, vectors_ref, in_bias_ref
):
    wide, narrow = lax.axis_index("wide"), lax.axis_index("narrow")
    total = held_ref[0] + came_ref[0].astype(F32)
    query_ref[...] = total[0:64]
    key_ref[...] = total[64:128]
    value_ref[...] = total[128:192]
    table_ref[...] = total[192:256]
    row = lax.broadcasted_iota(jnp.int32, (8, 128), 0)

    def side_of(rows, second):
        return jnp.where(second == 1, rows[:, 64:128], rows[:, 0:64])

    def row_of(rows, which):
        return column_sum(jnp.where(row == which, rows, 0.0))

    vectors = jnp.concatenate(
        [row_of(total[256:264], narrow * 2), row_of(total[256:264], narrow * 2 + 1)], axis=0
    )
    vectors_ref[...] = side_of(vectors, wide % 2)
    bins = row_of(total[264:272], 2 * (wide % 4) + narrow // 2)
    in_bias_ref[...] = side_of(bins, narrow % 2)


def vmem():
    return pl.BlockSpec(memory_space=pltpu.VMEM)


def hbm():
    return pl.BlockSpec(memory_space=pl.ANY)


def cost(macs, touched):
    return pl.CostEstimate(flops=2 * macs, bytes_accessed=touched, transcendentals=0)


def params(mebibytes):
    return pltpu.CompilerParams(vmem_limit_bytes=mebibytes << 20)


def shape(dims, dtype):
    return jax.ShapeDtypeStruct(dims, dtype)


def attend_call(direct, segments, x, blocks):
    windows, length = segments.shape
    total = windows * length
    return pl.pallas_call(
        partial(attend_kernel, direct),
        out_shape=(
            shape((total, 1536), BF16),
            shape((total, 512), BF16),
            shape((NARROW, windows, length // 128, 256), F32),
            shape((total, 512), F32),
            shape((total, 512), BF16),
            shape((4, 8, 128), F32),
            shape((2, 8, 128), F32),
            shape((512, 1536), BF16),
            shape((windows, length // 128, 384, 128), F32),
        ),
        in_specs=[vmem(), vmem()] + [hbm()] * 4,
        out_specs=tuple([vmem()] * 9),
        scratch_shapes=[
            pltpu.VMEM((512, 512), BF16),
            pltpu.VMEM((PLACES, 16, 128), BF16),
            pltpu.SemaphoreType.DMA((3,)),
        ],
        compiler_params=params(ATTEND_MIB),
        cost_estimate=cost(6000 << 20, 12 << 20),
        name="attend",
    )(segments, x, *blocks)


ROWS = 512
ATTEND_MIB = 24
FORWARD_MIB = 20
BACKWARD_MIB = 16
ATTEND_BACK_MIB = 32


def forward_call(direct, attended, passed, cotangent, vec, bins, blocks):
    total = attended.shape[0]
    return pl.pallas_call(
        partial(forward_kernel, direct),
        out_shape=(
            shape((total, 512), BF16),
            shape((total, 2048), F32),
            shape((total, 512), F32),
            shape((total, 512), F32),
            shape((WIDE, 64, total), BF16),
            shape((HALF, 256, 128), F32),
            shape((HALF, 256, 128), BF16),
            shape((8, 512), F32),
            shape((512, 512), BF16),
            shape((16, 512, 128), BF16),
            shape((32, 64, 512), BF16),
        ),
        in_specs=[vmem()] * 5 + [hbm()] * 4,
        out_specs=tuple([vmem()] * 11),
        scratch_shapes=[
            pltpu.VMEM((total, 2048), BF16),
            pltpu.VMEM((NARROW, 128, total), BF16),
            pltpu.SemaphoreType.DMA((3,)),
        ],
        compiler_params=params(FORWARD_MIB),
        cost_estimate=cost(6000 << 20, 24 << 20),
        name="forward",
    )(attended, passed, cotangent, vec, bins, *blocks)


def backward_call(direct, slope, grad_second, first_sum, low_t, attended, vec, weights):
    total = attended.shape[0]
    return pl.pallas_call(
        partial(backward_kernel, direct),
        out_shape=(
            shape((total, 512), F32),
            shape((total, 512), BF16),
            shape((HALF, 5, 64, 128), F32),
            shape((HALF, 5, 64, 128), BF16),
            shape((8, 512), F32),
            shape((2, 8, 128), F32),
        ),
        in_specs=[vmem()] * 9,
        out_specs=tuple([vmem()] * 6),
        scratch_shapes=[
            pltpu.VMEM((total, 2048), BF16),
            pltpu.VMEM((total, 512), BF16),
            pltpu.VMEM((WIDE, 64, total), BF16),
        ],
        compiler_params=params(BACKWARD_MIB),
        cost_estimate=cost(7000 << 20, 24 << 20),
        name="backward",
    )(slope, grad_second, first_sum, low_t, attended, vec, *weights)


def attend_back_call(direct, qkv, grad_attended, lse, mixed, grad_first, sums, weights, bias):
    windows, blocks = lse.shape[1:3]
    length = blocks * 128
    total = windows * length
    return pl.pallas_call(
        partial(attend_back_kernel, direct),
        out_shape=(
            shape((total, 512), BF16),
            shape((HALF, 272, 128), F32),
            shape((HALF, 272, 128), BF16),
        ),
        in_specs=[vmem()] * 10,
        out_specs=(vmem(), vmem(), vmem()),
        scratch_shapes=[
            pltpu.VMEM((WIDE, 64, total), BF16),
            pltpu.VMEM((total, 1536), BF16),
            pltpu.VMEM((length, 512), F32),
            pltpu.VMEM((4, 8, 128), F32),
        ],
        compiler_params=params(ATTEND_BACK_MIB),
        cost_estimate=cost(7000 << 20, 16 << 20),
        name="attend_back",
    )(qkv, grad_attended, lse, mixed, grad_first, *sums, weights, bias)


def pack_call(*shards):
    return pl.pallas_call(
        pack_kernel,
        out_shape=(shape((272, 128), BF16), shape((9, 64, 128), BF16)),
        in_specs=[vmem()] * 9,
        out_specs=(vmem(), vmem()),
        name="pack",
    )(*shards)


def finish_call(held, came):
    return pl.pallas_call(
        finish_kernel,
        out_shape=tuple([shape((64, 128), F32)] * 4 + [shape((2, 64), F32), shape((1, 64), F32)]),
        in_specs=[vmem()] * 2,
        out_specs=tuple([vmem()] * 6),
        name="finish",
    )(held, came)


def swap(array, order, step):
    return lax.ppermute(array, AXES, pairs(order, step))


def after(value, *others):
    return lax.optimization_barrier((value,) + others)[0]


def grow(held, order, step):
    return jnp.concatenate([held, swap(held, order, step)], axis=0)


def start_halving(keep, send, order):
    return keep, swap(send, order, 4)


def halve(held, came, order, step):
    size = 1 << step
    upper = (held[size:] + came[size:].astype(F32)).astype(BF16)
    lower = held[:size] + came[:size].astype(F32)
    return lower, swap(upper, order, step)


def small_block(vectors, in_bias, wide, narrow):
    row = lax.broadcasted_iota(jnp.int32, (8, 128), 0)
    side = lax.broadcasted_iota(jnp.int32, (8, 128), 1) // 64
    spread = jnp.tile(vectors, (4, 2))
    first = jnp.where((row // 2 == narrow) & (side == wide % 2), spread, 0)
    spread = jnp.tile(in_bias[None], (8, 2))
    second = jnp.where((row == 2 * (wide % 4) + narrow // 2) & (side == narrow % 2), spread, 0)
    return jnp.concatenate([first, second], axis=0).astype(BF16)


def first_block(w_query, w_key, w_value, table, small):
    return jnp.concatenate([w_query, w_key, w_value, table, small], axis=0)


def second_block(w_out, w_in, w_back):
    return jnp.concatenate(
        [w_out[None]]
        + [w_in[None, :, part * 128 : part * 128 + 128] for part in range(4)]
        + [w_back.reshape(4, 64, 128)],
        axis=0,
    )


def turned(total):
    return jnp.concatenate([total[0:128].T, total[128:256].T], axis=0)


def per_device(
    inputs,
    segment_ids,
    cotangent,
    w_query,
    w_key,
    w_value,
    w_out,
    w_in,
    w_back,
    position_table,
    vectors,
    in_bias,
):
    windows, length, features = inputs.shape
    rows = windows * length
    x = inputs.reshape(rows, features)
    early, late = pack_call(
        w_query, w_key, w_value, w_out, w_in, w_back, position_table, vectors, in_bias[None]
    )
    early, late = early[None], late[None]
    early = grow(early, ORDER_FIRST, 0)
    for step in range(3):
        early_came = swap(early, ORDER_FIRST, step + 1)
        late_came = swap(late, ORDER_SECOND, step)
        early_came, late_came = lax.optimization_barrier((early_came, late_came))
        if step < 2:
            early = jnp.concatenate([early, early_came], axis=0)
        else:
            early_far = early_came
        late = jnp.concatenate([late, late_came], axis=0)
    first = (early, early_far, swap(early, ORDER_FIRST, 4), swap(early_far, ORDER_FIRST, 4))
    late_far = swap(late, ORDER_SECOND, 3)
    qkv, attended, lse, passed, mixed, vec, bins, w_qkv, bias = attend_call(
        True, segment_ids, after(x, late), first
    )
    late_far = after(late_far, attended)
    second = (late, late_far, swap(late, ORDER_SECOND, 4), swap(late_far, ORDER_SECOND, 4))
    output, slope, grad_second, first_sum, low_t, keep_back, send_back, sums_a, *whole = forward_call(
        True, attended, passed, cotangent.reshape(rows, features), vec, bins, second
    )
    back = start_halving(keep_back, send_back, ORDER_SECOND)
    grad_first, grad_attended, keep_in, send_in, sums_b, bin_sums = backward_call(
        True, slope, grad_second, first_sum, low_t, attended, vec, whole
    )
    back = halve(*back, ORDER_SECOND, 3)
    inner = start_halving(keep_in, send_in, ORDER_SECOND)
    stream, keep_first, send_first = attend_back_call(
        True,
        qkv,
        after(grad_attended, back[0]),
        lse,
        mixed,
        grad_first,
        (sums_a, sums_b, bin_sums),
        w_qkv,
        bias,
    )
    keep_first, send_first, back_came, inner_came = lax.optimization_barrier(
        (keep_first, send_first, back[1], inner[1])
    )
    outer = start_halving(keep_first, send_first, ORDER_FIRST)
    back = halve(back[0], back_came, ORDER_SECOND, 2)
    inner = halve(inner[0], inner_came, ORDER_SECOND, 3)
    for step in (2, 1, 0):
        outer = halve(*outer, ORDER_FIRST, step + 1)
        if step > 0:
            back = halve(back[0], after(back[1], outer[1]), ORDER_SECOND, step - 1)
        inner = halve(inner[0], after(inner[1], outer[1]), ORDER_SECOND, step)
    outer = halve(*outer, ORDER_FIRST, 0)
    back = back[0][0] + back[1][0].astype(F32)
    inner = inner[0][0] + inner[1][0].astype(F32)
    grad_query, grad_key, grad_value, grad_table, vec, bins = finish_call(*outer)
    return (
        output.reshape(inputs.shape),
        stream.reshape(inputs.shape),
        grad_query,
        grad_key,
        grad_value,
        inner[4],
        jnp.concatenate([inner[part] for part in range(4)], axis=1),
        turned(back),
        grad_table,
        vec,
        bins[0],
    )


def listed(order):
    return block_masks(order, 0) + [1 ^ mask for mask in block_masks(order, 1)]


def canonical(array, axis_tiles):
    rows, columns = array.shape
    across, along = axis_tiles
    return (
        array.reshape(across, rows // across, along, columns // along)
        .transpose(0, 2, 1, 3)
        .reshape(PLACES, rows // across, columns // along)
    )


def uncanonical(blocks, rows, columns):
    return (
        blocks.reshape(WIDE, NARROW, rows // WIDE, columns // NARROW)
        .transpose(0, 2, 1, 3)
        .reshape(rows, columns)
    )


def per_device_any(
    inputs,
    segment_ids,
    cotangent,
    w_query,
    w_key,
    w_value,
    w_out,
    w_in,
    w_back,
    position_table,
    vectors,
    in_bias,
):
    def whole(array):
        array = lax.all_gather(array, "narrow", axis=1, tiled=True)
        return lax.all_gather(array, "wide", axis=0, tiled=True)

    def fours(blocks, order):
        blocks = jnp.stack([blocks[place] for place in listed(order)])
        return tuple(blocks[at * 8 : at * 8 + 8] for at in range(4))

    vectors = lax.all_gather(vectors, "narrow", axis=0, tiled=True)
    vectors = lax.all_gather(vectors, "wide", axis=1, tiled=True)
    in_bias = lax.all_gather(in_bias, AXES, axis=0, tiled=True)
    places = jnp.arange(PLACES)
    pieces = vectors.reshape(NARROW, 2, WIDE, 64).transpose(2, 0, 1, 3).reshape(PLACES, 2, 64)
    small = jax.vmap(small_block)(
        pieces, in_bias.reshape(PLACES, 64), places // NARROW, places % NARROW
    )
    tiles = (WIDE, NARROW)
    first = jax.vmap(first_block)(
        canonical(whole(w_query), tiles),
        canonical(whole(w_key), tiles),
        canonical(whole(w_value), tiles),
        canonical(whole(position_table), tiles),
        small,
    )
    second = jax.vmap(second_block)(
        canonical(whole(w_out), tiles),
        canonical(whole(w_in), tiles),
        canonical(whole(w_back), tiles),
    )
    windows, length, features = inputs.shape
    rows = windows * length
    first, second = fours(first, ORDER_FIRST), fours(second, ORDER_SECOND)
    qkv, attended, lse, passed, mixed, vec, bins, w_qkv, bias = attend_call(
        False, segment_ids, inputs.reshape(rows, features), first
    )
    output, slope, grad_second, first_sum, low_t, keep_back, send_back, sums_a, *whole_w = forward_call(
        False, attended, passed, cotangent.reshape(rows, features), vec, bins, second
    )
    grad_first, grad_attended, keep_in, send_in, sums_b, bin_sums = backward_call(
        False, slope, grad_second, first_sum, low_t, attended, vec, whole_w
    )
    stream, keep_first, send_first = attend_back_call(
        False,
        qkv,
        grad_attended,
        lse,
        mixed,
        grad_first,
        (sums_a, sums_b, bin_sums),
        w_qkv,
        bias,
    )

    def joined(pair, order):
        both = jnp.concatenate([pair[0], pair[1].astype(F32)], axis=0)
        return jnp.stack([both[listed(order).index(place)] for place in range(PLACES)])

    def summed(array):
        array = lax.psum_scatter(array, "wide", scatter_dimension=0, tiled=True)
        return lax.psum_scatter(array, "narrow", scatter_dimension=1, tiled=True)

    back = joined((keep_back, send_back), ORDER_SECOND)
    inner = joined((keep_in, send_in), ORDER_SECOND)
    outer = joined((keep_first, send_first), ORDER_FIRST)
    back = jax.vmap(turned)(back)
    grad_in = inner[:, 0:4].transpose(0, 2, 1, 3).reshape(PLACES, 64, 512)
    vec = outer.reshape(WIDE, NARROW, 272, 128)[::2, 0, 256:264]
    vec = vec.transpose(1, 0, 2).reshape(8, 512)
    vec = lax.psum_scatter(vec, "wide", scatter_dimension=1, tiled=True)
    vec = lax.psum_scatter(vec, "narrow", scatter_dimension=0, tiled=True)
    bins = outer.reshape(WIDE, NARROW, 272, 128)[::4, 0, 264:272].reshape(2048)
    bins = lax.psum_scatter(bins, AXES, scatter_dimension=0, tiled=True)
    return (
        output.reshape(inputs.shape),
        stream.reshape(inputs.shape),
        summed(uncanonical(outer[:, 0:64], 512, 512)),
        summed(uncanonical(outer[:, 64:128], 512, 512)),
        summed(uncanonical(outer[:, 128:192], 512, 512)),
        summed(uncanonical(inner[:, 4], 512, 512)),
        summed(uncanonical(grad_in, 512, 2048)),
        summed(uncanonical(back, 2048, 512)),
        summed(uncanonical(outer[:, 192:256], 512, 512)),
        vec,
        bins,
    )


def solution(mesh):
    matrix = P("wide", "narrow")
    rows = P(AXES, None, None)
    direct = mesh.shape["wide"] == WIDE and mesh.shape["narrow"] == NARROW
    return jax.shard_map(
        per_device if direct else per_device_any,
        mesh=mesh,
        in_specs=(
            rows,
            P(AXES, None),
            rows,
            matrix,
            matrix,
            matrix,
            matrix,
            matrix,
            matrix,
            matrix,
            P("narrow", "wide"),
            P(AXES),
        ),
        out_specs=(
            rows,
            rows,
            matrix,
            matrix,
            matrix,
            matrix,
            matrix,
            matrix,
            matrix,
            P("narrow", "wide"),
            P(AXES),
        ),
        check_vma=False,
    )
```

time: 214 us -> 151 us (0.71)
  Pallas kernels: 85.5 us -> 49.6 us
  starting transfers between devices: 40.7 us -> 26.4 us
  local copies, waits for them, and re-layouts: 12.2 us -> 6.8 us
  waiting for transfers between devices: 65.3 us -> 61.6 us
  other arithmetic: 8.17 us -> 5.91 us
    pallas_call x3 -> x5, Pallas kernels: 61.4 us -> 36.1 us  [the longest x1 14.1 us: forward_call(): pl.pallas_call(partial(forward_kernel, direct), out_shape=(shape((total,...]
    ppermute x27, starting transfers between devices: 40.7 us -> 26.4 us  [swap(): return lax.ppermute(array, AXES, pairs(order, step))]
    pallas_call x1, Pallas kernels: 24.1 us -> 13.5 us  [attend_back_call(): pl.pallas_call(partial(attend_back_kernel, direct), out_shape=(shape((tot...]
    add x15 -> x2, other arithmetic: 5.47 us -> 0.05 us  [the longest x1 0.03 us: per_device(): inner = inner[0][0] + inner[1][0].astype(F32)]
    ppermute x27, waiting for transfers between devices: 65.3 us -> 61.6 us  [swap(): return lax.ppermute(array, AXES, pairs(order, step))]
    slice x14 -> x0, local copies, waits for them, and re-layouts: 2.86 us -> none  [the longest x12 2.21 us: scatter_sum(): total[size:].astype(BF16)]
    convert_element_type x0 -> x12, other arithmetic: none -> 2.21 us  [halve(): upper = (held[size:] + came[size:].astype(F32)).astype(BF16)]
    unnamed x46 -> x25, local copies, waits for them, and re-layouts: 7.11 us -> 6.16 us
  transfers between devices with their start and end apart: 27 -> 27, of which waited for: 16 -> 17; matrix products, arithmetic and copies ran while one was open for 5% -> 3% of each run, Pallas kernels for 31% -> 22%
where the time goes in v2:
time: 151 us
  waiting for transfers between devices  61.6 us (41%)
  Pallas kernels  49.6 us (33%)
  starting transfers between devices  26.4 us (17%)
  local copies, waits for them, and re-layouts  6.8 us (5%)
  other arithmetic  5.91 us (4%)
    ppermute x27, waiting for transfers between devices, swap(): return lax.ppermute(array, AXES, pairs(order, step))  61.6 us
    ppermute x27, starting transfers between devices, swap(): return lax.ppermute(array, AXES, pairs(order, step))  26.4 us
    pallas_call x1, Pallas kernels, forward_call(): pl.pallas_call(partial(forward_kernel, direct), out_shape=(shape((total,...  14.1 us
    pallas_call x1, Pallas kernels, attend_back_call(): pl.pallas_call(partial(attend_back_kernel, direct), out_shape=(shape((tot...  13.5 us
    pallas_call x1, Pallas kernels, backward_call(): pl.pallas_call(partial(backward_kernel, direct), out_shape=(shape((total,...  10.2 us
    pallas_call x1, Pallas kernels, attend_call(): pl.pallas_call(partial(attend_kernel, direct), out_shape=(shape((total, 1...  8.49 us
    unnamed x25, local copies, waits for them, and re-layouts  6.16 us
  transfers between devices with their start and end apart: 27, of which 17 were waited for; matrix products, arithmetic and copies ran while one was open for 3% of the time, Pallas kernels for 22%

profile of v2, /device:TPU:0, one launch (start us, length us, event | category | flops | bytes accessed | tf_op | source)
XLA Modules:
  0.0 151.2 jit_solution(13155776537189904530)
XLA Ops:
  0.6 1.7 %pack.1 = (bf16[272,128]{1,0:T(8,128)(2,1)}, bf16[9,64,128]{2,1,0:T(8,128)(2,1)}) custom-call(bf16[64,128]{1,0:T(8,128)(2,1)} %w_query_ref.1, bf16[64,128]{1,0:T(8,128)(2,1)} %w_key_ref.1, bf16[64,128]{1,0:T(8,128)(2,1)} %w_value_ref.1, bf16[64,128]{1,0:T(8,128)(2,1)} %w_out_ref.1, bf16[64,512]{1,0:T(8,128)(2,1)} %w_in_ref.1, bf16[256,128]{1,0:T(8,128)(2,1)} %w_back_ref.1, ...), custom_call_target="tpu_custom_call" | custom-call | tf_op jit(solution)/shard_map/pack/pallas_call | solution.py:786
  2.3 4.1 %collective-permute-start = (bf16[1,272,128]{2,1,0:T(8,128)(2,1)}, bf16[1,272,128]{2,1,0:T(8,128)(2,1)S(1)}, u32[]{:S(2)}, u32[]{:S(2)}) collective-permute-start(bf16[1,272,128]{2,1,0:T(8,128)(2,1)} %bitcast.32), channel_id=1, source_target_pairs={{0,16},{1,9},{2,18},{3,11},{4,20},{5,13},{6,22},{7,15},{8,24},{9,1... | collective-permute-start | bytes 208904 | tf_op jit(solution)/shard_map/ppermute | solution.py:806
  6.5 2.5 %collective-permute-done = bf16[1,272,128]{2,1,0:T(8,128)(2,1)S(1)} collective-permute-done((bf16[1,272,128]{2,1,0:T(8,128)(2,1)}, bf16[1,272,128]{2,1,0:T(8,128)(2,1)S(1)}, u32[]{:S(2)}, u32[]{:S(2)}) %collective-permute-start) | collective-permute-done | bytes 69664 | tf_op jit(solution)/shard_map/ppermute | solution.py:806
  9.9 1.9 %collective-permute-start.1 = (bf16[2,272,128]{2,1,0:T(8,128)(2,1)S(1)}, bf16[2,272,128]{2,1,0:T(8,128)(2,1)S(1)}, u32[]{:S(2)}, u32[]{:S(2)}) collective-permute-start(bf16[2,272,128]{2,1,0:T(8,128)(2,1)S(1)} %pad_maximum_fusion.5), channel_id=1, source_target_pairs={{0,4},{1,3},{2,6},{3,1},{4,0},{5,7},{6,2},{7,5},{8,12},{9,11},{10,... | collective-permute-start | bytes 417800 | tf_op jit(solution)/shard_map/ppermute | solution.py:806
  11.8 2.4 %collective-permute-done.2 = bf16[1,9,64,128]{3,2,1,0:T(8,128)(2,1)S(1)} collective-permute-done((bf16[1,9,64,128]{3,2,1,0:T(8,128)(2,1)}, bf16[1,9,64,128]{3,2,1,0:T(8,128)(2,1)S(1)}, u32[]{:S(2)}, u32[]{:S(2)}) %collective-permute-start.2) | collective-permute-done | bytes 147488 | tf_op jit(solution)/shard_map/ppermute | solution.py:806
  16.0 3.5 %collective-permute-start.4 = (bf16[2,9,64,128]{3,2,1,0:T(8,128)(2,1)S(1)}, bf16[2,9,64,128]{3,2,1,0:T(8,128)(2,1)S(1)}, u32[]{:S(2)}, u32[]{:S(2)}) collective-permute-start(bf16[2,9,64,128]{3,2,1,0:T(8,128)(2,1)S(1)} %pad_maximum_fusion.3), channel_id=1, source_target_pairs={{0,8},{1,17},{2,10},{3,19},{4,12},{5,21},{6,14},{7,23},{8,0},{9,25... | collective-permute-start | bytes 884744 | tf_op jit(solution)/shard_map/ppermute | solution.py:806
  22.0 6.5 %collective-permute-done.3 = bf16[4,272,128]{2,1,0:T(8,128)(2,1)S(1)} collective-permute-done((bf16[4,272,128]{2,1,0:T(8,128)(2,1)S(1)}, bf16[4,272,128]{2,1,0:T(8,128)(2,1)S(1)}, u32[]{:S(2)}, u32[]{:S(2)}) %collective-permute-start.3) | collective-permute-done | bytes 278560 | tf_op jit(solution)/shard_map/ppermute | solution.py:806
  30.2 14.9 %collective-permute-done.5.p1_ref = bf16[8,272,128]{2,1,0:T(8,128)(2,1)S(1)} collective-permute-done((bf16[8,272,128]{2,1,0:T(8,128)(2,1)S(1)}, bf16[8,272,128]{2,1,0:T(8,128)(2,1)S(1)}, u32[]{:S(2)}, u32[]{:S(2)}) %collective-permute-start.5) | collective-permute-done | bytes 557088 | tf_op jit(solution)/shard_map/ppermute | solution.py:806
  47.0 8.5 %attend.1 = (bf16[1024,1536]{1,0:T(8,128)(2,1)S(1)}, bf16[1024,512]{1,0:T(8,128)(2,1)S(1)}, f32[4,2,4,256]{3,2,1,0:T(4,128)S(1)}, f32[1024,512]{1,0:T(8,128)S(1)...) custom-call(s32[2,512]{1,0:T(2,128)S(1)} %copy-done.2, ...), custom_call_target="tpu_custom_call" | custom-call | flops 12582912000 | bytes 12582912 | tf_op jit(solution)/shard_map/attend/pallas_call | solution.py:672
  55.5 1.6 %copy-done.3 = bf16[1024,1536]{1,0:T(8,128)(2,1)} copy-done((bf16[1024,1536]{1,0:T(8,128)(2,1)}, bf16[1024,1536]{1,0:T(8,128)(2,1)S(1)}, u32[]{:S(2)}) %copy-start.3) | copy-done | bytes 3145752
  59.3 2.7 %collective-permute-done.9.p1_ref = bf16[8,9,64,128]{3,2,1,0:T(8,128)(2,1)S(1)} collective-permute-done((bf16[8,9,64,128]{3,2,1,0:T(8,128)(2,1)S(1)}, bf16[8,9,64,128]{3,2,1,0:T(8,128)(2,1)S(1)}, u32[]{:S(2)}, u32[]{:S(2)}) %collective-permute-start.9) | collective-permute-done | bytes 1179680 | tf_op jit(solution)/shard_map/ppermute | solution.py:806
  62.0 2.8 %collective-permute-done.11.p3_ref = bf16[8,9,64,128]{3,2,1,0:T(8,128)(2,1)S(1)} collective-permute-done((bf16[8,9,64,128]{3,2,1,0:T(8,128)(2,1)S(1)}, bf16[8,9,64,128]{3,2,1,0:T(8,128)(2,1)S(1)}, u32[]{:S(2)}, u32[]{:S(2)}) %collective-permute-start.11) | collective-permute-done | bytes 1179680 | tf_op jit(solution)/shard_map/ppermute | solution.py:806
  64.8 14.1 %forward.1 = (bf16[1024,512]{1,0:T(8,128)(2,1)}, f32[1024,2048]{1,0:T(8,128)S(1)}, f32[1024,512]{1,0:T(8,128)S(1)}, f32[1024,512]{1,0:T(8,128)S(1)}, bf16[8,64,1...) custom-call(bf16[1024,512]{1,0:T(8,128)(2,1)S(1)} %get-tuple-element, ...), custom_call_target="tpu_custom_call" | custom-call | flops 12582912000 | bytes 25165824 | tf_op jit(solution)/shard_map/forward/pallas_call | solution.py:707
  79.1 10.2 %backward.1 = (f32[1024,512]{1,0:T(8,128)S(1)}, bf16[1024,512]{1,0:T(8,128)(2,1)S(1)}, f32[16,5,64,128]{3,2,1,0:T(8,128)S(1)}, bf16[16,5,64,128]{3,2,1,0:T(8,128...) custom-call(f32[1024,2048]{1,0:T(8,128)S(1)} %get-tuple-element.82.slope_ref, ...), custom_call_target="tpu_custom_call" | custom-call | flops 14680064000 | bytes 25165824 | tf_op jit(solution)/shard_map/backward/pallas_call | solution.py:737
  92.0 13.5 %attend_back.1 = (bf16[1024,512]{1,0:T(8,128)(2,1)}, f32[16,272,128]{2,1,0:T(8,128)S(1)}, bf16[16,272,128]{2,1,0:T(8,128)(2,1)S(1)}) custom-call(bf16[1024,1536]{1,0:T(8,128)(2,1)S(1)} %copy-done.4, bf16[1024,512]{1,0:T(8,128)(2,1)S(1)} %get-tuple-element.92.grad_attended_ref, f32[4,2,4,256]{3,2,1,0:T(4,128)S(1)} %get-tuple-element.93.lse_ref, ...), custom_call_target="tpu_custom_call" | custom-call | flops 14680064000 | bytes 16777216 | tf_op jit(solution)/shard_map/attend_back/pallas_call | solution.py:764
  105.7 2.5 %collective-permute-done.15 = bf16[16,272,128]{2,1,0:T(8,128)(2,1)S(1)} collective-permute-done((bf16[16,272,128]{2,1,0:T(8,128)(2,1)S(1)}, bf16[16,272,128]{2,1,0:T(8,128)(2,1)S(1)}, u32[]{:S(2)}, u32[]{:S(2)}) %collective-permute-start.15) | collective-permute-done | bytes 1114144 | tf_op jit(solution)/shard_map/ppermute | solution.py:806
  111.1 5.6 %collective-permute-done.24 = bf16[4,256,128]{2,1,0:T(8,128)(2,1)S(1)} collective-permute-done((bf16[4,256,128]{2,1,0:T(8,128)(2,1)S(1)}, bf16[4,256,128]{2,1,0:T(8,128)(2,1)S(1)}, u32[]{:S(2)}, u32[]{:S(2)}) %collective-permute-start.24) | collective-permute-done | bytes 262176 | tf_op jit(solution)/shard_map/ppermute | solution.py:806
  116.7 7.3 %collective-permute-done.16 = bf16[8,272,128]{2,1,0:T(8,128)(2,1)S(1)} collective-permute-done((bf16[8,272,128]{2,1,0:T(8,128)(2,1)S(1)}, bf16[8,272,128]{2,1,0:T(8,128)(2,1)S(1)}, u32[]{:S(2)}, u32[]{:S(2)}) %collective-permute-start.16) | collective-permute-done | bytes 557088 | tf_op jit(solution)/shard_map/ppermute | solution.py:806
  126.4 5.0 %collective-permute-done.25 = bf16[2,256,128]{2,1,0:T(8,128)(2,1)S(1)} collective-permute-done((bf16[2,256,128]{2,1,0:T(8,128)(2,1)S(1)}, bf16[2,256,128]{2,1,0:T(8,128)(2,1)S(1)}, u32[]{:S(2)}, u32[]{:S(2)}) %collective-permute-start.25) | collective-permute-done | bytes 131104 | tf_op jit(solution)/shard_map/ppermute | solution.py:806
  131.4 2.0 %collective-permute-done.17 = bf16[4,272,128]{2,1,0:T(8,128)(2,1)S(1)} collective-permute-done((bf16[4,272,128]{2,1,0:T(8,128)(2,1)S(1)}, bf16[4,272,128]{2,1,0:T(8,128)(2,1)S(1)}, u32[]{:S(2)}, u32[]{:S(2)}) %collective-permute-start.17) | collective-permute-done | bytes 278560 | tf_op jit(solution)/shard_map/ppermute | solution.py:806
  133.8 4.3 %collective-permute-start.22 = (bf16[2,5,64,128]{3,2,1,0:T(8,128)(2,1)S(1)}, bf16[2,5,64,128]{3,2,1,0:T(8,128)(2,1)S(1)}, u32[]{:S(2)}, u32[]{:S(2)}) collective-permute-start(bf16[2,5,64,128]{3,2,1,0:T(8,128)(2,1)S(1)} %get-tuple-element.144), channel_id=1, source_target_pairs={{0,8},{1,17},{2,10},{3,19},{4,12},{5,21},{6,14},{7,23},{8,0},{9,25... | collective-permute-start | bytes 491528 | tf_op jit(solution)/shard_map/ppermute | solution.py:806
  138.1 2.9 %collective-permute-done.26 = bf16[1,256,128]{2,1,0:T(8,128)(2,1)S(1)} collective-permute-done((bf16[1,256,128]{2,1,0:T(8,128)(2,1)S(1)}, bf16[1,256,128]{2,1,0:T(8,128)(2,1)S(1)}, u32[]{:S(2)}, u32[]{:S(2)}) %collective-permute-start.26) | collective-permute-done | bytes 65568 | tf_op jit(solution)/shard_map/ppermute | solution.py:806
  145.5 1.8 %collective-permute-done.19.came_ref = bf16[1,272,128]{2,1,0:T(8,128)(2,1)S(1)} collective-permute-done((bf16[1,272,128]{2,1,0:T(8,128)(2,1)S(1)}, bf16[1,272,128]{2,1,0:T(8,128)(2,1)S(1)}, u32[]{:S(2)}, u32[]{:S(2)}) %collective-permute-start.19) | collective-permute-done | bytes 69664 | tf_op jit(solution)/shard_map/ppermute | solution.py:806
  148.0 1.7 %finish.1 = (f32[64,128]{1,0:T(8,128)}, f32[64,128]{1,0:T(8,128)}, f32[64,128]{1,0:T(8,128)}, f32[64,128]{1,0:T(8,128)}, f32[2,64]{1,0:T(2,128)}, /*index=5*/f32[1,64]{1,0:T(1,128)}) custom-call(f32[1,272,128]{2,1,0:T(8,128)} %get-tuple-element.151.held_ref, bf16[1,272,128]{2,1,0:T(8,128)(2,1)} %copy-done.11), custom_call_target="tpu_custom_call" | custom-call | tf_op jit(solution)/shard_map/finish/pallas_call | solution.py:796
  (85 shorter events, 26.3 us)
Async XLA Ops:
  2.3 6.7 %collective-permute-start = (bf16[1,272,128]{2,1,0:T(8,128)(2,1)}, bf16[1,272,128]{2,1,0:T(8,128)(2,1)S(1)}, u32[]{:S(2)}, u32[]{:S(2)}) collective-permute-start(bf16[1,272,128]{2,1,0:T(8,128)(2,1)} %bitcast.32), channel_id=1, source_target_pairs={{0,16},{1,9},{2,18},{3,11},{4,20},{5,13},{6,22},{7,15},{8,24},{9,1... | collective-permute-start | bytes 208904 | tf_op jit(solution)/shard_map/ppermute | solution.py:806
  6.4 7.8 %collective-permute-start.2 = (bf16[1,9,64,128]{3,2,1,0:T(8,128)(2,1)}, bf16[1,9,64,128]{3,2,1,0:T(8,128)(2,1)S(1)}, u32[]{:S(2)}, u32[]{:S(2)}) collective-permute-start(bf16[1,9,64,128]{3,2,1,0:T(8,128)(2,1)} %bitcast.28), channel_id=1, source_target_pairs={{0,16},{1,9},{2,18},{3,11},{4,20},{5,13},{6,22},{7,15},{8,24},{9,1... | collective-permute-start | bytes 442376 | tf_op jit(solution)/shard_map/ppermute | solution.py:806
  9.9 5.1 %collective-permute-start.1 = (bf16[2,272,128]{2,1,0:T(8,128)(2,1)S(1)}, bf16[2,272,128]{2,1,0:T(8,128)(2,1)S(1)}, u32[]{:S(2)}, u32[]{:S(2)}) collective-permute-start(bf16[2,272,128]{2,1,0:T(8,128)(2,1)S(1)} %pad_maximum_fusion.5), channel_id=1, source_target_pairs={{0,4},{1,3},{2,6},{3,1},{4,0},{5,7},{6,2},{7,5},{8,12},{9,11},{10,... | collective-permute-start | bytes 417800 | tf_op jit(solution)/shard_map/ppermute | solution.py:806
  16.0 12.5 %collective-permute-start.4 = (bf16[2,9,64,128]{3,2,1,0:T(8,128)(2,1)S(1)}, bf16[2,9,64,128]{3,2,1,0:T(8,128)(2,1)S(1)}, u32[]{:S(2)}, u32[]{:S(2)}) collective-permute-start(bf16[2,9,64,128]{3,2,1,0:T(8,128)(2,1)S(1)} %pad_maximum_fusion.3), channel_id=1, source_target_pairs={{0,8},{1,17},{2,10},{3,19},{4,12},{5,21},{6,14},{7,23},{8,0},{9,25... | collective-permute-start | bytes 884744 | tf_op jit(solution)/shard_map/ppermute | solution.py:806
  20.4 8.1 %collective-permute-start.3 = (bf16[4,272,128]{2,1,0:T(8,128)(2,1)S(1)}, bf16[4,272,128]{2,1,0:T(8,128)(2,1)S(1)}, u32[]{:S(2)}, u32[]{:S(2)}) collective-permute-start(bf16[4,272,128]{2,1,0:T(8,128)(2,1)S(1)} %pad_maximum_fusion.4), channel_id=1, source_target_pairs={{0,2},{1,5},{2,0},{3,7},{4,6},{5,1},{6,4},{7,3},{8,10},{9,13},{10,... | collective-permute-start | bytes 835592 | tf_op jit(solution)/shard_map/ppermute | solution.py:806
  28.6 16.5 %collective-permute-start.6 = (bf16[4,9,64,128]{3,2,1,0:T(8,128)(2,1)S(1)}, bf16[4,9,64,128]{3,2,1,0:T(8,128)(2,1)S(1)}, u32[]{:S(2)}, u32[]{:S(2)}) collective-permute-start(bf16[4,9,64,128]{3,2,1,0:T(8,128)(2,1)S(1)} %pad_maximum_fusion.1), channel_id=1, source_target_pairs={{0,4},{1,3},{2,6},{3,1},{4,0},{5,7},{6,2},{7,5},{8,12},{9,11},{10,... | collective-permute-start | bytes 1769480 | tf_op jit(solution)/shard_map/ppermute | solution.py:806
  30.0 15.0 %collective-permute-start.5 = (bf16[8,272,128]{2,1,0:T(8,128)(2,1)S(1)}, bf16[8,272,128]{2,1,0:T(8,128)(2,1)S(1)}, u32[]{:S(2)}, u32[]{:S(2)}) collective-permute-start(bf16[8,272,128]{2,1,0:T(8,128)(2,1)S(1)} %pad_maximum_fusion.2.p0_ref), channel_id=1, source_target_pairs={{0,8},{1,17},{2,10},{3,19},{4,12},{5,21},{6,14},{7,23},{8,0},{9,25... | collective-permute-start | bytes 1671176 | tf_op jit(solution)/shard_map/ppermute | solution.py:806
  30.1 16.7 %collective-permute-start.7 = (bf16[8,272,128]{2,1,0:T(8,128)(2,1)S(1)}, bf16[8,272,128]{2,1,0:T(8,128)(2,1)S(1)}, u32[]{:S(2)}, u32[]{:S(2)}) collective-permute-start(bf16[8,272,128]{2,1,0:T(8,128)(2,1)S(1)} %pad_maximum_fusion.2.p0_ref), channel_id=1, source_target_pairs={{0,1},{1,0},{2,3},{3,2},{4,5},{5,4},{6,7},{7,6},{8,9},{9,8},{10,11... | collective-permute-start | bytes 1671176 | tf_op jit(solution)/shard_map/ppermute | solution.py:806
  45.2 16.8 %collective-permute-start.10 = (bf16[8,9,64,128]{3,2,1,0:T(8,128)(2,1)S(1)}, bf16[8,9,64,128]{3,2,1,0:T(8,128)(2,1)S(1)}, u32[]{:S(2)}, u32[]{:S(2)}) collective-permute-start(bf16[8,9,64,128]{3,2,1,0:T(8,128)(2,1)S(1)} %pad_maximum_fusion.p0_ref), channel_id=1, source_target_pairs={{0,1},{1,0},{2,3},{3,2},{4,5},{5,4},{6,7},{7,6},{8,9},{9,8},{10,11... | collective-permute-start | bytes 3538952 | tf_op jit(solution)/shard_map/ppermute | solution.py:806
  45.8 16.2 %collective-permute-start.9 = (bf16[8,9,64,128]{3,2,1,0:T(8,128)(2,1)S(1)}, bf16[8,9,64,128]{3,2,1,0:T(8,128)(2,1)S(1)}, u32[]{:S(2)}, u32[]{:S(2)}) collective-permute-start(bf16[8,9,64,128]{3,2,1,0:T(8,128)(2,1)S(1)} %pad_maximum_fusion.p0_ref), channel_id=1, source_target_pairs={{0,2},{1,5},{2,0},{3,7},{4,6},{5,1},{6,4},{7,3},{8,10},{9,13},{10,... | collective-permute-start | bytes 3538952 | tf_op jit(solution)/shard_map/ppermute | solution.py:806
  78.9 10.8 %collective-permute-start.12 = (bf16[16,256,128]{2,1,0:T(8,128)(2,1)S(1)}, bf16[16,256,128]{2,1,0:T(8,128)(2,1)S(1)}, u32[]{:S(2)}, u32[]{:S(2)}) collective-permute-start(bf16[16,256,128]{2,1,0:T(8,128)(2,1)S(1)} %get-tuple-element.91), channel_id=1, source_target_pairs={{0,1},{1,0},{2,3},{3,2},{4,5},{5,4},{6,7},{7,6},{8,9},{9,8},{10,11... | collective-permute-start | bytes 3145736 | tf_op jit(solution)/shard_map/ppermute | solution.py:806
  89.3 16.2 %collective-permute-start.14 = (bf16[16,5,64,128]{3,2,1,0:T(8,128)(2,1)S(1)}, bf16[16,5,64,128]{3,2,1,0:T(8,128)(2,1)S(1)}, u32[]{:S(2)}, u32[]{:S(2)}) collective-permute-start(bf16[16,5,64,128]{3,2,1,0:T(8,128)(2,1)S(1)} %get-tuple-element.104), channel_id=1, source_target_pairs={{0,1},{1,0},{2,3},{3,2},{4,5},{5,4},{6,7},{7,6},{8,9},{9,8},{10,11... | collective-permute-start | bytes 3932168 | tf_op jit(solution)/shard_map/ppermute | solution.py:806
  89.9 15.6 %collective-permute-start.13 = (bf16[8,256,128]{2,1,0:T(8,128)(2,1)S(1)}, bf16[8,256,128]{2,1,0:T(8,128)(2,1)S(1)}, u32[]{:S(2)}, u32[]{:S(2)}) collective-permute-start(bf16[8,256,128]{2,1,0:T(8,128)(2,1)S(1)} %get-tuple-element.136), channel_id=1, source_target_pairs={{0,2},{1,5},{2,0},{3,7},{4,6},{5,1},{6,4},{7,3},{8,10},{9,13},{10,... | collective-permute-start | bytes 1572872 | tf_op jit(solution)/shard_map/ppermute | solution.py:806
  108.4 15.6 %collective-permute-start.16 = (bf16[8,272,128]{2,1,0:T(8,128)(2,1)S(1)}, bf16[8,272,128]{2,1,0:T(8,128)(2,1)S(1)}, u32[]{:S(2)}, u32[]{:S(2)}) collective-permute-start(bf16[8,272,128]{2,1,0:T(8,128)(2,1)S(1)} %get-tuple-element.134), channel_id=1, source_target_pairs={{0,8},{1,17},{2,10},{3,19},{4,12},{5,21},{6,14},{7,23},{8,0},{9,25... | collective-permute-start | bytes 1671176 | tf_op jit(solution)/shard_map/ppermute | solution.py:806
  108.6 8.1 %collective-permute-start.24 = (bf16[4,256,128]{2,1,0:T(8,128)(2,1)S(1)}, bf16[4,256,128]{2,1,0:T(8,128)(2,1)S(1)}, u32[]{:S(2)}, u32[]{:S(2)}) collective-permute-start(bf16[4,256,128]{2,1,0:T(8,128)(2,1)S(1)} %get-tuple-element.142), channel_id=1, source_target_pairs={{0,4},{1,3},{2,6},{3,1},{4,0},{5,7},{6,2},{7,5},{8,12},{9,11},{10,... | collective-permute-start | bytes 786440 | tf_op jit(solution)/shard_map/ppermute | solution.py:806
  109.9 15.4 %collective-permute-start.20 = (bf16[8,5,64,128]{3,2,1,0:T(8,128)(2,1)S(1)}, bf16[8,5,64,128]{3,2,1,0:T(8,128)(2,1)S(1)}, u32[]{:S(2)}, u32[]{:S(2)}) collective-permute-start(bf16[8,5,64,128]{3,2,1,0:T(8,128)(2,1)S(1)} %get-tuple-element.132), channel_id=1, source_target_pairs={{0,2},{1,5},{2,0},{3,7},{4,6},{5,1},{6,4},{7,3},{8,10},{9,13},{10,... | collective-permute-start | bytes 1966088 | tf_op jit(solution)/shard_map/ppermute | solution.py:806
  124.1 9.3 %collective-permute-start.17 = (bf16[4,272,128]{2,1,0:T(8,128)(2,1)S(1)}, bf16[4,272,128]{2,1,0:T(8,128)(2,1)S(1)}, u32[]{:S(2)}, u32[]{:S(2)}) collective-permute-start(bf16[4,272,128]{2,1,0:T(8,128)(2,1)S(1)} %get-tuple-element.140), channel_id=1, source_target_pairs={{0,2},{1,5},{2,0},{3,7},{4,6},{5,1},{6,4},{7,3},{8,10},{9,13},{10,... | collective-permute-start | bytes 835592 | tf_op jit(solution)/shard_map/ppermute | solution.py:806
  125.3 6.0 %collective-permute-start.25 = (bf16[2,256,128]{2,1,0:T(8,128)(2,1)S(1)}, bf16[2,256,128]{2,1,0:T(8,128)(2,1)S(1)}, u32[]{:S(2)}, u32[]{:S(2)}) collective-permute-start(bf16[2,256,128]{2,1,0:T(8,128)(2,1)S(1)} %get-tuple-element.148), channel_id=1, source_target_pairs={{0,8},{1,17},{2,10},{3,19},{4,12},{5,21},{6,14},{7,23},{8,0},{9,25... | collective-permute-start | bytes 393224 | tf_op jit(solution)/shard_map/ppermute | solution.py:806
  125.6 8.1 %collective-permute-start.21 = (bf16[4,5,64,128]{3,2,1,0:T(8,128)(2,1)S(1)}, bf16[4,5,64,128]{3,2,1,0:T(8,128)(2,1)S(1)}, u32[]{:S(2)}, u32[]{:S(2)}) collective-permute-start(bf16[4,5,64,128]{3,2,1,0:T(8,128)(2,1)S(1)} %get-tuple-element.138), channel_id=1, source_target_pairs={{0,4},{1,3},{2,6},{3,1},{4,0},{5,7},{6,2},{7,5},{8,12},{9,11},{10,... | collective-permute-start | bytes 983048 | tf_op jit(solution)/shard_map/ppermute | solution.py:806
  133.4 7.6 %collective-permute-start.26 = (bf16[1,256,128]{2,1,0:T(8,128)(2,1)S(1)}, bf16[1,256,128]{2,1,0:T(8,128)(2,1)S(1)}, u32[]{:S(2)}, u32[]{:S(2)}) collective-permute-start(bf16[1,256,128]{2,1,0:T(8,128)(2,1)S(1)} %fusion.9), channel_id=1, source_target_pairs={{0,16},{1,9},{2,18},{3,11},{4,20},{5,13},{6,22},{7,15},{8,24},{9,1... | collective-permute-start | bytes 196616 | tf_op jit(solution)/shard_map/ppermute | solution.py:806
  133.5 7.6 %collective-permute-start.18 = (bf16[2,272,128]{2,1,0:T(8,128)(2,1)S(1)}, bf16[2,272,128]{2,1,0:T(8,128)(2,1)S(1)}, u32[]{:S(2)}, u32[]{:S(2)}) collective-permute-start(bf16[2,272,128]{2,1,0:T(8,128)(2,1)S(1)} %get-tuple-element.146), channel_id=1, source_target_pairs={{0,4},{1,3},{2,6},{3,1},{4,0},{5,7},{6,2},{7,5},{8,12},{9,11},{10,... | collective-permute-start | bytes 417800 | tf_op jit(solution)/shard_map/ppermute | solution.py:806
  133.8 9.9 %collective-permute-start.22 = (bf16[2,5,64,128]{3,2,1,0:T(8,128)(2,1)S(1)}, bf16[2,5,64,128]{3,2,1,0:T(8,128)(2,1)S(1)}, u32[]{:S(2)}, u32[]{:S(2)}) collective-permute-start(bf16[2,5,64,128]{3,2,1,0:T(8,128)(2,1)S(1)} %get-tuple-element.144), channel_id=1, source_target_pairs={{0,8},{1,17},{2,10},{3,19},{4,12},{5,21},{6,14},{7,23},{8,0},{9,25... | collective-permute-start | bytes 491528 | tf_op jit(solution)/shard_map/ppermute | solution.py:806
  141.8 5.6 %collective-permute-start.19 = (bf16[1,272,128]{2,1,0:T(8,128)(2,1)S(1)}, bf16[1,272,128]{2,1,0:T(8,128)(2,1)S(1)}, u32[]{:S(2)}, u32[]{:S(2)}) collective-permute-start(bf16[1,272,128]{2,1,0:T(8,128)(2,1)S(1)} %get-tuple-element.150), channel_id=1, source_target_pairs={{0,16},{1,9},{2,18},{3,11},{4,20},{5,13},{6,22},{7,15},{8,24},{9,1... | collective-permute-start | bytes 208904 | tf_op jit(solution)/shard_map/ppermute | solution.py:806
  143.7 6.1 %collective-permute-start.23 = (bf16[1,5,64,128]{3,2,1,0:T(8,128)(2,1)S(1)}, bf16[1,5,64,128]{3,2,1,0:T(8,128)(2,1)S(1)}, u32[]{:S(2)}, u32[]{:S(2)}) collective-permute-start(bf16[1,5,64,128]{3,2,1,0:T(8,128)(2,1)S(1)} %fusion.6), channel_id=1, source_target_pairs={{0,16},{1,9},{2,18},{3,11},{4,20},{5,13},{6,22},{7,15},{8,24},{9,1... | collective-permute-start | bytes 245768 | tf_op jit(solution)/shard_map/ppermute | solution.py:806
  (15 other events, 133.9 us)

commit v3 on v2

--- a/solution.py
+++ b/solution.py
@@ -22,8 +22,11 @@
 HALF = PLACES // 2
 
 Z1, Z0, X, Y = 16, 8, 4, 2
-ORDER_FIRST = ((Z1, X, Y, Z0), (Z0, Y, X, Z1))
+ORDER_FIRST = ((X, Y, Z1, Z0), (X, Y, Z0, Z1))
 ORDER_SECOND = ((Z1, Z0, X, Y), (Z0, Z1, Y, X))
+ORDER_OUTER = ((Z1, Z0, X, Y), (Z0, Z1, Y, X))
+ORDER_INNER = ((X, Z1, Z0, Y), (Y, Z0, Z1, X))
+ORDER_BACK = ((Z1, Y, Z0, X), (Y, X, Z1, Z0))
 
 
 def nn(left, right):
@@ -144,6 +147,7 @@
     bin_ref,
     weights,
     bias,
+    qkv,
     table,
     small,
     sems,
@@ -200,22 +204,25 @@
             own = own.astype(BF16)
             if part == 0:
                 own = own * BF16(0.125)
-            qkv_ref[:, (chunk * 2 + side) * 128 : (chunk * 2 + side) * 128 + 128] = own
+            qkv[:, (chunk * 2 + side) * 128 : (chunk * 2 + side) * 128 + 128] = own
+
+    leave = pltpu.make_async_copy(qkv, qkv_ref, sems.at[3])
+    leave.start()
 
     def per_pair(pair, unused):
         spans = block_spans(windows, length)
         turned_values = [
             jnp.transpose(
-                qkv_ref[window * length : (window + 1) * length, part_lanes(pair, 2)]
+                qkv[window * length : (window + 1) * length, part_lanes(pair, 2)]
             )
             for window in range(windows)
         ]
         scores = []
         for window, block, here, there, span in spans:
-            query = stack_heads(qkv_ref[here, part_lanes(pair, 0)], low)
+            query = stack_heads(qkv[here, part_lanes(pair, 0)], low)
             mask = bias[window, block, 0:span, :]
             scores.append(
-                nt(qkv_ref[there, part_lanes(pair, 1)], query)
+                nt(qkv[there, part_lanes(pair, 1)], query)
                 + jnp.concatenate([mask, mask], axis=1)
             )
         shares = []
@@ -235,6 +242,7 @@
         return unused
 
     lax.fori_loop(0, NARROW, per_pair, 0)
+    leave.wait()
 
 
 def norm_parts(values):
@@ -379,7 +387,7 @@
         piece = nn(grads, active[:, columns])
         for narrow in range(NARROW):
             target = (keep_ref, send_ref)[narrow & 1]
-            block = block_at(ORDER_SECOND, me, wide * NARROW + narrow)
+            block = block_at(ORDER_BACK, me, wide * NARROW + narrow)
             own = piece[narrow * 128 : narrow * 128 + 128]
             target[block, 0:128, :] = own[:, 0:128].astype(target.dtype)
             target[block, 128:256, :] = own[:, 128:256].astype(target.dtype)
@@ -451,53 +459,33 @@
             columns = pl.ds(pl.multiple_of(at * 512 + part * 256, 256), 256)
             piece = nn(lows, grad_pre[:, columns])
             for wide in range(WIDE):
-                block = block_at(ORDER_SECOND, me, wide * NARROW + narrow)
+                block = block_at(ORDER_INNER, me, wide * NARROW + narrow)
                 own = piece[wide * 64 : wide * 64 + 64]
                 target[block, part * 2] = own[:, 0:128].astype(target.dtype)
                 target[block, part * 2 + 1] = own[:, 128:256].astype(target.dtype)
         piece = nn(joined, grad_branch[:, pl.ds(pl.multiple_of(at * 128, 128), 128)])
         for wide in range(WIDE):
-            block = block_at(ORDER_SECOND, me, wide * NARROW + narrow)
+            block = block_at(ORDER_INNER, me, wide * NARROW + narrow)
             target[block, 4] = piece[wide * 64 : wide * 64 + 64].astype(target.dtype)
 
 
 def attend_back_kernel(
     direct,
+    segments_ref,
     qkv_ref,
     grad_attended_ref,
     lse_ref,
-    mixed_ref,
-    grad_first_ref,
-    sums_a_ref,
-    sums_b_ref,
-    bin_sums_ref,
-    weights,
+    grads,
+    vec_sums,
     bias,
-    stream_ref,
-    keep_ref,
-    send_ref,
-    mixed_t,
-    grads,
-    stream,
-    vec_sums,
 ):
-    windows, blocks = lse_ref.shape[1:3]
-    length = blocks * 128
+    windows, length = segments_ref.shape
     me = my_place() if direct else jnp.int32(0)
-    turned_low = jnp.transpose(mixed_ref[...])
-    for wide in range(WIDE):
-        mixed_t[wide ^ (me >> 2), :, :] = turned_low[wide * 64 : wide * 64 + 64, :]
+    fill_bias(segments_ref, bias, windows)
     vec_sums[...] = jnp.zeros_like(vec_sums)
-    for tile in range(4):
-        lanes = slice(tile * 128, tile * 128 + 128)
-        vec_sums[tile, 2:3, :] = sums_b_ref[0:1, lanes]
-        vec_sums[tile, 3:4, :] = sums_a_ref[0:1, lanes]
-        vec_sums[tile, 4:6, :] = sums_b_ref[1:3, lanes]
-        vec_sums[tile, 6:8, :] = sums_a_ref[1:3, lanes]
     low = head_masks(128)
 
-    def per_pair(core, upper, unused):
-        apart = 2 * upper + core
+    def per_pair(apart, unused):
         pair = (me & 3) ^ apart
         spans = block_spans(windows, length)
         lanes = pl.ds(pl.multiple_of(pair * 128, 128), 128)
@@ -548,8 +536,39 @@
             vec_sums[pair, 1:2, :] += column_sum(grad.astype(F32))
         return unused
 
-    lax.fori_loop(0, 2, partial(per_pair, 0), 0)
-    lax.fori_loop(0, 2, partial(per_pair, 1), 0)
+    lax.fori_loop(0, NARROW, per_pair, 0)
+
+
+def project_back_kernel(
+    direct,
+    windows,
+    grads,
+    mixed_ref,
+    grad_first_ref,
+    pair_sums_ref,
+    sums_a_ref,
+    sums_b_ref,
+    bin_sums_ref,
+    weights,
+    stream_ref,
+    keep_ref,
+    send_ref,
+    mixed_t,
+    stream,
+    vec_sums,
+):
+    length = mixed_ref.shape[0] // windows
+    me = my_place() if direct else jnp.int32(0)
+    turned_low = jnp.transpose(mixed_ref[...])
+    for wide in range(WIDE):
+        mixed_t[wide ^ (me >> 2), :, :] = turned_low[wide * 64 : wide * 64 + 64, :]
+    for tile in range(4):
+        lanes = slice(tile * 128, tile * 128 + 128)
+        vec_sums[tile, 0:2, :] = pair_sums_ref[tile, 0:2, :]
+        vec_sums[tile, 2:3, :] = sums_b_ref[0:1, lanes]
+        vec_sums[tile, 3:4, :] = sums_a_ref[0:1, lanes]
+        vec_sums[tile, 4:6, :] = sums_b_ref[1:3, lanes]
+        vec_sums[tile, 6:8, :] = sums_a_ref[1:3, lanes]
     turned_mixed = mixed_t[...].reshape(512, windows * length)
     for chunk in range(6):
         weight_grads = nn(turned_mixed, grads[:, chunk * 256 : chunk * 256 + 256])
@@ -557,7 +576,7 @@
             apart, part = divmod(chunk * 2 + side, 3)
             target = (keep_ref, send_ref)[apart & 1]
             for wide in range(WIDE):
-                block = block_at(ORDER_FIRST, me, wide * NARROW + apart)
+                block = block_at(ORDER_OUTER, me, wide * NARROW + apart)
                 target[block, part * 64 : part * 64 + 64, :] = weight_grads[
                     wide * 64 : wide * 64 + 64, side * 128 : side * 128 + 128
                 ].astype(target.dtype)
@@ -574,7 +593,7 @@
         stream[row : row + 256, :] = total
     for half, target in ((0, keep_ref), (1, send_ref)):
         for block in range(HALF):
-            wide, narrow = place_of(ORDER_FIRST, me, half, block)
+            wide, narrow = place_of(ORDER_OUTER, me, half, block)
             target[block, 192:256, :] = stream[
                 pl.ds(pl.multiple_of(wide * 64, 64), 64),
                 pl.ds(pl.multiple_of(narrow * 128, 128), 128),
@@ -622,10 +641,32 @@
 
 
 def finish_kernel(
-    held_ref, came_ref, query_ref, key_ref, value_ref, table_ref, vectors_ref, in_bias_ref
+    outer_ref,
+    outer_came_ref,
+    inner_ref,
+    inner_came_ref,
+    back_ref,
+    back_came_ref,
+    query_ref,
+    key_ref,
+    value_ref,
+    out_ref,
+    in_ref,
+    w_back_ref,
+    table_ref,
+    vectors_ref,
+    in_bias_ref,
 ):
     wide, narrow = lax.axis_index("wide"), lax.axis_index("narrow")
-    total = held_ref[0] + came_ref[0].astype(F32)
+    total = back_ref[0] + back_came_ref[0].astype(F32)
+    w_back_ref[0:128, :] = jnp.transpose(total[0:128])
+    w_back_ref[128:256, :] = jnp.transpose(total[128:256])
+    for part in range(4):
+        in_ref[:, part * 128 : part * 128 + 128] = inner_ref[0, part] + inner_came_ref[
+            0, part
+        ].astype(F32)
+    out_ref[...] = inner_ref[0, 4] + inner_came_ref[0, 4].astype(F32)
+    total = outer_ref[0] + outer_came_ref[0].astype(F32)
     query_ref[...] = total[0:64]
     key_ref[...] = total[64:128]
     value_ref[...] = total[128:192]
@@ -664,6 +705,14 @@
 
 def shape(dims, dtype):
     return jax.ShapeDtypeStruct(dims, dtype)
+
+
+def near(dims, dtype):
+    return pltpu.VMEM(dims, dtype)
+
+
+def kept(array):
+    return pltpu.with_memory_space_constraint(array, pltpu.VMEM)
 
 
 def attend_call(direct, segments, x, blocks):
@@ -672,22 +721,23 @@
     return pl.pallas_call(
         partial(attend_kernel, direct),
         out_shape=(
-            shape((total, 1536), BF16),
+            pltpu.HBM((total, 1536), BF16),
             shape((total, 512), BF16),
             shape((NARROW, windows, length // 128, 256), F32),
-            shape((total, 512), F32),
+            near((total, 512), F32),
             shape((total, 512), BF16),
             shape((4, 8, 128), F32),
             shape((2, 8, 128), F32),
             shape((512, 1536), BF16),
-            shape((windows, length // 128, 384, 128), F32),
         ),
         in_specs=[vmem(), vmem()] + [hbm()] * 4,
-        out_specs=tuple([vmem()] * 9),
+        out_specs=(pl.BlockSpec(memory_space=pltpu.HBM),) + tuple([vmem()] * 7),
         scratch_shapes=[
+            pltpu.VMEM((windows, length // 128, 384, 128), F32),
+            pltpu.VMEM((total, 1536), BF16),
             pltpu.VMEM((512, 512), BF16),
             pltpu.VMEM((PLACES, 16, 128), BF16),
-            pltpu.SemaphoreType.DMA((3,)),
+            pltpu.SemaphoreType.DMA((4,)),
         ],
         compiler_params=params(ATTEND_MIB),
         cost_estimate=cost(6000 << 20, 12 << 20),
@@ -697,9 +747,10 @@
 
 ROWS = 512
 ATTEND_MIB = 24
-FORWARD_MIB = 20
-BACKWARD_MIB = 16
-ATTEND_BACK_MIB = 32
+FORWARD_MIB = 14
+BACKWARD_MIB = 14
+ATTEND_BACK_MIB = 20
+PROJECT_BACK_MIB = 16
 
 
 def forward_call(direct, attended, passed, cotangent, vec, bins, blocks):
@@ -708,16 +759,16 @@
         partial(forward_kernel, direct),
         out_shape=(
             shape((total, 512), BF16),
-            shape((total, 2048), F32),
-            shape((total, 512), F32),
-            shape((total, 512), F32),
-            shape((WIDE, 64, total), BF16),
-            shape((HALF, 256, 128), F32),
-            shape((HALF, 256, 128), BF16),
+            near((total, 2048), F32),
+            near((total, 512), F32),
+            near((total, 512), F32),
+            near((WIDE, 64, total), BF16),
+            near((HALF, 256, 128), F32),
+            near((HALF, 256, 128), BF16),
             shape((8, 512), F32),
-            shape((512, 512), BF16),
-            shape((16, 512, 128), BF16),
-            shape((32, 64, 512), BF16),
+            near((512, 512), BF16),
+            near((16, 512, 128), BF16),
+            near((32, 64, 512), BF16),
         ),
         in_specs=[vmem()] * 5 + [hbm()] * 4,
         out_specs=tuple([vmem()] * 11),
@@ -728,8 +779,9 @@
         ],
         compiler_params=params(FORWARD_MIB),
         cost_estimate=cost(6000 << 20, 24 << 20),
+        input_output_aliases={1: 3},
         name="forward",
-    )(attended, passed, cotangent, vec, bins, *blocks)
+    )(attended, kept(passed), cotangent, vec, bins, *blocks)
 
 
 def backward_call(direct, slope, grad_second, first_sum, low_t, attended, vec, weights):
@@ -754,52 +806,102 @@
         compiler_params=params(BACKWARD_MIB),
         cost_estimate=cost(7000 << 20, 24 << 20),
         name="backward",
-    )(slope, grad_second, first_sum, low_t, attended, vec, *weights)
-
-
-def attend_back_call(direct, qkv, grad_attended, lse, mixed, grad_first, sums, weights, bias):
-    windows, blocks = lse.shape[1:3]
-    length = blocks * 128
+    )(
+        kept(slope),
+        kept(grad_second),
+        kept(first_sum),
+        kept(low_t),
+        attended,
+        vec,
+        *(kept(weight) for weight in weights),
+    )
+
+
+def attend_back_call(direct, segments, qkv, grad_attended, lse):
+    windows, length = segments.shape
     total = windows * length
     return pl.pallas_call(
         partial(attend_back_kernel, direct),
+        out_shape=(shape((total, 1536), BF16), shape((4, 8, 128), F32)),
+        in_specs=[vmem()] * 4,
+        out_specs=(vmem(), vmem()),
+        scratch_shapes=[pltpu.VMEM((windows, length // 128, 384, 128), F32)],
+        compiler_params=params(ATTEND_BACK_MIB),
+        cost_estimate=cost(4000 << 20, 8 << 20),
+        name="attend_back",
+    )(segments, qkv, grad_attended, lse)
+
+
+def project_back_call(direct, windows, grads, mixed, grad_first, sums, weights):
+    total = mixed.shape[0]
+    return pl.pallas_call(
+        partial(project_back_kernel, direct, windows),
         out_shape=(
             shape((total, 512), BF16),
             shape((HALF, 272, 128), F32),
             shape((HALF, 272, 128), BF16),
         ),
-        in_specs=[vmem()] * 10,
+        in_specs=[vmem()] * 8,
         out_specs=(vmem(), vmem(), vmem()),
         scratch_shapes=[
             pltpu.VMEM((WIDE, 64, total), BF16),
-            pltpu.VMEM((total, 1536), BF16),
-            pltpu.VMEM((length, 512), F32),
+            pltpu.VMEM((total // windows, 512), F32),
             pltpu.VMEM((4, 8, 128), F32),
         ],
-        compiler_params=params(ATTEND_BACK_MIB),
-        cost_estimate=cost(7000 << 20, 16 << 20),
-        name="attend_back",
-    )(qkv, grad_attended, lse, mixed, grad_first, *sums, weights, bias)
+        compiler_params=params(PROJECT_BACK_MIB),
+        cost_estimate=cost(3000 << 20, 8 << 20),
+        name="project_back",
+    )(grads, mixed, grad_first, *sums, weights)
 
 
 def pack_call(*shards):
     return pl.pallas_call(
         pack_kernel,
-        out_shape=(shape((272, 128), BF16), shape((9, 64, 128), BF16)),
+        out_shape=(near((272, 128), BF16), near((9, 64, 128), BF16)),
         in_specs=[vmem()] * 9,
         out_specs=(vmem(), vmem()),
         name="pack",
     )(*shards)
 
 
-def finish_call(held, came):
+def join_kernel(first_ref, second_ref, joined_ref):
+    half = first_ref.shape[0]
+    joined_ref[0:half] = first_ref[...]
+    joined_ref[half:] = second_ref[...]
+
+
+def joined_blocks(first, second):
+    count = 2 * first.shape[0]
+    return pl.pallas_call(
+        join_kernel,
+        out_shape=near((count,) + first.shape[1:], first.dtype),
+        in_specs=[vmem()] * 2,
+        out_specs=vmem(),
+        compiler_params=params(2),
+        name="join",
+    )(kept(first), kept(second))
+
+
+def finish_call(outer, inner, back):
+    block = shape((64, 128), F32)
     return pl.pallas_call(
         finish_kernel,
-        out_shape=tuple([shape((64, 128), F32)] * 4 + [shape((2, 64), F32), shape((1, 64), F32)]),
-        in_specs=[vmem()] * 2,
-        out_specs=tuple([vmem()] * 6),
+        out_shape=(
+            block,
+            block,
+            block,
+            block,
+            shape((64, 512), F32),
+            shape((256, 128), F32),
+            block,
+            shape((2, 64), F32),
+            shape((1, 64), F32),
+        ),
+        in_specs=[vmem()] * 6,
+        out_specs=tuple([vmem()] * 9),
+        compiler_params=params(6),
         name="finish",
-    )(held, came)
+    )(*outer, *inner, *back)
 
 
 def swap(array, order, step):
@@ -873,68 +975,61 @@
         w_query, w_key, w_value, w_out, w_in, w_back, position_table, vectors, in_bias[None]
     )
     early, late = early[None], late[None]
-    early = grow(early, ORDER_FIRST, 0)
-    for step in range(3):
-        early_came = swap(early, ORDER_FIRST, step + 1)
+    for step in range(4):
+        early_came = swap(early, ORDER_FIRST, step)
         late_came = swap(late, ORDER_SECOND, step)
         early_came, late_came = lax.optimization_barrier((early_came, late_came))
-        if step < 2:
-            early = jnp.concatenate([early, early_came], axis=0)
+        if step < 3:
+            early = joined_blocks(early, early_came)
+            late = joined_blocks(late, late_came)
         else:
-            early_far = early_came
-        late = jnp.concatenate([late, late_came], axis=0)
+            early_far, late_far = early_came, late_came
     first = (early, early_far, swap(early, ORDER_FIRST, 4), swap(early_far, ORDER_FIRST, 4))
-    late_far = swap(late, ORDER_SECOND, 3)
-    qkv, attended, lse, passed, mixed, vec, bins, w_qkv, bias = attend_call(
+    second = (late, late_far, swap(late, ORDER_SECOND, 4), swap(late_far, ORDER_SECOND, 4))
+    qkv, attended, lse, passed, mixed, vec, bins, w_qkv = attend_call(
         True, segment_ids, after(x, late), first
     )
-    late_far = after(late_far, attended)
-    second = (late, late_far, swap(late, ORDER_SECOND, 4), swap(late_far, ORDER_SECOND, 4))
-    output, slope, grad_second, first_sum, low_t, keep_back, send_back, sums_a, *whole = forward_call(
+    *second, attended = lax.optimization_barrier((*second, attended))
+    output, slope, grad_second, first_sum, low_t, keep, send, sums_a, *whole = forward_call(
         True, attended, passed, cotangent.reshape(rows, features), vec, bins, second
     )
-    back = start_halving(keep_back, send_back, ORDER_SECOND)
-    grad_first, grad_attended, keep_in, send_in, sums_b, bin_sums = backward_call(
+    back = start_halving(keep, send, ORDER_BACK)
+    grad_first, grad_attended, keep, send, sums_b, bin_sums = backward_call(
         True, slope, grad_second, first_sum, low_t, attended, vec, whole
     )
-    back = halve(*back, ORDER_SECOND, 3)
-    inner = start_halving(keep_in, send_in, ORDER_SECOND)
-    stream, keep_first, send_first = attend_back_call(
+    back = halve(*back, ORDER_BACK, 3)
+    inner = start_halving(keep, send, ORDER_INNER)
+    grads, pair_sums = attend_back_call(
+        True, segment_ids, qkv, after(grad_attended, back[0]), lse
+    )
+    grads, back_came, inner_came = lax.optimization_barrier((grads, back[1], inner[1]))
+    back = halve(back[0], back_came, ORDER_BACK, 2)
+    inner = halve(inner[0], inner_came, ORDER_INNER, 3)
+    stream, keep, send = project_back_call(
         True,
-        qkv,
-        after(grad_attended, back[0]),
-        lse,
+        windows,
+        after(grads, back[0], inner[0]),
         mixed,
         grad_first,
-        (sums_a, sums_b, bin_sums),
+        (pair_sums, sums_a, sums_b, bin_sums),
         w_qkv,
-        bias,
-    )
-    keep_first, send_first, back_came, inner_came = lax.optimization_barrier(
-        (keep_first, send_first, back[1], inner[1])
-    )
-    outer = start_halving(keep_first, send_first, ORDER_FIRST)
-    back = halve(back[0], back_came, ORDER_SECOND, 2)
-    inner = halve(inner[0], inner_came, ORDER_SECOND, 3)
-    for step in (2, 1, 0):
-        outer = halve(*outer, ORDER_FIRST, step + 1)
-        if step > 0:
-            back = halve(back[0], after(back[1], outer[1]), ORDER_SECOND, step - 1)
-        inner = halve(inner[0], after(inner[1], outer[1]), ORDER_SECOND, step)
-    outer = halve(*outer, ORDER_FIRST, 0)
-    back = back[0][0] + back[1][0].astype(F32)
-    inner = inner[0][0] + inner[1][0].astype(F32)
-    grad_query, grad_key, grad_value, grad_table, vec, bins = finish_call(*outer)
+    )
+    keep, send, back_came, inner_came = lax.optimization_barrier((keep, send, back[1], inner[1]))
+    outer = start_halving(keep, send, ORDER_OUTER)
+    back = halve(back[0], back_came, ORDER_BACK, 1)
+    inner = halve(inner[0], inner_came, ORDER_INNER, 2)
+    for step in (3, 2, 1):
+        outer = halve(*outer, ORDER_OUTER, step)
+        if step == 3:
+            back = halve(back[0], after(back[1], outer[1]), ORDER_BACK, 0)
+        if step > 1:
+            inner = halve(inner[0], after(inner[1], outer[1]), ORDER_INNER, step - 2)
+    outer = halve(*outer, ORDER_OUTER, 0)
+    *matrices, vec, bins = finish_call(outer, inner, back)
     return (
         output.reshape(inputs.shape),
         stream.reshape(inputs.shape),
-        grad_query,
-        grad_key,
-        grad_value,
-        inner[4],
-        jnp.concatenate([inner[part] for part in range(4)], axis=1),
-        turned(back),
-        grad_table,
+        *matrices,
         vec,
         bins[0],
     )
@@ -1008,7 +1103,7 @@
     windows, length, features = inputs.shape
     rows = windows * length
     first, second = fours(first, ORDER_FIRST), fours(second, ORDER_SECOND)
-    qkv, attended, lse, passed, mixed, vec, bins, w_qkv, bias = attend_call(
+    qkv, attended, lse, passed, mixed, vec, bins, w_qkv = attend_call(
         False, segment_ids, inputs.reshape(rows, features), first
     )
     output, slope, grad_second, first_sum, low_t, keep_back, send_back, sums_a, *whole_w = forward_call(
@@ -1017,16 +1112,15 @@
     grad_first, grad_attended, keep_in, send_in, sums_b, bin_sums = backward_call(
         False, slope, grad_second, first_sum, low_t, attended, vec, whole_w
     )
-    stream, keep_first, send_first = attend_back_call(
+    grads, pair_sums = attend_back_call(False, segment_ids, qkv, grad_attended, lse)
+    stream, keep_first, send_first = project_back_call(
         False,
-        qkv,
-        grad_attended,
-        lse,
+        windows,
+        grads,
         mixed,
         grad_first,
-        (sums_a, sums_b, bin_sums),
+        (pair_sums, sums_a, sums_b, bin_sums),
         w_qkv,
-        bias,
     )
 
     def joined(pair, order):
@@ -1037,9 +1131,9 @@
         array = lax.psum_scatter(array, "wide", scatter_dimension=0, tiled=True)
         return lax.psum_scatter(array, "narrow", scatter_dimension=1, tiled=True)
 
-    back = joined((keep_back, send_back), ORDER_SECOND)
-    inner = joined((keep_in, send_in), ORDER_SECOND)
-    outer = joined((keep_first, send_first), ORDER_FIRST)
+    back = joined((keep_back, send_back), ORDER_BACK)
+    inner = joined((keep_in, send_in), ORDER_INNER)
+    outer = joined((keep_first, send_first), ORDER_OUTER)
     back = jax.vmap(turned)(back)
     grad_in = inner[:, 0:4].transpose(0, 2, 1, 3).reshape(PLACES, 64, 512)
     vec = outer.reshape(WIDE, NARROW, 272, 128)[::2, 0, 256:264]

time: 151 us -> 142 us (0.940)
  local copies, waits for them, and re-layouts: 6.8 us -> 1.06 us
  other arithmetic: 5.91 us -> 1.71 us
  waiting for transfers between devices: 61.6 us -> 65.4 us
  Pallas kernels: 49.6 us -> 47.9 us
  starting transfers between devices: 26.4 us -> 24.7 us
    pallas_call x1, Pallas kernels: 13.5 us -> 8.06 us  [attend_back_call(): pl.pallas_call(partial(attend_back_kernel, direct), out_shape=(shape((tot...]
    unnamed x25 -> x8, local copies, waits for them, and re-layouts: 6.16 us -> 1.06 us
    pallas_call x3 -> x10, Pallas kernels: 11.8 us -> 15.7 us  [the longest x1 8.34 us: attend_call(): pl.pallas_call(partial(attend_kernel, direct), out_shape=(pltpu.HBM((tota...]
    ppermute x27, waiting for transfers between devices: 61.6 us -> 65.4 us  [swap(): return lax.ppermute(array, AXES, pairs(order, step))]
    concatenate x8 -> x0, other arithmetic: 3.65 us -> none  [the longest x3 1.12 us: per_device(): late = jnp.concatenate([late, late_came], axis=0)]
    ppermute x27, starting transfers between devices: 26.4 us -> 24.7 us  [swap(): return lax.ppermute(array, AXES, pairs(order, step))]
  transfers between devices with their start and end apart: 27 -> 27, of which waited for: 17 -> 14; matrix products, arithmetic and copies ran while one was open for 3% -> 1% of each run, Pallas kernels for 22% -> 23%
where the time goes in v3:
time: 142 us
  waiting for transfers between devices  65.4 us (46%)
  Pallas kernels  47.9 us (34%)
  starting transfers between devices  24.7 us (17%)
  other arithmetic  1.71 us (1%)
    ppermute x27, waiting for transfers between devices, swap(): return lax.ppermute(array, AXES, pairs(order, step))  65.4 us
    ppermute x27, starting transfers between devices, swap(): return lax.ppermute(array, AXES, pairs(order, step))  24.7 us
    pallas_call x1, Pallas kernels, forward_call(): pl.pallas_call(partial(forward_kernel, direct), out_shape=(shape((total,...  13.9 us
    pallas_call x1, Pallas kernels, backward_call(): pl.pallas_call(partial(backward_kernel, direct), out_shape=(shape((total,...  10.3 us
    pallas_call x1, Pallas kernels, attend_call(): pl.pallas_call(partial(attend_kernel, direct), out_shape=(pltpu.HBM((tota...  8.34 us
    pallas_call x1, Pallas kernels, attend_back_call(): pl.pallas_call(partial(attend_back_kernel, direct), out_shape=(shape((tot...  8.06 us
    pallas_call x1, Pallas kernels, project_back_call(): pl.pallas_call(partial(project_back_kernel, direct, windows), out_shape=(...  5.28 us
  transfers between devices with their start and end apart: 27, of which 14 were waited for; matrix products, arithmetic and copies ran while one was open for 1% of the time, Pallas kernels for 23%

profile of v3, /device:TPU:0, one launch (start us, length us, event | category | flops | bytes accessed | tf_op | source)
XLA Modules:
  0.0 141.7 jit_solution(4617704343821802390)
XLA Ops:
  1.7 4.1 %collective-permute-start.1 = (bf16[1,9,64,128]{3,2,1,0:T(8,128)(2,1)S(1)}, bf16[1,9,64,128]{3,2,1,0:T(8,128)(2,1)S(1)}, u32[]{:S(2)}, u32[]{:S(2)}) collective-permute-start(bf16[1,9,64,128]{3,2,1,0:T(8,128)(2,1)S(1)} %bitcast.8), channel_id=1, source_target_pairs={{0,16},{1,9},{2,18},{3,11},{4,20},{5,13},{6,22},{7,15},{8,24},{9,1... | collective-permute-start | bytes 442376 | tf_op jit(solution)/shard_map/ppermute | solution.py:908
  5.8 1.5 %collective-permute-start = (bf16[1,272,128]{2,1,0:T(8,128)(2,1)S(1)}, bf16[1,272,128]{2,1,0:T(8,128)(2,1)S(1)}, u32[]{:S(2)}, u32[]{:S(2)}) collective-permute-start(bf16[1,272,128]{2,1,0:T(8,128)(2,1)S(1)} %bitcast.10), channel_id=1, source_target_pairs={{0,4},{1,5},{2,6},{3,7},{4,0},{5,1},{6,2},{7,3},{8,12},{9,13},{10,... | collective-permute-start | bytes 208904 | tf_op jit(solution)/shard_map/ppermute | solution.py:908
  7.3 2.8 %collective-permute-done.second_ref = bf16[1,272,128]{2,1,0:T(8,128)(2,1)S(1)} collective-permute-done((bf16[1,272,128]{2,1,0:T(8,128)(2,1)S(1)}, bf16[1,272,128]{2,1,0:T(8,128)(2,1)S(1)}, u32[]{:S(2)}, u32[]{:S(2)}) %collective-permute-start) | collective-permute-done | bytes 69664 | tf_op jit(solution)/shard_map/ppermute | solution.py:908
  10.1 1.6 %collective-permute-start.3 = (bf16[2,9,64,128]{3,2,1,0:T(8,128)(2,1)S(1)}, bf16[2,9,64,128]{3,2,1,0:T(8,128)(2,1)S(1)}, u32[]{:S(2)}, u32[]{:S(2)}) collective-permute-start(bf16[2,9,64,128]{3,2,1,0:T(8,128)(2,1)S(1)} %join.6.first_ref), channel_id=1, source_target_pairs={{0,8},{1,17},{2,10},{3,19},{4,12},{5,21},{6,14},{7,23},{8,0},{9,25... | collective-permute-start | bytes 884744 | tf_op jit(solution)/shard_map/ppermute | solution.py:908
  11.8 1.6 %collective-permute-start.2 = (bf16[2,272,128]{2,1,0:T(8,128)(2,1)S(1)}, bf16[2,272,128]{2,1,0:T(8,128)(2,1)S(1)}, u32[]{:S(2)}, u32[]{:S(2)}) collective-permute-start(bf16[2,272,128]{2,1,0:T(8,128)(2,1)S(1)} %join.7.first_ref), channel_id=1, source_target_pairs={{0,2},{1,3},{2,0},{3,1},{4,6},{5,7},{6,4},{7,5},{8,10},{9,11},{10,... | collective-permute-start | bytes 417800 | tf_op jit(solution)/shard_map/ppermute | solution.py:908
  13.3 3.5 %collective-permute-done.2.second_ref = bf16[2,272,128]{2,1,0:T(8,128)(2,1)S(1)} collective-permute-done((bf16[2,272,128]{2,1,0:T(8,128)(2,1)S(1)}, bf16[2,272,128]{2,1,0:T(8,128)(2,1)S(1)}, u32[]{:S(2)}, u32[]{:S(2)}) %collective-permute-start.2) | collective-permute-done | bytes 139296 | tf_op jit(solution)/shard_map/ppermute | solution.py:908
  16.9 3.1 %collective-permute-done.3.second_ref = bf16[2,9,64,128]{3,2,1,0:T(8,128)(2,1)S(1)} collective-permute-done((bf16[2,9,64,128]{3,2,1,0:T(8,128)(2,1)S(1)}, bf16[2,9,64,128]{3,2,1,0:T(8,128)(2,1)S(1)}, u32[]{:S(2)}, u32[]{:S(2)}) %collective-permute-start.3) | collective-permute-done | bytes 294944 | tf_op jit(solution)/shard_map/ppermute | solution.py:908
  20.0 1.6 %collective-permute-start.5 = (bf16[4,9,64,128]{3,2,1,0:T(8,128)(2,1)S(1)}, bf16[4,9,64,128]{3,2,1,0:T(8,128)(2,1)S(1)}, u32[]{:S(2)}, u32[]{:S(2)}) collective-permute-start(bf16[4,9,64,128]{3,2,1,0:T(8,128)(2,1)S(1)} %join.8.first_ref), channel_id=1, source_target_pairs={{0,4},{1,3},{2,6},{3,1},{4,0},{5,7},{6,2},{7,5},{8,12},{9,11},{10,... | collective-permute-start | bytes 1769480 | tf_op jit(solution)/shard_map/ppermute | solution.py:908
  22.7 9.4 %collective-permute-done.4.second_ref = bf16[4,272,128]{2,1,0:T(8,128)(2,1)S(1)} collective-permute-done((bf16[4,272,128]{2,1,0:T(8,128)(2,1)S(1)}, bf16[4,272,128]{2,1,0:T(8,128)(2,1)S(1)}, u32[]{:S(2)}, u32[]{:S(2)}) %collective-permute-start.4) | collective-permute-done | bytes 278560 | tf_op jit(solution)/shard_map/ppermute | solution.py:908
  32.2 1.6 %collective-permute-start.7 = (bf16[8,9,64,128]{3,2,1,0:T(8,128)(2,1)S(1)}, bf16[8,9,64,128]{3,2,1,0:T(8,128)(2,1)S(1)}, u32[]{:S(2)}, u32[]{:S(2)}) collective-permute-start(bf16[8,9,64,128]{3,2,1,0:T(8,128)(2,1)S(1)} %join.10.p0_ref), channel_id=1, source_target_pairs={{0,2},{1,5},{2,0},{3,7},{4,6},{5,1},{6,4},{7,3},{8,10},{9,13},{10,... | collective-permute-start | bytes 3538952 | tf_op jit(solution)/shard_map/ppermute | solution.py:908
  34.0 15.3 %collective-permute-done.6.p1_ref = bf16[8,272,128]{2,1,0:T(8,128)(2,1)S(1)} collective-permute-done((bf16[8,272,128]{2,1,0:T(8,128)(2,1)S(1)}, bf16[8,272,128]{2,1,0:T(8,128)(2,1)S(1)}, u32[]{:S(2)}, u32[]{:S(2)}) %collective-permute-start.6) | collective-permute-done | bytes 557088 | tf_op jit(solution)/shard_map/ppermute | solution.py:908
  51.2 8.3 %attend.1 = (bf16[1024,1536]{1,0:T(8,128)(2,1)}, bf16[1024,512]{1,0:T(8,128)(2,1)S(1)}, f32[4,2,4,256]{3,2,1,0:T(4,128)S(1)}, f32[1024,512]{1,0:T(8,128)S(1)}, b...) custom-call(s32[2,512]{1,0:T(2,128)S(1)} %copy-done.2, ...), custom_call_target="tpu_custom_call" | custom-call | flops 12582912000 | bytes 12582912 | tf_op jit(solution)/shard_map/attend/pallas_call | solution.py:721
  59.6 13.9 %forward.1 = (bf16[1024,512]{1,0:T(8,128)(2,1)}, f32[1024,2048]{1,0:T(8,128)S(1)}, f32[1024,512]{1,0:T(8,128)S(1)}, f32[1024,512]{1,0:T(8,128)S(1)}, bf16[8,64,1...) custom-call(bf16[1024,512]{1,0:T(8,128)(2,1)S(1)} %get-tuple-element, ...), custom_call_target="tpu_custom_call", output_to_operand_aliasing={{3}: (1, {})} | custom-call | flops 12582912000 | bytes 25165824 | tf_op jit(solution)/shard_map/forward/pallas_call | solution.py:758
  73.7 10.3 %backward.1 = (f32[1024,512]{1,0:T(8,128)S(1)}, bf16[1024,512]{1,0:T(8,128)(2,1)S(1)}, f32[16,5,64,128]{3,2,1,0:T(8,128)S(1)}, bf16[16,5,64,128]{3,2,1,0:T(8,128...) custom-call(f32[1024,2048]{1,0:T(8,128)S(1)} %get-tuple-element.100.slope_ref, ...), custom_call_target="tpu_custom_call" | custom-call | flops 14680064000 | bytes 25165824 | tf_op jit(solution)/shard_map/backward/pallas_call | solution.py:789
  86.2 8.1 %attend_back.1 = (bf16[1024,1536]{1,0:T(8,128)(2,1)S(1)}, f32[4,8,128]{2,1,0:T(8,128)S(1)}) custom-call(s32[2,512]{1,0:T(2,128)S(1)} %copy-done.2, bf16[1024,1536]{1,0:T(8,128)(2,1)S(1)} %copy-done.3, bf16[1024,512]{1,0:T(8,128)(2,1)S(1)} %get-tuple-element.110.grad_attended_ref, f32[4,2,4,256]{3,2,1,0:T(4,128)S(1)} %get-tuple-element.111.lse_ref), custom_call_target="tpu_custom_call" | custom-call | flops 8388608000 | bytes 8388608 | tf_op jit(solution)/shard_map/attend_back/pallas_call | solution.py:823
  95.8 5.3 %project_back.1 = (bf16[1024,512]{1,0:T(8,128)(2,1)}, f32[16,272,128]{2,1,0:T(8,128)S(1)}, bf16[16,272,128]{2,1,0:T(8,128)(2,1)S(1)}) custom-call(bf16[1024,1536]{1,0:T(8,128)(2,1)S(1)} %get-tuple-element.118.grads, bf16[1024,512]{1,0:T(8,128)(2,1)S(1)} %get-tuple-element.119.mixed_ref, f32[1024,512]{1,0:T(8,128)S(1)} %get-tuple-element.120.grad_first_ref, ...), custom_call_target="tpu_custom_call" | custom-call | flops 6291456000 | bytes 8388608 | tf_op jit(solution)/shard_map/project_back/pallas_call | solution.py:837
  101.1 3.8 %collective-permute-done.15 = bf16[4,256,128]{2,1,0:T(8,128)(2,1)S(1)} collective-permute-done((bf16[4,256,128]{2,1,0:T(8,128)(2,1)S(1)}, bf16[4,256,128]{2,1,0:T(8,128)(2,1)S(1)}, u32[]{:S(2)}, u32[]{:S(2)}) %collective-permute-start.15) | collective-permute-done | bytes 262176 | tf_op jit(solution)/shard_map/ppermute | solution.py:908
  105.5 2.8 %collective-permute-done.17 = bf16[16,272,128]{2,1,0:T(8,128)(2,1)S(1)} collective-permute-done((bf16[16,272,128]{2,1,0:T(8,128)(2,1)S(1)}, bf16[16,272,128]{2,1,0:T(8,128)(2,1)S(1)}, u32[]{:S(2)}, u32[]{:S(2)}) %collective-permute-start.17) | collective-permute-done | bytes 1114144 | tf_op jit(solution)/shard_map/ppermute | solution.py:908
  109.5 10.5 %collective-permute-done.22 = bf16[4,5,64,128]{3,2,1,0:T(8,128)(2,1)S(1)} collective-permute-done((bf16[4,5,64,128]{3,2,1,0:T(8,128)(2,1)S(1)}, bf16[4,5,64,128]{3,2,1,0:T(8,128)(2,1)S(1)}, u32[]{:S(2)}, u32[]{:S(2)}) %collective-permute-start.22) | collective-permute-done | bytes 327712 | tf_op jit(solution)/shard_map/ppermute | solution.py:908
  122.5 4.1 %collective-permute-done.25 = bf16[2,256,128]{2,1,0:T(8,128)(2,1)S(1)} collective-permute-done((bf16[2,256,128]{2,1,0:T(8,128)(2,1)S(1)}, bf16[2,256,128]{2,1,0:T(8,128)(2,1)S(1)}, u32[]{:S(2)}, u32[]{:S(2)}) %collective-permute-start.25) | collective-permute-done | bytes 131104 | tf_op jit(solution)/shard_map/ppermute | solution.py:908
  127.3 2.3 %collective-permute-start.20 = (bf16[2,272,128]{2,1,0:T(8,128)(2,1)S(1)}, bf16[2,272,128]{2,1,0:T(8,128)(2,1)S(1)}, u32[]{:S(2)}, u32[]{:S(2)}) collective-permute-start(bf16[2,272,128]{2,1,0:T(8,128)(2,1)S(1)} %get-tuple-element.159), channel_id=1, source_target_pairs={{0,8},{1,17},{2,10},{3,19},{4,12},{5,21},{6,14},{7,23},{8,0},{9,25... | collective-permute-start | bytes 417800 | tf_op jit(solution)/shard_map/ppermute | solution.py:908
  130.3 2.5 %collective-permute-done.20 = bf16[2,272,128]{2,1,0:T(8,128)(2,1)S(1)} collective-permute-done((bf16[2,272,128]{2,1,0:T(8,128)(2,1)S(1)}, bf16[2,272,128]{2,1,0:T(8,128)(2,1)S(1)}, u32[]{:S(2)}, u32[]{:S(2)}) %collective-permute-start.20) | collective-permute-done | bytes 139296 | tf_op jit(solution)/shard_map/ppermute | solution.py:908
  132.9 2.4 %collective-permute-start.21 = (bf16[1,272,128]{2,1,0:T(8,128)(2,1)S(1)}, bf16[1,272,128]{2,1,0:T(8,128)(2,1)S(1)}, u32[]{:S(2)}, u32[]{:S(2)}) collective-permute-start(bf16[1,272,128]{2,1,0:T(8,128)(2,1)S(1)} %get-tuple-element.165), channel_id=1, source_target_pairs={{0,16},{1,9},{2,18},{3,11},{4,20},{5,13},{6,22},{7,15},{8,24},{9,1... | collective-permute-start | bytes 208904 | tf_op jit(solution)/shard_map/ppermute | solution.py:908
  136.0 4.9 %collective-permute-done.26.back_came_ref = bf16[1,256,128]{2,1,0:T(8,128)(2,1)S(1)} collective-permute-done((bf16[1,256,128]{2,1,0:T(8,128)(2,1)S(1)}, bf16[1,256,128]{2,1,0:T(8,128)(2,1)S(1)}, u32[]{:S(2)}, u32[]{:S(2)}) %collective-permute-start.26) | collective-permute-done | bytes 65568 | tf_op jit(solution)/shard_map/ppermute | solution.py:908
  (63 shorter events, 15.7 us)
Async XLA Ops:
  1.7 8.4 %collective-permute-start.1 = (bf16[1,9,64,128]{3,2,1,0:T(8,128)(2,1)S(1)}, bf16[1,9,64,128]{3,2,1,0:T(8,128)(2,1)S(1)}, u32[]{:S(2)}, u32[]{:S(2)}) collective-permute-start(bf16[1,9,64,128]{3,2,1,0:T(8,128)(2,1)S(1)} %bitcast.8), channel_id=1, source_target_pairs={{0,16},{1,9},{2,18},{3,11},{4,20},{5,13},{6,22},{7,15},{8,24},{9,1... | collective-permute-start | bytes 442376 | tf_op jit(solution)/shard_map/ppermute | solution.py:908
  10.1 9.8 %collective-permute-start.3 = (bf16[2,9,64,128]{3,2,1,0:T(8,128)(2,1)S(1)}, bf16[2,9,64,128]{3,2,1,0:T(8,128)(2,1)S(1)}, u32[]{:S(2)}, u32[]{:S(2)}) collective-permute-start(bf16[2,9,64,128]{3,2,1,0:T(8,128)(2,1)S(1)} %join.6.first_ref), channel_id=1, source_target_pairs={{0,8},{1,17},{2,10},{3,19},{4,12},{5,21},{6,14},{7,23},{8,0},{9,25... | collective-permute-start | bytes 884744 | tf_op jit(solution)/shard_map/ppermute | solution.py:908
  11.8 5.1 %collective-permute-start.2 = (bf16[2,272,128]{2,1,0:T(8,128)(2,1)S(1)}, bf16[2,272,128]{2,1,0:T(8,128)(2,1)S(1)}, u32[]{:S(2)}, u32[]{:S(2)}) collective-permute-start(bf16[2,272,128]{2,1,0:T(8,128)(2,1)S(1)} %join.7.first_ref), channel_id=1, source_target_pairs={{0,2},{1,3},{2,0},{3,1},{4,6},{5,7},{6,4},{7,5},{8,10},{9,11},{10,... | collective-permute-start | bytes 417800 | tf_op jit(solution)/shard_map/ppermute | solution.py:908
  20.0 12.1 %collective-permute-start.5 = (bf16[4,9,64,128]{3,2,1,0:T(8,128)(2,1)S(1)}, bf16[4,9,64,128]{3,2,1,0:T(8,128)(2,1)S(1)}, u32[]{:S(2)}, u32[]{:S(2)}) collective-permute-start(bf16[4,9,64,128]{3,2,1,0:T(8,128)(2,1)S(1)} %join.8.first_ref), channel_id=1, source_target_pairs={{0,4},{1,3},{2,6},{3,1},{4,0},{5,7},{6,2},{7,5},{8,12},{9,11},{10,... | collective-permute-start | bytes 1769480 | tf_op jit(solution)/shard_map/ppermute | solution.py:908
  21.6 10.5 %collective-permute-start.4 = (bf16[4,272,128]{2,1,0:T(8,128)(2,1)S(1)}, bf16[4,272,128]{2,1,0:T(8,128)(2,1)S(1)}, u32[]{:S(2)}, u32[]{:S(2)}) collective-permute-start(bf16[4,272,128]{2,1,0:T(8,128)(2,1)S(1)} %join.9.first_ref), channel_id=1, source_target_pairs={{0,16},{1,9},{2,18},{3,11},{4,20},{5,13},{6,22},{7,15},{8,24},{9,1... | collective-permute-start | bytes 835592 | tf_op jit(solution)/shard_map/ppermute | solution.py:908
  32.2 17.1 %collective-permute-start.7 = (bf16[8,9,64,128]{3,2,1,0:T(8,128)(2,1)S(1)}, bf16[8,9,64,128]{3,2,1,0:T(8,128)(2,1)S(1)}, u32[]{:S(2)}, u32[]{:S(2)}) collective-permute-start(bf16[8,9,64,128]{3,2,1,0:T(8,128)(2,1)S(1)} %join.10.p0_ref), channel_id=1, source_target_pairs={{0,2},{1,5},{2,0},{3,7},{4,6},{5,1},{6,4},{7,3},{8,10},{9,13},{10,... | collective-permute-start | bytes 3538952 | tf_op jit(solution)/shard_map/ppermute | solution.py:908
  33.8 15.5 %collective-permute-start.6 = (bf16[8,272,128]{2,1,0:T(8,128)(2,1)S(1)}, bf16[8,272,128]{2,1,0:T(8,128)(2,1)S(1)}, u32[]{:S(2)}, u32[]{:S(2)}) collective-permute-start(bf16[8,272,128]{2,1,0:T(8,128)(2,1)S(1)} %join.11.p0_ref), channel_id=1, source_target_pairs={{0,8},{1,17},{2,10},{3,19},{4,12},{5,21},{6,14},{7,23},{8,0},{9,25... | collective-permute-start | bytes 1671176 | tf_op jit(solution)/shard_map/ppermute | solution.py:908
  33.9 15.9 %collective-permute-start.10 = (bf16[8,272,128]{2,1,0:T(8,128)(2,1)S(1)}, bf16[8,272,128]{2,1,0:T(8,128)(2,1)S(1)}, u32[]{:S(2)}, u32[]{:S(2)}) collective-permute-start(bf16[8,272,128]{2,1,0:T(8,128)(2,1)S(1)} %join.11.p0_ref), channel_id=1, source_target_pairs={{0,1},{1,0},{2,3},{3,2},{4,5},{5,4},{6,7},{7,6},{8,9},{9,8},{10,11... | collective-permute-start | bytes 1671176 | tf_op jit(solution)/shard_map/ppermute | solution.py:908
  49.3 10.3 %collective-permute-start.8 = (bf16[8,9,64,128]{3,2,1,0:T(8,128)(2,1)S(1)}, bf16[8,9,64,128]{3,2,1,0:T(8,128)(2,1)S(1)}, u32[]{:S(2)}, u32[]{:S(2)}) collective-permute-start(bf16[8,9,64,128]{3,2,1,0:T(8,128)(2,1)S(1)} %join.10.p0_ref), channel_id=1, source_target_pairs={{0,1},{1,0},{2,3},{3,2},{4,5},{5,4},{6,7},{7,6},{8,9},{9,8},{10,11... | collective-permute-start | bytes 3538952 | tf_op jit(solution)/shard_map/ppermute | solution.py:908
  49.8 9.8 %collective-permute-start.9 = (bf16[8,9,64,128]{3,2,1,0:T(8,128)(2,1)S(1)}, bf16[8,9,64,128]{3,2,1,0:T(8,128)(2,1)S(1)}, u32[]{:S(2)}, u32[]{:S(2)}) collective-permute-start(bf16[8,9,64,128]{3,2,1,0:T(8,128)(2,1)S(1)} %collective-permute-done.7.p1_ref), channel_id=1, source_target_pairs={{0,1},{1,0},{2,3},{3,2},{4,5},{5,4},{6,7},{7,6},{8,9},{9,8},{10,11... | collective-permute-start | bytes 3538952 | tf_op jit(solution)/shard_map/ppermute | solution.py:908
  73.5 10.8 %collective-permute-start.12 = (bf16[16,256,128]{2,1,0:T(8,128)(2,1)S(1)}, bf16[16,256,128]{2,1,0:T(8,128)(2,1)S(1)}, u32[]{:S(2)}, u32[]{:S(2)}) collective-permute-start(bf16[16,256,128]{2,1,0:T(8,128)(2,1)S(1)} %get-tuple-element.109), channel_id=1, source_target_pairs={{0,1},{1,0},{2,3},{3,2},{4,5},{5,4},{6,7},{7,6},{8,9},{9,8},{10,11... | collective-permute-start | bytes 3145736 | tf_op jit(solution)/shard_map/ppermute | solution.py:908
  84.0 10.3 %collective-permute-start.14 = (bf16[16,5,64,128]{3,2,1,0:T(8,128)(2,1)S(1)}, bf16[16,5,64,128]{3,2,1,0:T(8,128)(2,1)S(1)}, u32[]{:S(2)}, u32[]{:S(2)}) collective-permute-start(bf16[16,5,64,128]{3,2,1,0:T(8,128)(2,1)S(1)} %get-tuple-element.113), channel_id=1, source_target_pairs={{0,1},{1,0},{2,3},{3,2},{4,5},{5,4},{6,7},{7,6},{8,9},{9,8},{10,11... | collective-permute-start | bytes 3932168 | tf_op jit(solution)/shard_map/ppermute | solution.py:908
  84.6 9.7 %collective-permute-start.13 = (bf16[8,256,128]{2,1,0:T(8,128)(2,1)S(1)}, bf16[8,256,128]{2,1,0:T(8,128)(2,1)S(1)}, u32[]{:S(2)}, u32[]{:S(2)}) collective-permute-start(bf16[8,256,128]{2,1,0:T(8,128)(2,1)S(1)} %get-tuple-element.149), channel_id=1, source_target_pairs={{0,4},{1,9},{2,6},{3,11},{4,0},{5,13},{6,2},{7,15},{8,12},{9,1},{1... | collective-permute-start | bytes 1572872 | tf_op jit(solution)/shard_map/ppermute | solution.py:908
  94.9 10.7 %collective-permute-start.16 = (bf16[8,5,64,128]{3,2,1,0:T(8,128)(2,1)S(1)}, bf16[8,5,64,128]{3,2,1,0:T(8,128)(2,1)S(1)}, u32[]{:S(2)}, u32[]{:S(2)}) collective-permute-start(bf16[8,5,64,128]{3,2,1,0:T(8,128)(2,1)S(1)} %get-tuple-element.145), channel_id=1, source_target_pairs={{0,2},{1,5},{2,0},{3,7},{4,6},{5,1},{6,4},{7,3},{8,10},{9,13},{10,... | collective-permute-start | bytes 1966088 | tf_op jit(solution)/shard_map/ppermute | solution.py:908
  95.7 9.2 %collective-permute-start.15 = (bf16[4,256,128]{2,1,0:T(8,128)(2,1)S(1)}, bf16[4,256,128]{2,1,0:T(8,128)(2,1)S(1)}, u32[]{:S(2)}, u32[]{:S(2)}) collective-permute-start(bf16[4,256,128]{2,1,0:T(8,128)(2,1)S(1)} %get-tuple-element.155), channel_id=1, source_target_pairs={{0,8},{1,17},{2,10},{3,19},{4,12},{5,21},{6,14},{7,23},{8,0},{9,25... | collective-permute-start | bytes 786440 | tf_op jit(solution)/shard_map/ppermute | solution.py:908
  108.5 11.6 %collective-permute-start.18 = (bf16[8,272,128]{2,1,0:T(8,128)(2,1)S(1)}, bf16[8,272,128]{2,1,0:T(8,128)(2,1)S(1)}, u32[]{:S(2)}, u32[]{:S(2)}) collective-permute-start(bf16[8,272,128]{2,1,0:T(8,128)(2,1)S(1)} %get-tuple-element.147), channel_id=1, source_target_pairs={{0,2},{1,5},{2,0},{3,7},{4,6},{5,1},{6,4},{7,3},{8,10},{9,13},{10,... | collective-permute-start | bytes 1671176 | tf_op jit(solution)/shard_map/ppermute | solution.py:908
  109.5 10.6 %collective-permute-start.22 = (bf16[4,5,64,128]{3,2,1,0:T(8,128)(2,1)S(1)}, bf16[4,5,64,128]{3,2,1,0:T(8,128)(2,1)S(1)}, u32[]{:S(2)}, u32[]{:S(2)}) collective-permute-start(bf16[4,5,64,128]{3,2,1,0:T(8,128)(2,1)S(1)} %get-tuple-element.151), channel_id=1, source_target_pairs={{0,8},{1,17},{2,10},{3,19},{4,12},{5,21},{6,14},{7,23},{8,0},{9,25... | collective-permute-start | bytes 983048 | tf_op jit(solution)/shard_map/ppermute | solution.py:908
  120.2 7.1 %collective-permute-start.23 = (bf16[2,5,64,128]{3,2,1,0:T(8,128)(2,1)S(1)}, bf16[2,5,64,128]{3,2,1,0:T(8,128)(2,1)S(1)}, u32[]{:S(2)}, u32[]{:S(2)}) collective-permute-start(bf16[2,5,64,128]{3,2,1,0:T(8,128)(2,1)S(1)} %get-tuple-element.157), channel_id=1, source_target_pairs={{0,16},{1,9},{2,18},{3,11},{4,20},{5,13},{6,22},{7,15},{8,24},{9,1... | collective-permute-start | bytes 491528 | tf_op jit(solution)/shard_map/ppermute | solution.py:908
  120.4 6.9 %collective-permute-start.19 = (bf16[4,272,128]{2,1,0:T(8,128)(2,1)S(1)}, bf16[4,272,128]{2,1,0:T(8,128)(2,1)S(1)}, u32[]{:S(2)}, u32[]{:S(2)}) collective-permute-start(bf16[4,272,128]{2,1,0:T(8,128)(2,1)S(1)} %get-tuple-element.153), channel_id=1, source_target_pairs={{0,4},{1,3},{2,6},{3,1},{4,0},{5,7},{6,2},{7,5},{8,12},{9,11},{10,... | collective-permute-start | bytes 835592 | tf_op jit(solution)/shard_map/ppermute | solution.py:908
  121.5 5.0 %collective-permute-start.25 = (bf16[2,256,128]{2,1,0:T(8,128)(2,1)S(1)}, bf16[2,256,128]{2,1,0:T(8,128)(2,1)S(1)}, u32[]{:S(2)}, u32[]{:S(2)}) collective-permute-start(bf16[2,256,128]{2,1,0:T(8,128)(2,1)S(1)} %get-tuple-element.161), channel_id=1, source_target_pairs={{0,2},{1,5},{2,0},{3,7},{4,6},{5,1},{6,4},{7,3},{8,10},{9,13},{10,... | collective-permute-start | bytes 393224 | tf_op jit(solution)/shard_map/ppermute | solution.py:908
  127.3 5.6 %collective-permute-start.20 = (bf16[2,272,128]{2,1,0:T(8,128)(2,1)S(1)}, bf16[2,272,128]{2,1,0:T(8,128)(2,1)S(1)}, u32[]{:S(2)}, u32[]{:S(2)}) collective-permute-start(bf16[2,272,128]{2,1,0:T(8,128)(2,1)S(1)} %get-tuple-element.159), channel_id=1, source_target_pairs={{0,8},{1,17},{2,10},{3,19},{4,12},{5,21},{6,14},{7,23},{8,0},{9,25... | collective-permute-start | bytes 417800 | tf_op jit(solution)/shard_map/ppermute | solution.py:908
  129.6 11.2 %collective-permute-start.24 = (bf16[1,5,64,128]{3,2,1,0:T(8,128)(2,1)S(1)}, bf16[1,5,64,128]{3,2,1,0:T(8,128)(2,1)S(1)}, u32[]{:S(2)}, u32[]{:S(2)}) collective-permute-start(bf16[1,5,64,128]{3,2,1,0:T(8,128)(2,1)S(1)} %get-tuple-element.163), channel_id=1, source_target_pairs={{0,4},{1,3},{2,6},{3,1},{4,0},{5,7},{6,2},{7,5},{8,12},{9,11},{10,... | collective-permute-start | bytes 245768 | tf_op jit(solution)/shard_map/ppermute | solution.py:908
  132.9 8.0 %collective-permute-start.21 = (bf16[1,272,128]{2,1,0:T(8,128)(2,1)S(1)}, bf16[1,272,128]{2,1,0:T(8,128)(2,1)S(1)}, u32[]{:S(2)}, u32[]{:S(2)}) collective-permute-start(bf16[1,272,128]{2,1,0:T(8,128)(2,1)S(1)} %get-tuple-element.165), channel_id=1, source_target_pairs={{0,16},{1,9},{2,18},{3,11},{4,20},{5,13},{6,22},{7,15},{8,24},{9,1... | collective-permute-start | bytes 208904 | tf_op jit(solution)/shard_map/ppermute | solution.py:908
  135.3 5.5 %collective-permute-start.26 = (bf16[1,256,128]{2,1,0:T(8,128)(2,1)S(1)}, bf16[1,256,128]{2,1,0:T(8,128)(2,1)S(1)}, u32[]{:S(2)}, u32[]{:S(2)}) collective-permute-start(bf16[1,256,128]{2,1,0:T(8,128)(2,1)S(1)} %get-tuple-element.167), channel_id=1, source_target_pairs={{0,16},{1,3},{2,18},{3,1},{4,20},{5,7},{6,22},{7,5},{8,24},{9,11},... | collective-permute-start | bytes 196616 | tf_op jit(solution)/shard_map/ppermute | solution.py:908
  (7 other events, 80.1 us)

commit v4 on v3

--- a/solution.py
+++ b/solution.py
@@ -241,7 +241,7 @@
             ).astype(BF16)
         return unused
 
-    lax.fori_loop(0, NARROW, per_pair, 0)
+    lax.fori_loop(0, NARROW, per_pair, 0, unroll=2)
     leave.wait()
 
 
@@ -642,7 +642,9 @@
 
 def finish_kernel(
     outer_ref,
-    outer_came_ref,
+    outer_first_ref,
+    outer_second_ref,
+    outer_third_ref,
     inner_ref,
     inner_came_ref,
     back_ref,
@@ -666,7 +668,8 @@
             0, part
         ].astype(F32)
     out_ref[...] = inner_ref[0, 4] + inner_came_ref[0, 4].astype(F32)
-    total = outer_ref[0] + outer_came_ref[0].astype(F32)
+    total = outer_ref[0] + outer_first_ref[0].astype(F32)
+    total += outer_second_ref[0].astype(F32) + outer_third_ref[0].astype(F32)
     query_ref[...] = total[0:64]
     key_ref[...] = total[64:128]
     value_ref[...] = total[128:192]
@@ -897,7 +900,7 @@
             shape((2, 64), F32),
             shape((1, 64), F32),
         ),
-        in_specs=[vmem()] * 6,
+        in_specs=[vmem()] * 8,
         out_specs=tuple([vmem()] * 9),
         compiler_params=params(6),
         name="finish",
@@ -925,6 +928,18 @@
     upper = (held[size:] + came[size:].astype(F32)).astype(BF16)
     lower = held[:size] + came[:size].astype(F32)
     return lower, swap(upper, order, step)
+
+
+def scatter_rest(held, came, order):
+    own = held[:1] + came[:1].astype(F32)
+    others = []
+    for block in range(1, 4):
+        total = (held[block : block + 1] + came[block : block + 1].astype(F32)).astype(BF16)
+        partners = []
+        for place in range(PLACES):
+            partners.append((place, place ^ block_masks(order, place & 1)[block]))
+        others.append(lax.ppermute(total, AXES, partners))
+    return own, *others
 
 
 def small_block(vectors, in_bias, wide, narrow):
@@ -1018,13 +1033,15 @@
     outer = start_halving(keep, send, ORDER_OUTER)
     back = halve(back[0], back_came, ORDER_BACK, 1)
     inner = halve(inner[0], inner_came, ORDER_INNER, 2)
-    for step in (3, 2, 1):
-        outer = halve(*outer, ORDER_OUTER, step)
-        if step == 3:
-            back = halve(back[0], after(back[1], outer[1]), ORDER_BACK, 0)
-        if step > 1:
-            inner = halve(inner[0], after(inner[1], outer[1]), ORDER_INNER, step - 2)
-    outer = halve(*outer, ORDER_OUTER, 0)
+    outer = halve(*outer, ORDER_OUTER, 3)
+    came = lax.optimization_barrier((outer[1], inner[1], back[1]))
+    outer = halve(outer[0], came[0], ORDER_OUTER, 2)
+    inner = halve(inner[0], came[1], ORDER_INNER, 1)
+    back = halve(back[0], came[2], ORDER_BACK, 0)
+    came = lax.optimization_barrier((outer[1], inner[1], back[1]))
+    outer = scatter_rest(outer[0], came[0], ORDER_OUTER)
+    inner = halve(inner[0], came[1], ORDER_INNER, 0)
+    back = back[0], came[2]
     *matrices, vec, bins = finish_call(outer, inner, back)
     return (
         output.reshape(inputs.shape),

time: 142 us -> 138 us (0.972)
  waiting for transfers between devices: 65.4 us -> 60.2 us
    ppermute x27 -> x25, waiting for transfers between devices: 65.4 us -> 56.9 us  [swap(): return lax.ppermute(array, AXES, pairs(order, step))]
    ppermute x0 -> x3, starting transfers between devices: none -> 4.45 us  [scatter_rest(): others.append(lax.ppermute(total, AXES, partners))]
    ppermute x0 -> x3, waiting for transfers between devices: none -> 3.21 us  [scatter_rest(): others.append(lax.ppermute(total, AXES, partners))]
    ppermute x27 -> x25, starting transfers between devices: 24.7 us -> 21.6 us  [swap(): return lax.ppermute(array, AXES, pairs(order, step))]
  transfers between devices with their start and end apart: 27 -> 28, of which waited for: 14 -> 15; matrix products, arithmetic and copies ran while one was open for 1% -> 1% of each run, Pallas kernels for 23% -> 23%
where the time goes in v4:
time: 138 us; the launch traced here: 137 us
  waiting for transfers between devices  60.2 us (44%)
  Pallas kernels  47.5 us (34%)
  starting transfers between devices  26 us (19%)
  other arithmetic  1.66 us (1%)
    ppermute x25, waiting for transfers between devices, swap(): return lax.ppermute(array, AXES, pairs(order, step))  56.9 us
    ppermute x25, starting transfers between devices, swap(): return lax.ppermute(array, AXES, pairs(order, step))  21.6 us
    pallas_call x1, Pallas kernels, forward_call(): pl.pallas_call(partial(forward_kernel, direct), out_shape=(shape((total,...  14.1 us
    pallas_call x1, Pallas kernels, backward_call(): pl.pallas_call(partial(backward_kernel, direct), out_shape=(shape((total,...  10.2 us
    pallas_call x1, Pallas kernels, attend_back_call(): pl.pallas_call(partial(attend_back_kernel, direct), out_shape=(shape((tot...  8.06 us
    pallas_call x1, Pallas kernels, attend_call(): pl.pallas_call(partial(attend_kernel, direct), out_shape=(pltpu.HBM((tota...  7.85 us
    pallas_call x1, Pallas kernels, project_back_call(): pl.pallas_call(partial(project_back_kernel, direct, windows), out_shape=(...  5.28 us
    ppermute x3, starting transfers between devices, scatter_rest(): others.append(lax.ppermute(total, AXES, partners))  4.45 us
  transfers between devices with their start and end apart: 28, of which 15 were waited for; matrix products, arithmetic and copies ran while one was open for 1% of the time, Pallas kernels for 23%

profile of v4, /device:TPU:0, one launch (start us, length us, event | category | flops | bytes accessed | tf_op | source)
XLA Modules:
  0.0 137.3 jit_solution(7419784535854928259)
XLA Ops:
  1.7 4.1 %collective-permute-start.1 = (bf16[1,9,64,128]{3,2,1,0:T(8,128)(2,1)S(1)}, bf16[1,9,64,128]{3,2,1,0:T(8,128)(2,1)S(1)}, u32[]{:S(2)}, u32[]{:S(2)}) collective-permute-start(bf16[1,9,64,128]{3,2,1,0:T(8,128)(2,1)S(1)} %bitcast.8), channel_id=1, source_target_pairs={{0,16},{1,9},{2,18},{3,11},{4,20},{5,13},{6,22},{7,15},{8,24},{9,1... | collective-permute-start | bytes 442376 | tf_op jit(solution)/shard_map/ppermute | solution.py:911
  5.8 1.5 %collective-permute-start = (bf16[1,272,128]{2,1,0:T(8,128)(2,1)S(1)}, bf16[1,272,128]{2,1,0:T(8,128)(2,1)S(1)}, u32[]{:S(2)}, u32[]{:S(2)}) collective-permute-start(bf16[1,272,128]{2,1,0:T(8,128)(2,1)S(1)} %bitcast.10), channel_id=1, source_target_pairs={{0,4},{1,5},{2,6},{3,7},{4,0},{5,1},{6,2},{7,3},{8,12},{9,13},{10,... | collective-permute-start | bytes 208904 | tf_op jit(solution)/shard_map/ppermute | solution.py:911
  7.3 2.8 %collective-permute-done.second_ref = bf16[1,272,128]{2,1,0:T(8,128)(2,1)S(1)} collective-permute-done((bf16[1,272,128]{2,1,0:T(8,128)(2,1)S(1)}, bf16[1,272,128]{2,1,0:T(8,128)(2,1)S(1)}, u32[]{:S(2)}, u32[]{:S(2)}) %collective-permute-start) | collective-permute-done | bytes 69664 | tf_op jit(solution)/shard_map/ppermute | solution.py:911
  10.1 1.6 %collective-permute-start.3 = (bf16[2,9,64,128]{3,2,1,0:T(8,128)(2,1)S(1)}, bf16[2,9,64,128]{3,2,1,0:T(8,128)(2,1)S(1)}, u32[]{:S(2)}, u32[]{:S(2)}) collective-permute-start(bf16[2,9,64,128]{3,2,1,0:T(8,128)(2,1)S(1)} %join.6.first_ref), channel_id=1, source_target_pairs={{0,8},{1,17},{2,10},{3,19},{4,12},{5,21},{6,14},{7,23},{8,0},{9,25... | collective-permute-start | bytes 884744 | tf_op jit(solution)/shard_map/ppermute | solution.py:911
  11.8 1.6 %collective-permute-start.2 = (bf16[2,272,128]{2,1,0:T(8,128)(2,1)S(1)}, bf16[2,272,128]{2,1,0:T(8,128)(2,1)S(1)}, u32[]{:S(2)}, u32[]{:S(2)}) collective-permute-start(bf16[2,272,128]{2,1,0:T(8,128)(2,1)S(1)} %join.7.first_ref), channel_id=1, source_target_pairs={{0,2},{1,3},{2,0},{3,1},{4,6},{5,7},{6,4},{7,5},{8,10},{9,11},{10,... | collective-permute-start | bytes 417800 | tf_op jit(solution)/shard_map/ppermute | solution.py:911
  13.3 3.5 %collective-permute-done.2.second_ref = bf16[2,272,128]{2,1,0:T(8,128)(2,1)S(1)} collective-permute-done((bf16[2,272,128]{2,1,0:T(8,128)(2,1)S(1)}, bf16[2,272,128]{2,1,0:T(8,128)(2,1)S(1)}, u32[]{:S(2)}, u32[]{:S(2)}) %collective-permute-start.2) | collective-permute-done | bytes 139296 | tf_op jit(solution)/shard_map/ppermute | solution.py:911
  16.9 3.1 %collective-permute-done.3.second_ref = bf16[2,9,64,128]{3,2,1,0:T(8,128)(2,1)S(1)} collective-permute-done((bf16[2,9,64,128]{3,2,1,0:T(8,128)(2,1)S(1)}, bf16[2,9,64,128]{3,2,1,0:T(8,128)(2,1)S(1)}, u32[]{:S(2)}, u32[]{:S(2)}) %collective-permute-start.3) | collective-permute-done | bytes 294944 | tf_op jit(solution)/shard_map/ppermute | solution.py:911
  20.0 1.6 %collective-permute-start.5 = (bf16[4,9,64,128]{3,2,1,0:T(8,128)(2,1)S(1)}, bf16[4,9,64,128]{3,2,1,0:T(8,128)(2,1)S(1)}, u32[]{:S(2)}, u32[]{:S(2)}) collective-permute-start(bf16[4,9,64,128]{3,2,1,0:T(8,128)(2,1)S(1)} %join.8.first_ref), channel_id=1, source_target_pairs={{0,4},{1,3},{2,6},{3,1},{4,0},{5,7},{6,2},{7,5},{8,12},{9,11},{10,... | collective-permute-start | bytes 1769480 | tf_op jit(solution)/shard_map/ppermute | solution.py:911
  22.7 9.4 %collective-permute-done.4.second_ref = bf16[4,272,128]{2,1,0:T(8,128)(2,1)S(1)} collective-permute-done((bf16[4,272,128]{2,1,0:T(8,128)(2,1)S(1)}, bf16[4,272,128]{2,1,0:T(8,128)(2,1)S(1)}, u32[]{:S(2)}, u32[]{:S(2)}) %collective-permute-start.4) | collective-permute-done | bytes 278560 | tf_op jit(solution)/shard_map/ppermute | solution.py:911
  32.2 1.6 %collective-permute-start.7 = (bf16[8,9,64,128]{3,2,1,0:T(8,128)(2,1)S(1)}, bf16[8,9,64,128]{3,2,1,0:T(8,128)(2,1)S(1)}, u32[]{:S(2)}, u32[]{:S(2)}) collective-permute-start(bf16[8,9,64,128]{3,2,1,0:T(8,128)(2,1)S(1)} %join.10.p0_ref), channel_id=1, source_target_pairs={{0,2},{1,5},{2,0},{3,7},{4,6},{5,1},{6,4},{7,3},{8,10},{9,13},{10,... | collective-permute-start | bytes 3538952 | tf_op jit(solution)/shard_map/ppermute | solution.py:911
  34.0 15.3 %collective-permute-done.6.p1_ref = bf16[8,272,128]{2,1,0:T(8,128)(2,1)S(1)} collective-permute-done((bf16[8,272,128]{2,1,0:T(8,128)(2,1)S(1)}, bf16[8,272,128]{2,1,0:T(8,128)(2,1)S(1)}, u32[]{:S(2)}, u32[]{:S(2)}) %collective-permute-start.6) | collective-permute-done | bytes 557088 | tf_op jit(solution)/shard_map/ppermute | solution.py:911
  51.2 7.8 %attend.1 = (bf16[1024,1536]{1,0:T(8,128)(2,1)}, bf16[1024,512]{1,0:T(8,128)(2,1)S(1)}, f32[4,2,4,256]{3,2,1,0:T(4,128)S(1)}, f32[1024,512]{1,0:T(8,128)S(1)}, b...) custom-call(s32[2,512]{1,0:T(2,128)S(1)} %copy-done.2, ...), custom_call_target="tpu_custom_call" | custom-call | flops 12582912000 | bytes 12582912 | tf_op jit(solution)/shard_map/attend/pallas_call | solution.py:724
  59.1 14.1 %forward.1 = (bf16[1024,512]{1,0:T(8,128)(2,1)}, f32[1024,2048]{1,0:T(8,128)S(1)}, f32[1024,512]{1,0:T(8,128)S(1)}, f32[1024,512]{1,0:T(8,128)S(1)}, bf16[8,64,1...) custom-call(bf16[1024,512]{1,0:T(8,128)(2,1)S(1)} %get-tuple-element, ...), custom_call_target="tpu_custom_call", output_to_operand_aliasing={{3}: (1, {})} | custom-call | flops 12582912000 | bytes 25165824 | tf_op jit(solution)/shard_map/forward/pallas_call | solution.py:761
  73.4 10.2 %backward.1 = (f32[1024,512]{1,0:T(8,128)S(1)}, bf16[1024,512]{1,0:T(8,128)(2,1)S(1)}, f32[16,5,64,128]{3,2,1,0:T(8,128)S(1)}, bf16[16,5,64,128]{3,2,1,0:T(8,128...) custom-call(f32[1024,2048]{1,0:T(8,128)S(1)} %get-tuple-element.103.slope_ref, ...), custom_call_target="tpu_custom_call" | custom-call | flops 14680064000 | bytes 25165824 | tf_op jit(solution)/shard_map/backward/pallas_call | solution.py:792
  85.9 8.1 %attend_back.1 = (bf16[1024,1536]{1,0:T(8,128)(2,1)S(1)}, f32[4,8,128]{2,1,0:T(8,128)S(1)}) custom-call(s32[2,512]{1,0:T(2,128)S(1)} %copy-done.2, bf16[1024,1536]{1,0:T(8,128)(2,1)S(1)} %copy-done.3, bf16[1024,512]{1,0:T(8,128)(2,1)S(1)} %get-tuple-element.113.grad_attended_ref, f32[4,2,4,256]{3,2,1,0:T(4,128)S(1)} %get-tuple-element.114.lse_ref), custom_call_target="tpu_custom_call" | custom-call | flops 8388608000 | bytes 8388608 | tf_op jit(solution)/shard_map/attend_back/pallas_call | solution.py:826
  95.5 5.3 %project_back.1 = (bf16[1024,512]{1,0:T(8,128)(2,1)}, f32[16,272,128]{2,1,0:T(8,128)S(1)}, bf16[16,272,128]{2,1,0:T(8,128)(2,1)S(1)}) custom-call(bf16[1024,1536]{1,0:T(8,128)(2,1)S(1)} %get-tuple-element.121.grads, bf16[1024,512]{1,0:T(8,128)(2,1)S(1)} %get-tuple-element.122.mixed_ref, f32[1024,512]{1,0:T(8,128)S(1)} %get-tuple-element.123.grad_first_ref, ...), custom_call_target="tpu_custom_call" | custom-call | flops 6291456000 | bytes 8388608 | tf_op jit(solution)/shard_map/project_back/pallas_call | solution.py:840
  100.8 3.8 %collective-permute-done.15 = bf16[4,256,128]{2,1,0:T(8,128)(2,1)S(1)} collective-permute-done((bf16[4,256,128]{2,1,0:T(8,128)(2,1)S(1)}, bf16[4,256,128]{2,1,0:T(8,128)(2,1)S(1)}, u32[]{:S(2)}, u32[]{:S(2)}) %collective-permute-start.15) | collective-permute-done | bytes 262176 | tf_op jit(solution)/shard_map/ppermute | solution.py:911
  105.2 2.8 %collective-permute-done.17 = bf16[16,272,128]{2,1,0:T(8,128)(2,1)S(1)} collective-permute-done((bf16[16,272,128]{2,1,0:T(8,128)(2,1)S(1)}, bf16[16,272,128]{2,1,0:T(8,128)(2,1)S(1)}, u32[]{:S(2)}, u32[]{:S(2)}) %collective-permute-start.17) | collective-permute-done | bytes 1114144 | tf_op jit(solution)/shard_map/ppermute | solution.py:911
  110.6 8.5 %collective-permute-done.20 = bf16[2,256,128]{2,1,0:T(8,128)(2,1)S(1)} collective-permute-done((bf16[2,256,128]{2,1,0:T(8,128)(2,1)S(1)}, bf16[2,256,128]{2,1,0:T(8,128)(2,1)S(1)}, u32[]{:S(2)}, u32[]{:S(2)}) %collective-permute-start.20) | collective-permute-done | bytes 131104 | tf_op jit(solution)/shard_map/ppermute | solution.py:911
  121.2 2.1 %collective-permute-start.23 = (bf16[1,256,128]{2,1,0:T(8,128)(2,1)S(1)}, bf16[1,256,128]{2,1,0:T(8,128)(2,1)S(1)}, u32[]{:S(2)}, u32[]{:S(2)}) collective-permute-start(bf16[1,256,128]{2,1,0:T(8,128)(2,1)S(1)} %get-tuple-element.174), channel_id=1, source_target_pairs={{0,16},{1,3},{2,18},{3,1},{4,20},{5,7},{6,22},{7,5},{8,24},{9,11},... | collective-permute-start | bytes 196616 | tf_op jit(solution)/shard_map/ppermute | solution.py:911
  123.2 5.1 %collective-permute-done.23.back_came_ref = bf16[1,256,128]{2,1,0:T(8,128)(2,1)S(1)} collective-permute-done((bf16[1,256,128]{2,1,0:T(8,128)(2,1)S(1)}, bf16[1,256,128]{2,1,0:T(8,128)(2,1)S(1)}, u32[]{:S(2)}, u32[]{:S(2)}) %collective-permute-start.23) | collective-permute-done | bytes 65568 | tf_op jit(solution)/shard_map/ppermute | solution.py:911
  128.8 2.0 %collective-permute-start.26 = (bf16[1,272,128]{2,1,0:T(8,128)(2,1)S(1)}, bf16[1,272,128]{2,1,0:T(8,128)(2,1)S(1)}, u32[]{:S(2)}, u32[]{:S(2)}) collective-permute-start(bf16[1,272,128]{2,1,0:T(8,128)(2,1)S(1)} %get-tuple-element.165), channel_id=1, source_target_pairs={{0,24},{1,25},{2,26},{3,27},{4,28},{5,29},{6,30},{7,31},{8,16},{9,... | collective-permute-start | bytes 208904 | tf_op jit(solution)/shard_map/ppermute | solution.py:941
  131.2 2.1 %collective-permute-start.24 = (bf16[1,272,128]{2,1,0:T(8,128)(2,1)S(1)}, bf16[1,272,128]{2,1,0:T(8,128)(2,1)S(1)}, u32[]{:S(2)}, u32[]{:S(2)}) collective-permute-start(bf16[1,272,128]{2,1,0:T(8,128)(2,1)S(1)} %get-tuple-element.167), channel_id=1, source_target_pairs={{0,16},{1,9},{2,18},{3,11},{4,20},{5,13},{6,22},{7,15},{8,24},{9,1... | collective-permute-start | bytes 208904 | tf_op jit(solution)/shard_map/ppermute | solution.py:941
  133.3 1.8 %collective-permute-done.26.outer_third_ref = bf16[1,272,128]{2,1,0:T(8,128)(2,1)S(1)} collective-permute-done((bf16[1,272,128]{2,1,0:T(8,128)(2,1)S(1)}, bf16[1,272,128]{2,1,0:T(8,128)(2,1)S(1)}, u32[]{:S(2)}, u32[]{:S(2)}) %collective-permute-start.26) | collective-permute-done | bytes 69664 | tf_op jit(solution)/shard_map/ppermute | solution.py:941
  (64 shorter events, 16.9 us)
Async XLA Ops:
  1.7 8.4 %collective-permute-start.1 = (bf16[1,9,64,128]{3,2,1,0:T(8,128)(2,1)S(1)}, bf16[1,9,64,128]{3,2,1,0:T(8,128)(2,1)S(1)}, u32[]{:S(2)}, u32[]{:S(2)}) collective-permute-start(bf16[1,9,64,128]{3,2,1,0:T(8,128)(2,1)S(1)} %bitcast.8), channel_id=1, source_target_pairs={{0,16},{1,9},{2,18},{3,11},{4,20},{5,13},{6,22},{7,15},{8,24},{9,1... | collective-permute-start | bytes 442376 | tf_op jit(solution)/shard_map/ppermute | solution.py:911
  10.1 9.8 %collective-permute-start.3 = (bf16[2,9,64,128]{3,2,1,0:T(8,128)(2,1)S(1)}, bf16[2,9,64,128]{3,2,1,0:T(8,128)(2,1)S(1)}, u32[]{:S(2)}, u32[]{:S(2)}) collective-permute-start(bf16[2,9,64,128]{3,2,1,0:T(8,128)(2,1)S(1)} %join.6.first_ref), channel_id=1, source_target_pairs={{0,8},{1,17},{2,10},{3,19},{4,12},{5,21},{6,14},{7,23},{8,0},{9,25... | collective-permute-start | bytes 884744 | tf_op jit(solution)/shard_map/ppermute | solution.py:911
  11.8 5.1 %collective-permute-start.2 = (bf16[2,272,128]{2,1,0:T(8,128)(2,1)S(1)}, bf16[2,272,128]{2,1,0:T(8,128)(2,1)S(1)}, u32[]{:S(2)}, u32[]{:S(2)}) collective-permute-start(bf16[2,272,128]{2,1,0:T(8,128)(2,1)S(1)} %join.7.first_ref), channel_id=1, source_target_pairs={{0,2},{1,3},{2,0},{3,1},{4,6},{5,7},{6,4},{7,5},{8,10},{9,11},{10,... | collective-permute-start | bytes 417800 | tf_op jit(solution)/shard_map/ppermute | solution.py:911
  20.0 12.1 %collective-permute-start.5 = (bf16[4,9,64,128]{3,2,1,0:T(8,128)(2,1)S(1)}, bf16[4,9,64,128]{3,2,1,0:T(8,128)(2,1)S(1)}, u32[]{:S(2)}, u32[]{:S(2)}) collective-permute-start(bf16[4,9,64,128]{3,2,1,0:T(8,128)(2,1)S(1)} %join.8.first_ref), channel_id=1, source_target_pairs={{0,4},{1,3},{2,6},{3,1},{4,0},{5,7},{6,2},{7,5},{8,12},{9,11},{10,... | collective-permute-start | bytes 1769480 | tf_op jit(solution)/shard_map/ppermute | solution.py:911
  21.6 10.5 %collective-permute-start.4 = (bf16[4,272,128]{2,1,0:T(8,128)(2,1)S(1)}, bf16[4,272,128]{2,1,0:T(8,128)(2,1)S(1)}, u32[]{:S(2)}, u32[]{:S(2)}) collective-permute-start(bf16[4,272,128]{2,1,0:T(8,128)(2,1)S(1)} %join.9.first_ref), channel_id=1, source_target_pairs={{0,16},{1,9},{2,18},{3,11},{4,20},{5,13},{6,22},{7,15},{8,24},{9,1... | collective-permute-start | bytes 835592 | tf_op jit(solution)/shard_map/ppermute | solution.py:911
  32.2 17.1 %collective-permute-start.7 = (bf16[8,9,64,128]{3,2,1,0:T(8,128)(2,1)S(1)}, bf16[8,9,64,128]{3,2,1,0:T(8,128)(2,1)S(1)}, u32[]{:S(2)}, u32[]{:S(2)}) collective-permute-start(bf16[8,9,64,128]{3,2,1,0:T(8,128)(2,1)S(1)} %join.10.p0_ref), channel_id=1, source_target_pairs={{0,2},{1,5},{2,0},{3,7},{4,6},{5,1},{6,4},{7,3},{8,10},{9,13},{10,... | collective-permute-start | bytes 3538952 | tf_op jit(solution)/shard_map/ppermute | solution.py:911
  33.8 15.5 %collective-permute-start.6 = (bf16[8,272,128]{2,1,0:T(8,128)(2,1)S(1)}, bf16[8,272,128]{2,1,0:T(8,128)(2,1)S(1)}, u32[]{:S(2)}, u32[]{:S(2)}) collective-permute-start(bf16[8,272,128]{2,1,0:T(8,128)(2,1)S(1)} %join.11.p0_ref), channel_id=1, source_target_pairs={{0,8},{1,17},{2,10},{3,19},{4,12},{5,21},{6,14},{7,23},{8,0},{9,25... | collective-permute-start | bytes 1671176 | tf_op jit(solution)/shard_map/ppermute | solution.py:911
  33.9 15.9 %collective-permute-start.10 = (bf16[8,272,128]{2,1,0:T(8,128)(2,1)S(1)}, bf16[8,272,128]{2,1,0:T(8,128)(2,1)S(1)}, u32[]{:S(2)}, u32[]{:S(2)}) collective-permute-start(bf16[8,272,128]{2,1,0:T(8,128)(2,1)S(1)} %join.11.p0_ref), channel_id=1, source_target_pairs={{0,1},{1,0},{2,3},{3,2},{4,5},{5,4},{6,7},{7,6},{8,9},{9,8},{10,11... | collective-permute-start | bytes 1671176 | tf_op jit(solution)/shard_map/ppermute | solution.py:911
  49.3 9.8 %collective-permute-start.8 = (bf16[8,9,64,128]{3,2,1,0:T(8,128)(2,1)S(1)}, bf16[8,9,64,128]{3,2,1,0:T(8,128)(2,1)S(1)}, u32[]{:S(2)}, u32[]{:S(2)}) collective-permute-start(bf16[8,9,64,128]{3,2,1,0:T(8,128)(2,1)S(1)} %join.10.p0_ref), channel_id=1, source_target_pairs={{0,1},{1,0},{2,3},{3,2},{4,5},{5,4},{6,7},{7,6},{8,9},{9,8},{10,11... | collective-permute-start | bytes 3538952 | tf_op jit(solution)/shard_map/ppermute | solution.py:911
  49.8 9.3 %collective-permute-start.9 = (bf16[8,9,64,128]{3,2,1,0:T(8,128)(2,1)S(1)}, bf16[8,9,64,128]{3,2,1,0:T(8,128)(2,1)S(1)}, u32[]{:S(2)}, u32[]{:S(2)}) collective-permute-start(bf16[8,9,64,128]{3,2,1,0:T(8,128)(2,1)S(1)} %collective-permute-done.7.p1_ref), channel_id=1, source_target_pairs={{0,1},{1,0},{2,3},{3,2},{4,5},{5,4},{6,7},{7,6},{8,9},{9,8},{10,11... | collective-permute-start | bytes 3538952 | tf_op jit(solution)/shard_map/ppermute | solution.py:911
  73.2 10.8 %collective-permute-start.12 = (bf16[16,256,128]{2,1,0:T(8,128)(2,1)S(1)}, bf16[16,256,128]{2,1,0:T(8,128)(2,1)S(1)}, u32[]{:S(2)}, u32[]{:S(2)}) collective-permute-start(bf16[16,256,128]{2,1,0:T(8,128)(2,1)S(1)} %get-tuple-element.112), channel_id=1, source_target_pairs={{0,1},{1,0},{2,3},{3,2},{4,5},{5,4},{6,7},{7,6},{8,9},{9,8},{10,11... | collective-permute-start | bytes 3145736 | tf_op jit(solution)/shard_map/ppermute | solution.py:911
  83.6 10.4 %collective-permute-start.14 = (bf16[16,5,64,128]{3,2,1,0:T(8,128)(2,1)S(1)}, bf16[16,5,64,128]{3,2,1,0:T(8,128)(2,1)S(1)}, u32[]{:S(2)}, u32[]{:S(2)}) collective-permute-start(bf16[16,5,64,128]{3,2,1,0:T(8,128)(2,1)S(1)} %get-tuple-element.116), channel_id=1, source_target_pairs={{0,1},{1,0},{2,3},{3,2},{4,5},{5,4},{6,7},{7,6},{8,9},{9,8},{10,11... | collective-permute-start | bytes 3932168 | tf_op jit(solution)/shard_map/ppermute | solution.py:911
  84.3 9.7 %collective-permute-start.13 = (bf16[8,256,128]{2,1,0:T(8,128)(2,1)S(1)}, bf16[8,256,128]{2,1,0:T(8,128)(2,1)S(1)}, u32[]{:S(2)}, u32[]{:S(2)}) collective-permute-start(bf16[8,256,128]{2,1,0:T(8,128)(2,1)S(1)} %get-tuple-element.155), channel_id=1, source_target_pairs={{0,4},{1,9},{2,6},{3,11},{4,0},{5,13},{6,2},{7,15},{8,12},{9,1},{1... | collective-permute-start | bytes 1572872 | tf_op jit(solution)/shard_map/ppermute | solution.py:911
  94.5 10.7 %collective-permute-start.16 = (bf16[8,5,64,128]{3,2,1,0:T(8,128)(2,1)S(1)}, bf16[8,5,64,128]{3,2,1,0:T(8,128)(2,1)S(1)}, u32[]{:S(2)}, u32[]{:S(2)}) collective-permute-start(bf16[8,5,64,128]{3,2,1,0:T(8,128)(2,1)S(1)} %get-tuple-element.151), channel_id=1, source_target_pairs={{0,2},{1,5},{2,0},{3,7},{4,6},{5,1},{6,4},{7,3},{8,10},{9,13},{10,... | collective-permute-start | bytes 1966088 | tf_op jit(solution)/shard_map/ppermute | solution.py:911
  95.4 9.2 %collective-permute-start.15 = (bf16[4,256,128]{2,1,0:T(8,128)(2,1)S(1)}, bf16[4,256,128]{2,1,0:T(8,128)(2,1)S(1)}, u32[]{:S(2)}, u32[]{:S(2)}) collective-permute-start(bf16[4,256,128]{2,1,0:T(8,128)(2,1)S(1)} %get-tuple-element.161), channel_id=1, source_target_pairs={{0,8},{1,17},{2,10},{3,19},{4,12},{5,21},{6,14},{7,23},{8,0},{9,25... | collective-permute-start | bytes 786440 | tf_op jit(solution)/shard_map/ppermute | solution.py:911
  108.1 11.6 %collective-permute-start.18 = (bf16[8,272,128]{2,1,0:T(8,128)(2,1)S(1)}, bf16[8,272,128]{2,1,0:T(8,128)(2,1)S(1)}, u32[]{:S(2)}, u32[]{:S(2)}) collective-permute-start(bf16[8,272,128]{2,1,0:T(8,128)(2,1)S(1)} %get-tuple-element.153), channel_id=1, source_target_pairs={{0,2},{1,5},{2,0},{3,7},{4,6},{5,1},{6,4},{7,3},{8,10},{9,13},{10,... | collective-permute-start | bytes 1671176 | tf_op jit(solution)/shard_map/ppermute | solution.py:911
  109.1 10.6 %collective-permute-start.19 = (bf16[4,5,64,128]{3,2,1,0:T(8,128)(2,1)S(1)}, bf16[4,5,64,128]{3,2,1,0:T(8,128)(2,1)S(1)}, u32[]{:S(2)}, u32[]{:S(2)}) collective-permute-start(bf16[4,5,64,128]{3,2,1,0:T(8,128)(2,1)S(1)} %get-tuple-element.158), channel_id=1, source_target_pairs={{0,8},{1,17},{2,10},{3,19},{4,12},{5,21},{6,14},{7,23},{8,0},{9,25... | collective-permute-start | bytes 983048 | tf_op jit(solution)/shard_map/ppermute | solution.py:911
  109.3 9.9 %collective-permute-start.20 = (bf16[2,256,128]{2,1,0:T(8,128)(2,1)S(1)}, bf16[2,256,128]{2,1,0:T(8,128)(2,1)S(1)}, u32[]{:S(2)}, u32[]{:S(2)}) collective-permute-start(bf16[2,256,128]{2,1,0:T(8,128)(2,1)S(1)} %get-tuple-element.170), channel_id=1, source_target_pairs={{0,2},{1,5},{2,0},{3,7},{4,6},{5,1},{6,4},{7,3},{8,10},{9,13},{10,... | collective-permute-start | bytes 393224 | tf_op jit(solution)/shard_map/ppermute | solution.py:911
  119.8 8.5 %collective-permute-start.22 = (bf16[2,5,64,128]{3,2,1,0:T(8,128)(2,1)S(1)}, bf16[2,5,64,128]{3,2,1,0:T(8,128)(2,1)S(1)}, u32[]{:S(2)}, u32[]{:S(2)}) collective-permute-start(bf16[2,5,64,128]{3,2,1,0:T(8,128)(2,1)S(1)} %get-tuple-element.164), channel_id=1, source_target_pairs={{0,16},{1,9},{2,18},{3,11},{4,20},{5,13},{6,22},{7,15},{8,24},{9,1... | collective-permute-start | bytes 491528 | tf_op jit(solution)/shard_map/ppermute | solution.py:911
  120.0 8.3 %collective-permute-start.21 = (bf16[4,272,128]{2,1,0:T(8,128)(2,1)S(1)}, bf16[4,272,128]{2,1,0:T(8,128)(2,1)S(1)}, u32[]{:S(2)}, u32[]{:S(2)}) collective-permute-start(bf16[4,272,128]{2,1,0:T(8,128)(2,1)S(1)} %get-tuple-element.159), channel_id=1, source_target_pairs={{0,4},{1,3},{2,6},{3,1},{4,0},{5,7},{6,2},{7,5},{8,12},{9,11},{10,... | collective-permute-start | bytes 835592 | tf_op jit(solution)/shard_map/ppermute | solution.py:911
  121.2 7.1 %collective-permute-start.23 = (bf16[1,256,128]{2,1,0:T(8,128)(2,1)S(1)}, bf16[1,256,128]{2,1,0:T(8,128)(2,1)S(1)}, u32[]{:S(2)}, u32[]{:S(2)}) collective-permute-start(bf16[1,256,128]{2,1,0:T(8,128)(2,1)S(1)} %get-tuple-element.174), channel_id=1, source_target_pairs={{0,16},{1,3},{2,18},{3,1},{4,20},{5,7},{6,22},{7,5},{8,24},{9,11},... | collective-permute-start | bytes 196616 | tf_op jit(solution)/shard_map/ppermute | solution.py:911
  128.3 8.1 %collective-permute-start.27 = (bf16[1,5,64,128]{3,2,1,0:T(8,128)(2,1)S(1)}, bf16[1,5,64,128]{3,2,1,0:T(8,128)(2,1)S(1)}, u32[]{:S(2)}, u32[]{:S(2)}) collective-permute-start(bf16[1,5,64,128]{3,2,1,0:T(8,128)(2,1)S(1)} %get-tuple-element.171), channel_id=1, source_target_pairs={{0,4},{1,3},{2,6},{3,1},{4,0},{5,7},{6,2},{7,5},{8,12},{9,11},{10,... | collective-permute-start | bytes 245768 | tf_op jit(solution)/shard_map/ppermute | solution.py:911
  128.8 6.2 %collective-permute-start.26 = (bf16[1,272,128]{2,1,0:T(8,128)(2,1)S(1)}, bf16[1,272,128]{2,1,0:T(8,128)(2,1)S(1)}, u32[]{:S(2)}, u32[]{:S(2)}) collective-permute-start(bf16[1,272,128]{2,1,0:T(8,128)(2,1)S(1)} %get-tuple-element.165), channel_id=1, source_target_pairs={{0,24},{1,25},{2,26},{3,27},{4,28},{5,29},{6,30},{7,31},{8,16},{9,... | collective-permute-start | bytes 208904 | tf_op jit(solution)/shard_map/ppermute | solution.py:941
  131.2 5.3 %collective-permute-start.24 = (bf16[1,272,128]{2,1,0:T(8,128)(2,1)S(1)}, bf16[1,272,128]{2,1,0:T(8,128)(2,1)S(1)}, u32[]{:S(2)}, u32[]{:S(2)}) collective-permute-start(bf16[1,272,128]{2,1,0:T(8,128)(2,1)S(1)} %get-tuple-element.167), channel_id=1, source_target_pairs={{0,16},{1,9},{2,18},{3,11},{4,20},{5,13},{6,22},{7,15},{8,24},{9,1... | collective-permute-start | bytes 208904 | tf_op jit(solution)/shard_map/ppermute | solution.py:941
  (8 other events, 84.5 us)

commit v5 on v4

--- a/solution.py
+++ b/solution.py
@@ -138,7 +138,7 @@
     p1_ref,
     p2_ref,
     p3_ref,
-    qkv_ref,
+    qkv,
     attended_ref,
     lse_ref,
     passed_ref,
@@ -147,7 +147,6 @@
     bin_ref,
     weights,
     bias,
-    qkv,
     table,
     small,
     sems,
@@ -206,9 +205,6 @@
                 own = own * BF16(0.125)
             qkv[:, (chunk * 2 + side) * 128 : (chunk * 2 + side) * 128 + 128] = own
 
-    leave = pltpu.make_async_copy(qkv, qkv_ref, sems.at[3])
-    leave.start()
-
     def per_pair(pair, unused):
         spans = block_spans(windows, length)
         turned_values = [
@@ -242,7 +238,6 @@
         return unused
 
     lax.fori_loop(0, NARROW, per_pair, 0, unroll=2)
-    leave.wait()
 
 
 def norm_parts(values):
@@ -273,12 +268,10 @@
 
 def gelu_both(pre):
     square = pre * pre
-    curve = jnp.tanh(pre * (GELU_SCALE + (GELU_SCALE * 0.044715) * square))
-    half = 0.5 + 0.5 * curve
-    slope = (0.5 * pre) * (1.0 - curve * curve) * (
-        GELU_SCALE + (3.0 * GELU_SCALE * 0.044715) * square
-    )
-    return pre * half, half + slope
+    half = jax.nn.sigmoid(pre * (2.0 * GELU_SCALE + (2.0 * GELU_SCALE * 0.044715) * square))
+    value = pre * half
+    bend = (1.0 - half) * (2.0 * GELU_SCALE + (6.0 * GELU_SCALE * 0.044715) * square)
+    return value, half + value * bend
 
 
 def load_second(me, blocks, w_out, w_in, w_back, sems):
@@ -431,11 +424,13 @@
             weight = w_back[chunk * 4 : chunk * 4 + 4].reshape(256, 512)
             grad = (nt(grad_low, weight) * slope_ref[here, columns]).astype(BF16)
             grad_pre[here, columns] = grad
-            grad_hidden += nt(grad, w_in_columns(w_in, chunk))
             sums = column_sum(grad.astype(F32))
             for part in range(2):
                 row = 2 * (chunk % 4) + part
                 bin_sums_ref[chunk // 4, row : row + 1, :] += sums[:, part * 128 : part * 128 + 128]
+        grad_hidden += nt(
+            grad_pre[here, :], jnp.concatenate([w_in[tile] for tile in range(16)], axis=1)
+        )
         hat, scale = norm_parts(first_ref[here, :])
         gains = vec_row(vec_ref, 4)
         grad_first = norm_back(hat, scale, gains, grad_hidden)
@@ -724,7 +719,7 @@
     return pl.pallas_call(
         partial(attend_kernel, direct),
         out_shape=(
-            pltpu.HBM((total, 1536), BF16),
+            near((total, 1536), BF16),
             shape((total, 512), BF16),
             shape((NARROW, windows, length // 128, 256), F32),
             near((total, 512), F32),
@@ -734,13 +729,12 @@
             shape((512, 1536), BF16),
         ),
         in_specs=[vmem(), vmem()] + [hbm()] * 4,
-        out_specs=(pl.BlockSpec(memory_space=pltpu.HBM),) + tuple([vmem()] * 7),
+        out_specs=tuple([vmem()] * 8),
         scratch_shapes=[
             pltpu.VMEM((windows, length // 128, 384, 128), F32),
-            pltpu.VMEM((total, 1536), BF16),
             pltpu.VMEM((512, 512), BF16),
             pltpu.VMEM((PLACES, 16, 128), BF16),
-            pltpu.SemaphoreType.DMA((4,)),
+            pltpu.SemaphoreType.DMA((3,)),
         ],
         compiler_params=params(ATTEND_MIB),
         cost_estimate=cost(6000 << 20, 12 << 20),
@@ -750,8 +744,8 @@
 
 ROWS = 512
 ATTEND_MIB = 24
-FORWARD_MIB = 14
-BACKWARD_MIB = 14
+FORWARD_MIB = 12
+BACKWARD_MIB = 11
 ATTEND_BACK_MIB = 20
 PROJECT_BACK_MIB = 16
 
@@ -808,6 +802,7 @@
         ],
         compiler_params=params(BACKWARD_MIB),
         cost_estimate=cost(7000 << 20, 24 << 20),
+        input_output_aliases={1: 0, 4: 1},
         name="backward",
     )(
         kept(slope),
@@ -832,7 +827,7 @@
         compiler_params=params(ATTEND_BACK_MIB),
         cost_estimate=cost(4000 << 20, 8 << 20),
         name="attend_back",
-    )(segments, qkv, grad_attended, lse)
+    )(segments, kept(qkv), grad_attended, lse)
 
 
 def project_back_call(direct, windows, grads, mixed, grad_first, sums, weights):
@@ -1029,11 +1024,13 @@
         (pair_sums, sums_a, sums_b, bin_sums),
         w_qkv,
     )
-    keep, send, back_came, inner_came = lax.optimization_barrier((keep, send, back[1], inner[1]))
-    outer = start_halving(keep, send, ORDER_OUTER)
+    keep, send, back_came = lax.optimization_barrier((keep, send, back[1]))
+    upper_came, lower_came = swap(send[8:], ORDER_OUTER, 4), swap(send[:8], ORDER_OUTER, 4)
     back = halve(back[0], back_came, ORDER_BACK, 1)
+    upper_came, inner_came = lax.optimization_barrier((upper_came, inner[1]))
+    upper = (keep[8:] + upper_came.astype(F32)).astype(BF16)
+    outer = keep[:8] + lower_came.astype(F32), swap(upper, ORDER_OUTER, 3)
     inner = halve(inner[0], inner_came, ORDER_INNER, 2)
-    outer = halve(*outer, ORDER_OUTER, 3)
     came = lax.optimization_barrier((outer[1], inner[1], back[1]))
     outer = halve(outer[0], came[0], ORDER_OUTER, 2)
     inner = halve(inner[0], came[1], ORDER_INNER, 1)

time: 138 us -> 135 us (0.978)
  waiting for transfers between devices: 60.2 us -> 56.9 us
  starting transfers between devices: 26 us -> 28.6 us
    ppermute x25 -> x26, waiting for transfers between devices: 56.9 us -> 53.7 us  [swap(): return lax.ppermute(array, AXES, pairs(order, step))]
    ppermute x25 -> x26, starting transfers between devices: 21.6 us -> 24.1 us  [swap(): return lax.ppermute(array, AXES, pairs(order, step))]
  transfers between devices with their start and end apart: 28 -> 29, of which waited for: 15 -> 14; matrix products, arithmetic and copies ran while one was open for 1% -> 1% of each run, Pallas kernels for 23% -> 23%
where the time goes in v5:
time: 135 us; the launch traced here: 134 us
  waiting for transfers between devices  56.9 us (42%)
  Pallas kernels  46.3 us (34%)
  starting transfers between devices  28.6 us (21%)
  other arithmetic  1.66 us (1%)
    ppermute x26, waiting for transfers between devices, swap(): return lax.ppermute(array, AXES, pairs(order, step))  53.7 us
    ppermute x26, starting transfers between devices, swap(): return lax.ppermute(array, AXES, pairs(order, step))  24.1 us
    pallas_call x1, Pallas kernels, forward_call(): pl.pallas_call(partial(forward_kernel, direct), out_shape=(shape((total,...  13 us
    pallas_call x1, Pallas kernels, backward_call(): pl.pallas_call(partial(backward_kernel, direct), out_shape=(shape((total,...  10 us
    pallas_call x1, Pallas kernels, attend_back_call(): pl.pallas_call(partial(attend_back_kernel, direct), out_shape=(shape((tot...  8.04 us
    pallas_call x1, Pallas kernels, attend_call(): pl.pallas_call(partial(attend_kernel, direct), out_shape=(near((total, 15...  7.83 us
    pallas_call x1, Pallas kernels, project_back_call(): pl.pallas_call(partial(project_back_kernel, direct, windows), out_shape=(...  5.29 us
    ppermute x3, starting transfers between devices, scatter_rest(): others.append(lax.ppermute(total, AXES, partners))  4.45 us
  transfers between devices with their start and end apart: 29, of which 14 were waited for; matrix products, arithmetic and copies ran while one was open for 1% of the time, Pallas kernels for 23%

profile of v5, /device:TPU:0, one launch (start us, length us, event | category | flops | bytes accessed | tf_op | source)
XLA Modules:
  0.0 134.4 jit_solution(3253183278331323583)
XLA Ops:
  1.7 4.1 %collective-permute-start.1 = (bf16[1,9,64,128]{3,2,1,0:T(8,128)(2,1)S(1)}, bf16[1,9,64,128]{3,2,1,0:T(8,128)(2,1)S(1)}, u32[]{:S(2)}, u32[]{:S(2)}) collective-permute-start(bf16[1,9,64,128]{3,2,1,0:T(8,128)(2,1)S(1)} %bitcast.8), channel_id=1, source_target_pairs={{0,16},{1,9},{2,18},{3,11},{4,20},{5,13},{6,22},{7,15},{8,24},{9,1... | collective-permute-start | bytes 442376 | tf_op jit(solution)/shard_map/ppermute | solution.py:906
  5.8 1.5 %collective-permute-start = (bf16[1,272,128]{2,1,0:T(8,128)(2,1)S(1)}, bf16[1,272,128]{2,1,0:T(8,128)(2,1)S(1)}, u32[]{:S(2)}, u32[]{:S(2)}) collective-permute-start(bf16[1,272,128]{2,1,0:T(8,128)(2,1)S(1)} %bitcast.10), channel_id=1, source_target_pairs={{0,4},{1,5},{2,6},{3,7},{4,0},{5,1},{6,2},{7,3},{8,12},{9,13},{10,... | collective-permute-start | bytes 208904 | tf_op jit(solution)/shard_map/ppermute | solution.py:906
  7.3 2.8 %collective-permute-done.second_ref = bf16[1,272,128]{2,1,0:T(8,128)(2,1)S(1)} collective-permute-done((bf16[1,272,128]{2,1,0:T(8,128)(2,1)S(1)}, bf16[1,272,128]{2,1,0:T(8,128)(2,1)S(1)}, u32[]{:S(2)}, u32[]{:S(2)}) %collective-permute-start) | collective-permute-done | bytes 69664 | tf_op jit(solution)/shard_map/ppermute | solution.py:906
  10.1 1.6 %collective-permute-start.3 = (bf16[2,9,64,128]{3,2,1,0:T(8,128)(2,1)S(1)}, bf16[2,9,64,128]{3,2,1,0:T(8,128)(2,1)S(1)}, u32[]{:S(2)}, u32[]{:S(2)}) collective-permute-start(bf16[2,9,64,128]{3,2,1,0:T(8,128)(2,1)S(1)} %join.6.first_ref), channel_id=1, source_target_pairs={{0,8},{1,17},{2,10},{3,19},{4,12},{5,21},{6,14},{7,23},{8,0},{9,25... | collective-permute-start | bytes 884744 | tf_op jit(solution)/shard_map/ppermute | solution.py:906
  11.8 1.6 %collective-permute-start.2 = (bf16[2,272,128]{2,1,0:T(8,128)(2,1)S(1)}, bf16[2,272,128]{2,1,0:T(8,128)(2,1)S(1)}, u32[]{:S(2)}, u32[]{:S(2)}) collective-permute-start(bf16[2,272,128]{2,1,0:T(8,128)(2,1)S(1)} %join.7.first_ref), channel_id=1, source_target_pairs={{0,2},{1,3},{2,0},{3,1},{4,6},{5,7},{6,4},{7,5},{8,10},{9,11},{10,... | collective-permute-start | bytes 417800 | tf_op jit(solution)/shard_map/ppermute | solution.py:906
  13.3 3.5 %collective-permute-done.2.second_ref = bf16[2,272,128]{2,1,0:T(8,128)(2,1)S(1)} collective-permute-done((bf16[2,272,128]{2,1,0:T(8,128)(2,1)S(1)}, bf16[2,272,128]{2,1,0:T(8,128)(2,1)S(1)}, u32[]{:S(2)}, u32[]{:S(2)}) %collective-permute-start.2) | collective-permute-done | bytes 139296 | tf_op jit(solution)/shard_map/ppermute | solution.py:906
  16.9 3.1 %collective-permute-done.3.second_ref = bf16[2,9,64,128]{3,2,1,0:T(8,128)(2,1)S(1)} collective-permute-done((bf16[2,9,64,128]{3,2,1,0:T(8,128)(2,1)S(1)}, bf16[2,9,64,128]{3,2,1,0:T(8,128)(2,1)S(1)}, u32[]{:S(2)}, u32[]{:S(2)}) %collective-permute-start.3) | collective-permute-done | bytes 294944 | tf_op jit(solution)/shard_map/ppermute | solution.py:906
  20.0 1.6 %collective-permute-start.5 = (bf16[4,9,64,128]{3,2,1,0:T(8,128)(2,1)S(1)}, bf16[4,9,64,128]{3,2,1,0:T(8,128)(2,1)S(1)}, u32[]{:S(2)}, u32[]{:S(2)}) collective-permute-start(bf16[4,9,64,128]{3,2,1,0:T(8,128)(2,1)S(1)} %join.8.first_ref), channel_id=1, source_target_pairs={{0,4},{1,3},{2,6},{3,1},{4,0},{5,7},{6,2},{7,5},{8,12},{9,11},{10,... | collective-permute-start | bytes 1769480 | tf_op jit(solution)/shard_map/ppermute | solution.py:906
  22.7 9.4 %collective-permute-done.4.second_ref = bf16[4,272,128]{2,1,0:T(8,128)(2,1)S(1)} collective-permute-done((bf16[4,272,128]{2,1,0:T(8,128)(2,1)S(1)}, bf16[4,272,128]{2,1,0:T(8,128)(2,1)S(1)}, u32[]{:S(2)}, u32[]{:S(2)}) %collective-permute-start.4) | collective-permute-done | bytes 278560 | tf_op jit(solution)/shard_map/ppermute | solution.py:906
  32.2 1.6 %collective-permute-start.7 = (bf16[8,9,64,128]{3,2,1,0:T(8,128)(2,1)S(1)}, bf16[8,9,64,128]{3,2,1,0:T(8,128)(2,1)S(1)}, u32[]{:S(2)}, u32[]{:S(2)}) collective-permute-start(bf16[8,9,64,128]{3,2,1,0:T(8,128)(2,1)S(1)} %join.10.p0_ref), channel_id=1, source_target_pairs={{0,2},{1,5},{2,0},{3,7},{4,6},{5,1},{6,4},{7,3},{8,10},{9,13},{10,... | collective-permute-start | bytes 3538952 | tf_op jit(solution)/shard_map/ppermute | solution.py:906
  34.0 15.3 %collective-permute-done.6.p1_ref = bf16[8,272,128]{2,1,0:T(8,128)(2,1)S(1)} collective-permute-done((bf16[8,272,128]{2,1,0:T(8,128)(2,1)S(1)}, bf16[8,272,128]{2,1,0:T(8,128)(2,1)S(1)}, u32[]{:S(2)}, u32[]{:S(2)}) %collective-permute-start.6) | collective-permute-done | bytes 557088 | tf_op jit(solution)/shard_map/ppermute | solution.py:906
  51.2 7.8 %attend.1 = (bf16[1024,1536]{1,0:T(8,128)(2,1)S(1)}, bf16[1024,512]{1,0:T(8,128)(2,1)S(1)}, f32[4,2,4,256]{3,2,1,0:T(4,128)S(1)}, f32[1024,512]{1,0:T(8,128)S(1)...) custom-call(s32[2,512]{1,0:T(2,128)S(1)} %copy-done.2, ...), custom_call_target="tpu_custom_call" | custom-call | flops 12582912000 | bytes 12582912 | tf_op jit(solution)/shard_map/attend/pallas_call | solution.py:719
  59.1 13.0 %forward.1 = (bf16[1024,512]{1,0:T(8,128)(2,1)}, f32[1024,2048]{1,0:T(8,128)S(1)}, f32[1024,512]{1,0:T(8,128)S(1)}, f32[1024,512]{1,0:T(8,128)S(1)}, bf16[8,64,1...) custom-call(bf16[1024,512]{1,0:T(8,128)(2,1)S(1)} %get-tuple-element, ...), custom_call_target="tpu_custom_call", output_to_operand_aliasing={{3}: (1, {})} | custom-call | flops 12582912000 | bytes 25165824 | tf_op jit(solution)/shard_map/forward/pallas_call | solution.py:755
  72.4 10.0 %backward.1 = (f32[1024,512]{1,0:T(8,128)S(1)}, bf16[1024,512]{1,0:T(8,128)(2,1)S(1)}, f32[16,5,64,128]{3,2,1,0:T(8,128)S(1)}, bf16[16,5,64,128]{3,2,1,0:T(8,128...) custom-call(f32[1024,2048]{1,0:T(8,128)S(1)} %get-tuple-element.104.slop, ...), custom_call_target="tpu_custom_call", output_to_operand_aliasing={{0}: (1, {}), {1}: (4, {})} | custom-call | flops 14680064000 | bytes 25165824 | tf_op jit(solution)/shard_map/backward/pallas_call | solution.py:786
  83.6 8.0 %attend_back.1 = (bf16[1024,1536]{1,0:T(8,128)(2,1)S(1)}, f32[4,8,128]{2,1,0:T(8,128)S(1)}) custom-call(s32[2,512]{1,0:T(2,128)S(1)} %copy-done.2, bf16[1024,1536]{1,0:T(8,128)(2,1)S(1)} %get-tuple-element.103.qkv_ref, bf16[1024,512]{1,0:T(8,128)(2,1)S(1)} %get-tuple-element.114.grad_attended_ref, f32[4,2,4,256]{3,2,1,0:T(4,128)S(1)} %get-tuple-element.115.lse_ref), custom_call_target="tpu_custom_call" | custom-call | flops 8388608000 | bytes 8388608 | tf_op jit(solution)/shard_map/attend_back/pallas_call | solution.py:821
  93.7 5.3 %project_back.1 = (bf16[1024,512]{1,0:T(8,128)(2,1)}, f32[16,272,128]{2,1,0:T(8,128)S(1)}, bf16[16,272,128]{2,1,0:T(8,128)(2,1)S(1)}) custom-call(bf16[1024,1536]{1,0:T(8,128)(2,1)S(1)} %get-tuple-element.122.grads, bf16[1024,512]{1,0:T(8,128)(2,1)S(1)} %get-tuple-element.123.mixed_ref, f32[1024,512]{1,0:T(8,128)S(1)} %get-tuple-element.124.grad_first_ref, ...), custom_call_target="tpu_custom_call" | custom-call | flops 6291456000 | bytes 8388608 | tf_op jit(solution)/shard_map/project_back/pallas_call | solution.py:835
  99.0 2.4 %collective-permute-done.15 = bf16[4,256,128]{2,1,0:T(8,128)(2,1)S(1)} collective-permute-done((bf16[4,256,128]{2,1,0:T(8,128)(2,1)S(1)}, bf16[4,256,128]{2,1,0:T(8,128)(2,1)S(1)}, u32[]{:S(2)}, u32[]{:S(2)}) %collective-permute-start.15) | collective-permute-done | bytes 262176 | tf_op jit(solution)/shard_map/ppermute | solution.py:906
  102.1 1.5 %collective-permute-done.18 = bf16[8,5,64,128]{3,2,1,0:T(8,128)(2,1)S(1)} collective-permute-done((bf16[8,5,64,128]{3,2,1,0:T(8,128)(2,1)S(1)}, bf16[8,5,64,128]{3,2,1,0:T(8,128)(2,1)S(1)}, u32[]{:S(2)}, u32[]{:S(2)}) %collective-permute-start.18) | collective-permute-done | bytes 655392 | tf_op jit(solution)/shard_map/ppermute | solution.py:906
  108.3 7.3 %collective-permute-done.21 = bf16[2,256,128]{2,1,0:T(8,128)(2,1)S(1)} collective-permute-done((bf16[2,256,128]{2,1,0:T(8,128)(2,1)S(1)}, bf16[2,256,128]{2,1,0:T(8,128)(2,1)S(1)}, u32[]{:S(2)}, u32[]{:S(2)}) %collective-permute-start.21) | collective-permute-done | bytes 131104 | tf_op jit(solution)/shard_map/ppermute | solution.py:906
  115.6 1.9 %collective-permute-start.23 = (bf16[2,5,64,128]{3,2,1,0:T(8,128)(2,1)S(1)}, bf16[2,5,64,128]{3,2,1,0:T(8,128)(2,1)S(1)}, u32[]{:S(2)}, u32[]{:S(2)}) collective-permute-start(bf16[2,5,64,128]{3,2,1,0:T(8,128)(2,1)S(1)} %get-tuple-element.168), channel_id=1, source_target_pairs={{0,16},{1,9},{2,18},{3,11},{4,20},{5,13},{6,22},{7,15},{8,24},{9,1... | collective-permute-start | bytes 491528 | tf_op jit(solution)/shard_map/ppermute | solution.py:906
  119.5 5.6 %collective-permute-done.24.back_came_ref = bf16[1,256,128]{2,1,0:T(8,128)(2,1)S(1)} collective-permute-done((bf16[1,256,128]{2,1,0:T(8,128)(2,1)S(1)}, bf16[1,256,128]{2,1,0:T(8,128)(2,1)S(1)}, u32[]{:S(2)}, u32[]{:S(2)}) %collective-permute-start.24) | collective-permute-done | bytes 65568 | tf_op jit(solution)/shard_map/ppermute | solution.py:906
  125.9 2.1 %collective-permute-start.27 = (bf16[1,272,128]{2,1,0:T(8,128)(2,1)S(1)}, bf16[1,272,128]{2,1,0:T(8,128)(2,1)S(1)}, u32[]{:S(2)}, u32[]{:S(2)}) collective-permute-start(bf16[1,272,128]{2,1,0:T(8,128)(2,1)S(1)} %get-tuple-element.169), channel_id=1, source_target_pairs={{0,24},{1,25},{2,26},{3,27},{4,28},{5,29},{6,30},{7,31},{8,16},{9,... | collective-permute-start | bytes 208904 | tf_op jit(solution)/shard_map/ppermute | solution.py:936
  128.0 2.4 %collective-permute-start.25 = (bf16[1,272,128]{2,1,0:T(8,128)(2,1)S(1)}, bf16[1,272,128]{2,1,0:T(8,128)(2,1)S(1)}, u32[]{:S(2)}, u32[]{:S(2)}) collective-permute-start(bf16[1,272,128]{2,1,0:T(8,128)(2,1)S(1)} %get-tuple-element.171), channel_id=1, source_target_pairs={{0,16},{1,9},{2,18},{3,11},{4,20},{5,13},{6,22},{7,15},{8,24},{9,1... | collective-permute-start | bytes 208904 | tf_op jit(solution)/shard_map/ppermute | solution.py:936
  130.3 1.8 %collective-permute-done.27.outer_third_ref = bf16[1,272,128]{2,1,0:T(8,128)(2,1)S(1)} collective-permute-done((bf16[1,272,128]{2,1,0:T(8,128)(2,1)S(1)}, bf16[1,272,128]{2,1,0:T(8,128)(2,1)S(1)}, u32[]{:S(2)}, u32[]{:S(2)}) %collective-permute-start.27) | collective-permute-done | bytes 69664 | tf_op jit(solution)/shard_map/ppermute | solution.py:936
  (65 shorter events, 18.4 us)
Async XLA Ops:
  1.7 8.4 %collective-permute-start.1 = (bf16[1,9,64,128]{3,2,1,0:T(8,128)(2,1)S(1)}, bf16[1,9,64,128]{3,2,1,0:T(8,128)(2,1)S(1)}, u32[]{:S(2)}, u32[]{:S(2)}) collective-permute-start(bf16[1,9,64,128]{3,2,1,0:T(8,128)(2,1)S(1)} %bitcast.8), channel_id=1, source_target_pairs={{0,16},{1,9},{2,18},{3,11},{4,20},{5,13},{6,22},{7,15},{8,24},{9,1... | collective-permute-start | bytes 442376 | tf_op jit(solution)/shard_map/ppermute | solution.py:906
  10.1 9.8 %collective-permute-start.3 = (bf16[2,9,64,128]{3,2,1,0:T(8,128)(2,1)S(1)}, bf16[2,9,64,128]{3,2,1,0:T(8,128)(2,1)S(1)}, u32[]{:S(2)}, u32[]{:S(2)}) collective-permute-start(bf16[2,9,64,128]{3,2,1,0:T(8,128)(2,1)S(1)} %join.6.first_ref), channel_id=1, source_target_pairs={{0,8},{1,17},{2,10},{3,19},{4,12},{5,21},{6,14},{7,23},{8,0},{9,25... | collective-permute-start | bytes 884744 | tf_op jit(solution)/shard_map/ppermute | solution.py:906
  20.0 12.1 %collective-permute-start.5 = (bf16[4,9,64,128]{3,2,1,0:T(8,128)(2,1)S(1)}, bf16[4,9,64,128]{3,2,1,0:T(8,128)(2,1)S(1)}, u32[]{:S(2)}, u32[]{:S(2)}) collective-permute-start(bf16[4,9,64,128]{3,2,1,0:T(8,128)(2,1)S(1)} %join.8.first_ref), channel_id=1, source_target_pairs={{0,4},{1,3},{2,6},{3,1},{4,0},{5,7},{6,2},{7,5},{8,12},{9,11},{10,... | collective-permute-start | bytes 1769480 | tf_op jit(solution)/shard_map/ppermute | solution.py:906
  21.6 10.5 %collective-permute-start.4 = (bf16[4,272,128]{2,1,0:T(8,128)(2,1)S(1)}, bf16[4,272,128]{2,1,0:T(8,128)(2,1)S(1)}, u32[]{:S(2)}, u32[]{:S(2)}) collective-permute-start(bf16[4,272,128]{2,1,0:T(8,128)(2,1)S(1)} %join.9.first_ref), channel_id=1, source_target_pairs={{0,16},{1,9},{2,18},{3,11},{4,20},{5,13},{6,22},{7,15},{8,24},{9,1... | collective-permute-start | bytes 835592 | tf_op jit(solution)/shard_map/ppermute | solution.py:906
  32.2 17.1 %collective-permute-start.7 = (bf16[8,9,64,128]{3,2,1,0:T(8,128)(2,1)S(1)}, bf16[8,9,64,128]{3,2,1,0:T(8,128)(2,1)S(1)}, u32[]{:S(2)}, u32[]{:S(2)}) collective-permute-start(bf16[8,9,64,128]{3,2,1,0:T(8,128)(2,1)S(1)} %join.10.p0_ref), channel_id=1, source_target_pairs={{0,2},{1,5},{2,0},{3,7},{4,6},{5,1},{6,4},{7,3},{8,10},{9,13},{10,... | collective-permute-start | bytes 3538952 | tf_op jit(solution)/shard_map/ppermute | solution.py:906
  33.8 15.5 %collective-permute-start.6 = (bf16[8,272,128]{2,1,0:T(8,128)(2,1)S(1)}, bf16[8,272,128]{2,1,0:T(8,128)(2,1)S(1)}, u32[]{:S(2)}, u32[]{:S(2)}) collective-permute-start(bf16[8,272,128]{2,1,0:T(8,128)(2,1)S(1)} %join.11.p0_ref), channel_id=1, source_target_pairs={{0,8},{1,17},{2,10},{3,19},{4,12},{5,21},{6,14},{7,23},{8,0},{9,25... | collective-permute-start | bytes 1671176 | tf_op jit(solution)/shard_map/ppermute | solution.py:906
  33.9 15.9 %collective-permute-start.10 = (bf16[8,272,128]{2,1,0:T(8,128)(2,1)S(1)}, bf16[8,272,128]{2,1,0:T(8,128)(2,1)S(1)}, u32[]{:S(2)}, u32[]{:S(2)}) collective-permute-start(bf16[8,272,128]{2,1,0:T(8,128)(2,1)S(1)} %join.11.p0_ref), channel_id=1, source_target_pairs={{0,1},{1,0},{2,3},{3,2},{4,5},{5,4},{6,7},{7,6},{8,9},{9,8},{10,11... | collective-permute-start | bytes 1671176 | tf_op jit(solution)/shard_map/ppermute | solution.py:906
  49.3 9.8 %collective-permute-start.8 = (bf16[8,9,64,128]{3,2,1,0:T(8,128)(2,1)S(1)}, bf16[8,9,64,128]{3,2,1,0:T(8,128)(2,1)S(1)}, u32[]{:S(2)}, u32[]{:S(2)}) collective-permute-start(bf16[8,9,64,128]{3,2,1,0:T(8,128)(2,1)S(1)} %join.10.p0_ref), channel_id=1, source_target_pairs={{0,1},{1,0},{2,3},{3,2},{4,5},{5,4},{6,7},{7,6},{8,9},{9,8},{10,11... | collective-permute-start | bytes 3538952 | tf_op jit(solution)/shard_map/ppermute | solution.py:906
  49.8 9.3 %collective-permute-start.9 = (bf16[8,9,64,128]{3,2,1,0:T(8,128)(2,1)S(1)}, bf16[8,9,64,128]{3,2,1,0:T(8,128)(2,1)S(1)}, u32[]{:S(2)}, u32[]{:S(2)}) collective-permute-start(bf16[8,9,64,128]{3,2,1,0:T(8,128)(2,1)S(1)} %collective-permute-done.7.p1_ref), channel_id=1, source_target_pairs={{0,1},{1,0},{2,3},{3,2},{4,5},{5,4},{6,7},{7,6},{8,9},{9,8},{10,11... | collective-permute-start | bytes 3538952 | tf_op jit(solution)/shard_map/ppermute | solution.py:906
  72.2 10.6 %collective-permute-start.12 = (bf16[16,256,128]{2,1,0:T(8,128)(2,1)S(1)}, bf16[16,256,128]{2,1,0:T(8,128)(2,1)S(1)}, u32[]{:S(2)}, u32[]{:S(2)}) collective-permute-start(bf16[16,256,128]{2,1,0:T(8,128)(2,1)S(1)} %get-tuple-element.113), channel_id=1, source_target_pairs={{0,1},{1,0},{2,3},{3,2},{4,5},{5,4},{6,7},{7,6},{8,9},{9,8},{10,11... | collective-permute-start | bytes 3145736 | tf_op jit(solution)/shard_map/ppermute | solution.py:906
  82.4 9.3 %collective-permute-start.14 = (bf16[16,5,64,128]{3,2,1,0:T(8,128)(2,1)S(1)}, bf16[16,5,64,128]{3,2,1,0:T(8,128)(2,1)S(1)}, u32[]{:S(2)}, u32[]{:S(2)}) collective-permute-start(bf16[16,5,64,128]{3,2,1,0:T(8,128)(2,1)S(1)} %get-tuple-element.117), channel_id=1, source_target_pairs={{0,1},{1,0},{2,3},{3,2},{4,5},{5,4},{6,7},{7,6},{8,9},{9,8},{10,11... | collective-permute-start | bytes 3932168 | tf_op jit(solution)/shard_map/ppermute | solution.py:906
  83.0 9.2 %collective-permute-start.13 = (bf16[8,256,128]{2,1,0:T(8,128)(2,1)S(1)}, bf16[8,256,128]{2,1,0:T(8,128)(2,1)S(1)}, u32[]{:S(2)}, u32[]{:S(2)}) collective-permute-start(bf16[8,256,128]{2,1,0:T(8,128)(2,1)S(1)} %get-tuple-element.155), channel_id=1, source_target_pairs={{0,4},{1,9},{2,6},{3,11},{4,0},{5,13},{6,2},{7,15},{8,12},{9,1},{1... | collective-permute-start | bytes 1572872 | tf_op jit(solution)/shard_map/ppermute | solution.py:906
  92.9 8.5 %collective-permute-start.15 = (bf16[4,256,128]{2,1,0:T(8,128)(2,1)S(1)}, bf16[4,256,128]{2,1,0:T(8,128)(2,1)S(1)}, u32[]{:S(2)}, u32[]{:S(2)}) collective-permute-start(bf16[4,256,128]{2,1,0:T(8,128)(2,1)S(1)} %get-tuple-element.163), channel_id=1, source_target_pairs={{0,8},{1,17},{2,10},{3,19},{4,12},{5,21},{6,14},{7,23},{8,0},{9,25... | collective-permute-start | bytes 786440 | tf_op jit(solution)/shard_map/ppermute | solution.py:906
  93.0 10.7 %collective-permute-start.18 = (bf16[8,5,64,128]{3,2,1,0:T(8,128)(2,1)S(1)}, bf16[8,5,64,128]{3,2,1,0:T(8,128)(2,1)S(1)}, u32[]{:S(2)}, u32[]{:S(2)}) collective-permute-start(bf16[8,5,64,128]{3,2,1,0:T(8,128)(2,1)S(1)} %get-tuple-element.153), channel_id=1, source_target_pairs={{0,2},{1,5},{2,0},{3,7},{4,6},{5,1},{6,4},{7,3},{8,10},{9,13},{10,... | collective-permute-start | bytes 1966088 | tf_op jit(solution)/shard_map/ppermute | solution.py:906
  104.5 11.0 %collective-permute-start.19 = (bf16[8,272,128]{2,1,0:T(8,128)(2,1)S(1)}, bf16[8,272,128]{2,1,0:T(8,128)(2,1)S(1)}, u32[]{:S(2)}, u32[]{:S(2)}) collective-permute-start(bf16[8,272,128]{2,1,0:T(8,128)(2,1)S(1)} %get-tuple-element.157), channel_id=1, source_target_pairs={{0,2},{1,5},{2,0},{3,7},{4,6},{5,1},{6,4},{7,3},{8,10},{9,13},{10,... | collective-permute-start | bytes 1671176 | tf_op jit(solution)/shard_map/ppermute | solution.py:906
  105.5 10.0 %collective-permute-start.20 = (bf16[4,5,64,128]{3,2,1,0:T(8,128)(2,1)S(1)}, bf16[4,5,64,128]{3,2,1,0:T(8,128)(2,1)S(1)}, u32[]{:S(2)}, u32[]{:S(2)}) collective-permute-start(bf16[4,5,64,128]{3,2,1,0:T(8,128)(2,1)S(1)} %get-tuple-element.160), channel_id=1, source_target_pairs={{0,8},{1,17},{2,10},{3,19},{4,12},{5,21},{6,14},{7,23},{8,0},{9,25... | collective-permute-start | bytes 983048 | tf_op jit(solution)/shard_map/ppermute | solution.py:906
  106.9 8.6 %collective-permute-start.21 = (bf16[2,256,128]{2,1,0:T(8,128)(2,1)S(1)}, bf16[2,256,128]{2,1,0:T(8,128)(2,1)S(1)}, u32[]{:S(2)}, u32[]{:S(2)}) collective-permute-start(bf16[2,256,128]{2,1,0:T(8,128)(2,1)S(1)} %get-tuple-element.174), channel_id=1, source_target_pairs={{0,2},{1,5},{2,0},{3,7},{4,6},{5,1},{6,4},{7,3},{8,10},{9,13},{10,... | collective-permute-start | bytes 393224 | tf_op jit(solution)/shard_map/ppermute | solution.py:906
  115.6 9.4 %collective-permute-start.23 = (bf16[2,5,64,128]{3,2,1,0:T(8,128)(2,1)S(1)}, bf16[2,5,64,128]{3,2,1,0:T(8,128)(2,1)S(1)}, u32[]{:S(2)}, u32[]{:S(2)}) collective-permute-start(bf16[2,5,64,128]{3,2,1,0:T(8,128)(2,1)S(1)} %get-tuple-element.168), channel_id=1, source_target_pairs={{0,16},{1,9},{2,18},{3,11},{4,20},{5,13},{6,22},{7,15},{8,24},{9,1... | collective-permute-start | bytes 491528 | tf_op jit(solution)/shard_map/ppermute | solution.py:906
  117.6 7.5 %collective-permute-start.22 = (bf16[4,272,128]{2,1,0:T(8,128)(2,1)S(1)}, bf16[4,272,128]{2,1,0:T(8,128)(2,1)S(1)}, u32[]{:S(2)}, u32[]{:S(2)}) collective-permute-start(bf16[4,272,128]{2,1,0:T(8,128)(2,1)S(1)} %get-tuple-element.161), channel_id=1, source_target_pairs={{0,4},{1,3},{2,6},{3,1},{4,0},{5,7},{6,2},{7,5},{8,12},{9,11},{10,... | collective-permute-start | bytes 835592 | tf_op jit(solution)/shard_map/ppermute | solution.py:906
  118.6 6.4 %collective-permute-start.24 = (bf16[1,256,128]{2,1,0:T(8,128)(2,1)S(1)}, bf16[1,256,128]{2,1,0:T(8,128)(2,1)S(1)}, u32[]{:S(2)}, u32[]{:S(2)}) collective-permute-start(bf16[1,256,128]{2,1,0:T(8,128)(2,1)S(1)} %get-tuple-element.178), channel_id=1, source_target_pairs={{0,16},{1,3},{2,18},{3,1},{4,20},{5,7},{6,22},{7,5},{8,24},{9,11},... | collective-permute-start | bytes 196616 | tf_op jit(solution)/shard_map/ppermute | solution.py:906
  125.1 8.4 %collective-permute-start.28 = (bf16[1,5,64,128]{3,2,1,0:T(8,128)(2,1)S(1)}, bf16[1,5,64,128]{3,2,1,0:T(8,128)(2,1)S(1)}, u32[]{:S(2)}, u32[]{:S(2)}) collective-permute-start(bf16[1,5,64,128]{3,2,1,0:T(8,128)(2,1)S(1)} %get-tuple-element.175), channel_id=1, source_target_pairs={{0,4},{1,3},{2,6},{3,1},{4,0},{5,7},{6,2},{7,5},{8,12},{9,11},{10,... | collective-permute-start | bytes 245768 | tf_op jit(solution)/shard_map/ppermute | solution.py:906
  125.9 6.2 %collective-permute-start.27 = (bf16[1,272,128]{2,1,0:T(8,128)(2,1)S(1)}, bf16[1,272,128]{2,1,0:T(8,128)(2,1)S(1)}, u32[]{:S(2)}, u32[]{:S(2)}) collective-permute-start(bf16[1,272,128]{2,1,0:T(8,128)(2,1)S(1)} %get-tuple-element.169), channel_id=1, source_target_pairs={{0,24},{1,25},{2,26},{3,27},{4,28},{5,29},{6,30},{7,31},{8,16},{9,... | collective-permute-start | bytes 208904 | tf_op jit(solution)/shard_map/ppermute | solution.py:936
  128.0 5.6 %collective-permute-start.26 = (bf16[1,272,128]{2,1,0:T(8,128)(2,1)S(1)}, bf16[1,272,128]{2,1,0:T(8,128)(2,1)S(1)}, u32[]{:S(2)}, u32[]{:S(2)}) collective-permute-start(bf16[1,272,128]{2,1,0:T(8,128)(2,1)S(1)} %get-tuple-element.170), channel_id=1, source_target_pairs={{0,8},{1,17},{2,10},{3,19},{4,12},{5,21},{6,14},{7,23},{8,0},{9,25... | collective-permute-start | bytes 208904 | tf_op jit(solution)/shard_map/ppermute | solution.py:936
  128.0 5.6 %collective-permute-start.25 = (bf16[1,272,128]{2,1,0:T(8,128)(2,1)S(1)}, bf16[1,272,128]{2,1,0:T(8,128)(2,1)S(1)}, u32[]{:S(2)}, u32[]{:S(2)}) collective-permute-start(bf16[1,272,128]{2,1,0:T(8,128)(2,1)S(1)} %get-tuple-element.171), channel_id=1, source_target_pairs={{0,16},{1,9},{2,18},{3,11},{4,20},{5,13},{6,22},{7,15},{8,24},{9,1... | collective-permute-start | bytes 208904 | tf_op jit(solution)/shard_map/ppermute | solution.py:936
  (8 other events, 84.9 us)

commit v6 on v5

--- a/solution.py
+++ b/solution.py
@@ -1029,10 +1029,10 @@
     back = halve(back[0], back_came, ORDER_BACK, 1)
     upper_came, inner_came = lax.optimization_barrier((upper_came, inner[1]))
     upper = (keep[8:] + upper_came.astype(F32)).astype(BF16)
-    outer = keep[:8] + lower_came.astype(F32), swap(upper, ORDER_OUTER, 3)
+    far = swap(upper, ORDER_OUTER, 3)
     inner = halve(inner[0], inner_came, ORDER_INNER, 2)
-    came = lax.optimization_barrier((outer[1], inner[1], back[1]))
-    outer = halve(outer[0], came[0], ORDER_OUTER, 2)
+    came = lax.optimization_barrier((far, inner[1], back[1], lower_came))
+    outer = halve(keep[:8] + came[3].astype(F32), came[0], ORDER_OUTER, 2)
     inner = halve(inner[0], came[1], ORDER_INNER, 1)
     back = halve(back[0], came[2], ORDER_BACK, 0)
     came = lax.optimization_barrier((outer[1], inner[1], back[1]))

time: 135 us -> 134 us (level)
  waiting for transfers between devices: 56.9 us -> 55.2 us
    ppermute x26, waiting for transfers between devices: 53.7 us -> 52 us  [swap(): return lax.ppermute(array, AXES, pairs(order, step))]
  transfers between devices with their start and end apart: 29 -> 29, of which waited for: 14 -> 13; matrix products, arithmetic and copies ran while one was open for 1% -> 1% of each run, Pallas kernels for 23% -> 23%
where the time goes in v6:
time: 134 us
  waiting for transfers between devices  55.2 us (41%)
  Pallas kernels  46.3 us (35%)
  starting transfers between devices  29.9 us (22%)
  other arithmetic  1.67 us (1%)
    ppermute x26, waiting for transfers between devices, swap(): return lax.ppermute(array, AXES, pairs(order, step))  52 us
    ppermute x26, starting transfers between devices, swap(): return lax.ppermute(array, AXES, pairs(order, step))  25.5 us
    pallas_call x1, Pallas kernels, forward_call(): pl.pallas_call(partial(forward_kernel, direct), out_shape=(shape((total,...  13 us
    pallas_call x1, Pallas kernels, backward_call(): pl.pallas_call(partial(backward_kernel, direct), out_shape=(shape((total,...  10 us
    pallas_call x1, Pallas kernels, attend_back_call(): pl.pallas_call(partial(attend_back_kernel, direct), out_shape=(shape((tot...  8.04 us
    pallas_call x1, Pallas kernels, attend_call(): pl.pallas_call(partial(attend_kernel, direct), out_shape=(near((total, 15...  7.83 us
    pallas_call x1, Pallas kernels, project_back_call(): pl.pallas_call(partial(project_back_kernel, direct, windows), out_shape=(...  5.29 us
    ppermute x3, starting transfers between devices, scatter_rest(): others.append(lax.ppermute(total, AXES, partners))  4.45 us
  transfers between devices with their start and end apart: 29, of which 13 were waited for; matrix products, arithmetic and copies ran while one was open for 1% of the time, Pallas kernels for 23%

profile of v6, /device:TPU:0, one launch (start us, length us, event | category | flops | bytes accessed | tf_op | source)
XLA Modules:
  0.0 134.1 jit_solution(15266225120443808028)
XLA Ops:
  1.7 4.1 %collective-permute-start.1 = (bf16[1,9,64,128]{3,2,1,0:T(8,128)(2,1)S(1)}, bf16[1,9,64,128]{3,2,1,0:T(8,128)(2,1)S(1)}, u32[]{:S(2)}, u32[]{:S(2)}) collective-permute-start(bf16[1,9,64,128]{3,2,1,0:T(8,128)(2,1)S(1)} %bitcast.8), channel_id=1, source_target_pairs={{0,16},{1,9},{2,18},{3,11},{4,20},{5,13},{6,22},{7,15},{8,24},{9,1... | collective-permute-start | bytes 442376 | tf_op jit(solution)/shard_map/ppermute | solution.py:906
  7.3 2.8 %collective-permute-done.second_ref = bf16[1,272,128]{2,1,0:T(8,128)(2,1)S(1)} collective-permute-done((bf16[1,272,128]{2,1,0:T(8,128)(2,1)S(1)}, bf16[1,272,128]{2,1,0:T(8,128)(2,1)S(1)}, u32[]{:S(2)}, u32[]{:S(2)}) %collective-permute-start) | collective-permute-done | bytes 69664 | tf_op jit(solution)/shard_map/ppermute | solution.py:906
  10.1 1.6 %collective-permute-start.3 = (bf16[2,9,64,128]{3,2,1,0:T(8,128)(2,1)S(1)}, bf16[2,9,64,128]{3,2,1,0:T(8,128)(2,1)S(1)}, u32[]{:S(2)}, u32[]{:S(2)}) collective-permute-start(bf16[2,9,64,128]{3,2,1,0:T(8,128)(2,1)S(1)} %join.6.first_ref), channel_id=1, source_target_pairs={{0,8},{1,17},{2,10},{3,19},{4,12},{5,21},{6,14},{7,23},{8,0},{9,25... | collective-permute-start | bytes 884744 | tf_op jit(solution)/shard_map/ppermute | solution.py:906
  11.8 1.6 %collective-permute-start.2 = (bf16[2,272,128]{2,1,0:T(8,128)(2,1)S(1)}, bf16[2,272,128]{2,1,0:T(8,128)(2,1)S(1)}, u32[]{:S(2)}, u32[]{:S(2)}) collective-permute-start(bf16[2,272,128]{2,1,0:T(8,128)(2,1)S(1)} %join.7.first_ref), channel_id=1, source_target_pairs={{0,2},{1,3},{2,0},{3,1},{4,6},{5,7},{6,4},{7,5},{8,10},{9,11},{10,... | collective-permute-start | bytes 417800 | tf_op jit(solution)/shard_map/ppermute | solution.py:906
  13.3 3.5 %collective-permute-done.2.second_ref = bf16[2,272,128]{2,1,0:T(8,128)(2,1)S(1)} collective-permute-done((bf16[2,272,128]{2,1,0:T(8,128)(2,1)S(1)}, bf16[2,272,128]{2,1,0:T(8,128)(2,1)S(1)}, u32[]{:S(2)}, u32[]{:S(2)}) %collective-permute-start.2) | collective-permute-done | bytes 139296 | tf_op jit(solution)/shard_map/ppermute | solution.py:906
  16.9 3.1 %collective-permute-done.3.second_ref = bf16[2,9,64,128]{3,2,1,0:T(8,128)(2,1)S(1)} collective-permute-done((bf16[2,9,64,128]{3,2,1,0:T(8,128)(2,1)S(1)}, bf16[2,9,64,128]{3,2,1,0:T(8,128)(2,1)S(1)}, u32[]{:S(2)}, u32[]{:S(2)}) %collective-permute-start.3) | collective-permute-done | bytes 294944 | tf_op jit(solution)/shard_map/ppermute | solution.py:906
  20.0 1.6 %collective-permute-start.5 = (bf16[4,9,64,128]{3,2,1,0:T(8,128)(2,1)S(1)}, bf16[4,9,64,128]{3,2,1,0:T(8,128)(2,1)S(1)}, u32[]{:S(2)}, u32[]{:S(2)}) collective-permute-start(bf16[4,9,64,128]{3,2,1,0:T(8,128)(2,1)S(1)} %join.8.first_ref), channel_id=1, source_target_pairs={{0,4},{1,3},{2,6},{3,1},{4,0},{5,7},{6,2},{7,5},{8,12},{9,11},{10,... | collective-permute-start | bytes 1769480 | tf_op jit(solution)/shard_map/ppermute | solution.py:906
  22.7 9.4 %collective-permute-done.4.second_ref = bf16[4,272,128]{2,1,0:T(8,128)(2,1)S(1)} collective-permute-done((bf16[4,272,128]{2,1,0:T(8,128)(2,1)S(1)}, bf16[4,272,128]{2,1,0:T(8,128)(2,1)S(1)}, u32[]{:S(2)}, u32[]{:S(2)}) %collective-permute-start.4) | collective-permute-done | bytes 278560 | tf_op jit(solution)/shard_map/ppermute | solution.py:906
  32.2 1.6 %collective-permute-start.7 = (bf16[8,9,64,128]{3,2,1,0:T(8,128)(2,1)S(1)}, bf16[8,9,64,128]{3,2,1,0:T(8,128)(2,1)S(1)}, u32[]{:S(2)}, u32[]{:S(2)}) collective-permute-start(bf16[8,9,64,128]{3,2,1,0:T(8,128)(2,1)S(1)} %join.10.p0_ref), channel_id=1, source_target_pairs={{0,2},{1,5},{2,0},{3,7},{4,6},{5,1},{6,4},{7,3},{8,10},{9,13},{10,... | collective-permute-start | bytes 3538952 | tf_op jit(solution)/shard_map/ppermute | solution.py:906
  34.0 15.3 %collective-permute-done.6.p1_ref = bf16[8,272,128]{2,1,0:T(8,128)(2,1)S(1)} collective-permute-done((bf16[8,272,128]{2,1,0:T(8,128)(2,1)S(1)}, bf16[8,272,128]{2,1,0:T(8,128)(2,1)S(1)}, u32[]{:S(2)}, u32[]{:S(2)}) %collective-permute-start.6) | collective-permute-done | bytes 557088 | tf_op jit(solution)/shard_map/ppermute | solution.py:906
  51.2 7.8 %attend.1 = (bf16[1024,1536]{1,0:T(8,128)(2,1)S(1)}, bf16[1024,512]{1,0:T(8,128)(2,1)S(1)}, f32[4,2,4,256]{3,2,1,0:T(4,128)S(1)}, f32[1024,512]{1,0:T(8,128)S(1)...) custom-call(s32[2,512]{1,0:T(2,128)S(1)} %copy-done.2, ...), custom_call_target="tpu_custom_call" | custom-call | flops 12582912000 | bytes 12582912 | tf_op jit(solution)/shard_map/attend/pallas_call | solution.py:719
  59.1 13.0 %forward.1 = (bf16[1024,512]{1,0:T(8,128)(2,1)}, f32[1024,2048]{1,0:T(8,128)S(1)}, f32[1024,512]{1,0:T(8,128)S(1)}, f32[1024,512]{1,0:T(8,128)S(1)}, bf16[8,64,1...) custom-call(bf16[1024,512]{1,0:T(8,128)(2,1)S(1)} %get-tuple-element, ...), custom_call_target="tpu_custom_call", output_to_operand_aliasing={{3}: (1, {})} | custom-call | flops 12582912000 | bytes 25165824 | tf_op jit(solution)/shard_map/forward/pallas_call | solution.py:755
  72.4 10.0 %backward.1 = (f32[1024,512]{1,0:T(8,128)S(1)}, bf16[1024,512]{1,0:T(8,128)(2,1)S(1)}, f32[16,5,64,128]{3,2,1,0:T(8,128)S(1)}, bf16[16,5,64,128]{3,2,1,0:T(8,128...) custom-call(f32[1024,2048]{1,0:T(8,128)S(1)} %get-tuple-element.105.slop, ...), custom_call_target="tpu_custom_call", output_to_operand_aliasing={{0}: (1, {}), {1}: (4, {})} | custom-call | flops 14680064000 | bytes 25165824 | tf_op jit(solution)/shard_map/backward/pallas_call | solution.py:786
  83.6 8.0 %attend_back.1 = (bf16[1024,1536]{1,0:T(8,128)(2,1)S(1)}, f32[4,8,128]{2,1,0:T(8,128)S(1)}) custom-call(s32[2,512]{1,0:T(2,128)S(1)} %copy-done.2, bf16[1024,1536]{1,0:T(8,128)(2,1)S(1)} %get-tuple-element.104.qkv_ref, bf16[1024,512]{1,0:T(8,128)(2,1)S(1)} %get-tuple-element.115.grad_attended_ref, f32[4,2,4,256]{3,2,1,0:T(4,128)S(1)} %get-tuple-element.116.lse_ref), custom_call_target="tpu_custom_call" | custom-call | flops 8388608000 | bytes 8388608 | tf_op jit(solution)/shard_map/attend_back/pallas_call | solution.py:821
  93.7 5.3 %project_back.1 = (bf16[1024,512]{1,0:T(8,128)(2,1)}, f32[16,272,128]{2,1,0:T(8,128)S(1)}, bf16[16,272,128]{2,1,0:T(8,128)(2,1)S(1)}) custom-call(bf16[1024,1536]{1,0:T(8,128)(2,1)S(1)} %get-tuple-element.123.grads, bf16[1024,512]{1,0:T(8,128)(2,1)S(1)} %get-tuple-element.124.mixed_ref, f32[1024,512]{1,0:T(8,128)S(1)} %get-tuple-element.125.grad_first_ref, ...), custom_call_target="tpu_custom_call" | custom-call | flops 6291456000 | bytes 8388608 | tf_op jit(solution)/shard_map/project_back/pallas_call | solution.py:835
  99.0 2.4 %collective-permute-done.15 = bf16[4,256,128]{2,1,0:T(8,128)(2,1)S(1)} collective-permute-done((bf16[4,256,128]{2,1,0:T(8,128)(2,1)S(1)}, bf16[4,256,128]{2,1,0:T(8,128)(2,1)S(1)}, u32[]{:S(2)}, u32[]{:S(2)}) %collective-permute-start.15) | collective-permute-done | bytes 262176 | tf_op jit(solution)/shard_map/ppermute | solution.py:906
  102.1 1.5 %collective-permute-done.17 = bf16[8,5,64,128]{3,2,1,0:T(8,128)(2,1)S(1)} collective-permute-done((bf16[8,5,64,128]{3,2,1,0:T(8,128)(2,1)S(1)}, bf16[8,5,64,128]{3,2,1,0:T(8,128)(2,1)S(1)}, u32[]{:S(2)}, u32[]{:S(2)}) %collective-permute-start.17) | collective-permute-done | bytes 655392 | tf_op jit(solution)/shard_map/ppermute | solution.py:906
  104.7 2.0 %collective-permute-start.19 = (bf16[4,5,64,128]{3,2,1,0:T(8,128)(2,1)S(1)}, bf16[4,5,64,128]{3,2,1,0:T(8,128)(2,1)S(1)}, u32[]{:S(2)}, u32[]{:S(2)}) collective-permute-start(bf16[4,5,64,128]{3,2,1,0:T(8,128)(2,1)S(1)} %get-tuple-element.160), channel_id=1, source_target_pairs={{0,8},{1,17},{2,10},{3,19},{4,12},{5,21},{6,14},{7,23},{8,0},{9,25... | collective-permute-start | bytes 983048 | tf_op jit(solution)/shard_map/ppermute | solution.py:906
  108.2 6.6 %collective-permute-done.20 = bf16[2,256,128]{2,1,0:T(8,128)(2,1)S(1)} collective-permute-done((bf16[2,256,128]{2,1,0:T(8,128)(2,1)S(1)}, bf16[2,256,128]{2,1,0:T(8,128)(2,1)S(1)}, u32[]{:S(2)}, u32[]{:S(2)}) %collective-permute-start.20) | collective-permute-done | bytes 131104 | tf_op jit(solution)/shard_map/ppermute | solution.py:906
  115.0 2.6 %collective-permute-start.23 = (bf16[2,5,64,128]{3,2,1,0:T(8,128)(2,1)S(1)}, bf16[2,5,64,128]{3,2,1,0:T(8,128)(2,1)S(1)}, u32[]{:S(2)}, u32[]{:S(2)}) collective-permute-start(bf16[2,5,64,128]{3,2,1,0:T(8,128)(2,1)S(1)} %get-tuple-element.168), channel_id=1, source_target_pairs={{0,16},{1,9},{2,18},{3,11},{4,20},{5,13},{6,22},{7,15},{8,24},{9,1... | collective-permute-start | bytes 491528 | tf_op jit(solution)/shard_map/ppermute | solution.py:906
  119.1 5.3 %collective-permute-done.24.back_came_ref = bf16[1,256,128]{2,1,0:T(8,128)(2,1)S(1)} collective-permute-done((bf16[1,256,128]{2,1,0:T(8,128)(2,1)S(1)}, bf16[1,256,128]{2,1,0:T(8,128)(2,1)S(1)}, u32[]{:S(2)}, u32[]{:S(2)}) %collective-permute-start.24) | collective-permute-done | bytes 65568 | tf_op jit(solution)/shard_map/ppermute | solution.py:906
  125.6 2.1 %collective-permute-start.27 = (bf16[1,272,128]{2,1,0:T(8,128)(2,1)S(1)}, bf16[1,272,128]{2,1,0:T(8,128)(2,1)S(1)}, u32[]{:S(2)}, u32[]{:S(2)}) collective-permute-start(bf16[1,272,128]{2,1,0:T(8,128)(2,1)S(1)} %get-tuple-element.169), channel_id=1, source_target_pairs={{0,24},{1,25},{2,26},{3,27},{4,28},{5,29},{6,30},{7,31},{8,16},{9,... | collective-permute-start | bytes 208904 | tf_op jit(solution)/shard_map/ppermute | solution.py:936
  127.6 2.4 %collective-permute-start.25 = (bf16[1,272,128]{2,1,0:T(8,128)(2,1)S(1)}, bf16[1,272,128]{2,1,0:T(8,128)(2,1)S(1)}, u32[]{:S(2)}, u32[]{:S(2)}) collective-permute-start(bf16[1,272,128]{2,1,0:T(8,128)(2,1)S(1)} %get-tuple-element.171), channel_id=1, source_target_pairs={{0,16},{1,9},{2,18},{3,11},{4,20},{5,13},{6,22},{7,15},{8,24},{9,1... | collective-permute-start | bytes 208904 | tf_op jit(solution)/shard_map/ppermute | solution.py:936
  130.0 1.8 %collective-permute-done.27.outer_third_ref = bf16[1,272,128]{2,1,0:T(8,128)(2,1)S(1)} collective-permute-done((bf16[1,272,128]{2,1,0:T(8,128)(2,1)S(1)}, bf16[1,272,128]{2,1,0:T(8,128)(2,1)S(1)}, u32[]{:S(2)}, u32[]{:S(2)}) %collective-permute-start.27) | collective-permute-done | bytes 69664 | tf_op jit(solution)/shard_map/ppermute | solution.py:936
  (66 shorter events, 17.8 us)
Async XLA Ops:
  1.7 8.4 %collective-permute-start.1 = (bf16[1,9,64,128]{3,2,1,0:T(8,128)(2,1)S(1)}, bf16[1,9,64,128]{3,2,1,0:T(8,128)(2,1)S(1)}, u32[]{:S(2)}, u32[]{:S(2)}) collective-permute-start(bf16[1,9,64,128]{3,2,1,0:T(8,128)(2,1)S(1)} %bitcast.8), channel_id=1, source_target_pairs={{0,16},{1,9},{2,18},{3,11},{4,20},{5,13},{6,22},{7,15},{8,24},{9,1... | collective-permute-start | bytes 442376 | tf_op jit(solution)/shard_map/ppermute | solution.py:906
  10.1 9.8 %collective-permute-start.3 = (bf16[2,9,64,128]{3,2,1,0:T(8,128)(2,1)S(1)}, bf16[2,9,64,128]{3,2,1,0:T(8,128)(2,1)S(1)}, u32[]{:S(2)}, u32[]{:S(2)}) collective-permute-start(bf16[2,9,64,128]{3,2,1,0:T(8,128)(2,1)S(1)} %join.6.first_ref), channel_id=1, source_target_pairs={{0,8},{1,17},{2,10},{3,19},{4,12},{5,21},{6,14},{7,23},{8,0},{9,25... | collective-permute-start | bytes 884744 | tf_op jit(solution)/shard_map/ppermute | solution.py:906
  20.0 12.1 %collective-permute-start.5 = (bf16[4,9,64,128]{3,2,1,0:T(8,128)(2,1)S(1)}, bf16[4,9,64,128]{3,2,1,0:T(8,128)(2,1)S(1)}, u32[]{:S(2)}, u32[]{:S(2)}) collective-permute-start(bf16[4,9,64,128]{3,2,1,0:T(8,128)(2,1)S(1)} %join.8.first_ref), channel_id=1, source_target_pairs={{0,4},{1,3},{2,6},{3,1},{4,0},{5,7},{6,2},{7,5},{8,12},{9,11},{10,... | collective-permute-start | bytes 1769480 | tf_op jit(solution)/shard_map/ppermute | solution.py:906
  21.6 10.5 %collective-permute-start.4 = (bf16[4,272,128]{2,1,0:T(8,128)(2,1)S(1)}, bf16[4,272,128]{2,1,0:T(8,128)(2,1)S(1)}, u32[]{:S(2)}, u32[]{:S(2)}) collective-permute-start(bf16[4,272,128]{2,1,0:T(8,128)(2,1)S(1)} %join.9.first_ref), channel_id=1, source_target_pairs={{0,16},{1,9},{2,18},{3,11},{4,20},{5,13},{6,22},{7,15},{8,24},{9,1... | collective-permute-start | bytes 835592 | tf_op jit(solution)/shard_map/ppermute | solution.py:906
  32.2 17.1 %collective-permute-start.7 = (bf16[8,9,64,128]{3,2,1,0:T(8,128)(2,1)S(1)}, bf16[8,9,64,128]{3,2,1,0:T(8,128)(2,1)S(1)}, u32[]{:S(2)}, u32[]{:S(2)}) collective-permute-start(bf16[8,9,64,128]{3,2,1,0:T(8,128)(2,1)S(1)} %join.10.p0_ref), channel_id=1, source_target_pairs={{0,2},{1,5},{2,0},{3,7},{4,6},{5,1},{6,4},{7,3},{8,10},{9,13},{10,... | collective-permute-start | bytes 3538952 | tf_op jit(solution)/shard_map/ppermute | solution.py:906
  33.8 15.5 %collective-permute-start.6 = (bf16[8,272,128]{2,1,0:T(8,128)(2,1)S(1)}, bf16[8,272,128]{2,1,0:T(8,128)(2,1)S(1)}, u32[]{:S(2)}, u32[]{:S(2)}) collective-permute-start(bf16[8,272,128]{2,1,0:T(8,128)(2,1)S(1)} %join.11.p0_ref), channel_id=1, source_target_pairs={{0,8},{1,17},{2,10},{3,19},{4,12},{5,21},{6,14},{7,23},{8,0},{9,25... | collective-permute-start | bytes 1671176 | tf_op jit(solution)/shard_map/ppermute | solution.py:906
  33.9 15.9 %collective-permute-start.10 = (bf16[8,272,128]{2,1,0:T(8,128)(2,1)S(1)}, bf16[8,272,128]{2,1,0:T(8,128)(2,1)S(1)}, u32[]{:S(2)}, u32[]{:S(2)}) collective-permute-start(bf16[8,272,128]{2,1,0:T(8,128)(2,1)S(1)} %join.11.p0_ref), channel_id=1, source_target_pairs={{0,1},{1,0},{2,3},{3,2},{4,5},{5,4},{6,7},{7,6},{8,9},{9,8},{10,11... | collective-permute-start | bytes 1671176 | tf_op jit(solution)/shard_map/ppermute | solution.py:906
  49.3 9.8 %collective-permute-start.8 = (bf16[8,9,64,128]{3,2,1,0:T(8,128)(2,1)S(1)}, bf16[8,9,64,128]{3,2,1,0:T(8,128)(2,1)S(1)}, u32[]{:S(2)}, u32[]{:S(2)}) collective-permute-start(bf16[8,9,64,128]{3,2,1,0:T(8,128)(2,1)S(1)} %join.10.p0_ref), channel_id=1, source_target_pairs={{0,1},{1,0},{2,3},{3,2},{4,5},{5,4},{6,7},{7,6},{8,9},{9,8},{10,11... | collective-permute-start | bytes 3538952 | tf_op jit(solution)/shard_map/ppermute | solution.py:906
  49.8 9.3 %collective-permute-start.9 = (bf16[8,9,64,128]{3,2,1,0:T(8,128)(2,1)S(1)}, bf16[8,9,64,128]{3,2,1,0:T(8,128)(2,1)S(1)}, u32[]{:S(2)}, u32[]{:S(2)}) collective-permute-start(bf16[8,9,64,128]{3,2,1,0:T(8,128)(2,1)S(1)} %collective-permute-done.7.p1_ref), channel_id=1, source_target_pairs={{0,1},{1,0},{2,3},{3,2},{4,5},{5,4},{6,7},{7,6},{8,9},{9,8},{10,11... | collective-permute-start | bytes 3538952 | tf_op jit(solution)/shard_map/ppermute | solution.py:906
  72.2 10.6 %collective-permute-start.12 = (bf16[16,256,128]{2,1,0:T(8,128)(2,1)S(1)}, bf16[16,256,128]{2,1,0:T(8,128)(2,1)S(1)}, u32[]{:S(2)}, u32[]{:S(2)}) collective-permute-start(bf16[16,256,128]{2,1,0:T(8,128)(2,1)S(1)} %get-tuple-element.114), channel_id=1, source_target_pairs={{0,1},{1,0},{2,3},{3,2},{4,5},{5,4},{6,7},{7,6},{8,9},{9,8},{10,11... | collective-permute-start | bytes 3145736 | tf_op jit(solution)/shard_map/ppermute | solution.py:906
  82.4 9.3 %collective-permute-start.14 = (bf16[16,5,64,128]{3,2,1,0:T(8,128)(2,1)S(1)}, bf16[16,5,64,128]{3,2,1,0:T(8,128)(2,1)S(1)}, u32[]{:S(2)}, u32[]{:S(2)}) collective-permute-start(bf16[16,5,64,128]{3,2,1,0:T(8,128)(2,1)S(1)} %get-tuple-element.118), channel_id=1, source_target_pairs={{0,1},{1,0},{2,3},{3,2},{4,5},{5,4},{6,7},{7,6},{8,9},{9,8},{10,11... | collective-permute-start | bytes 3932168 | tf_op jit(solution)/shard_map/ppermute | solution.py:906
  83.0 9.2 %collective-permute-start.13 = (bf16[8,256,128]{2,1,0:T(8,128)(2,1)S(1)}, bf16[8,256,128]{2,1,0:T(8,128)(2,1)S(1)}, u32[]{:S(2)}, u32[]{:S(2)}) collective-permute-start(bf16[8,256,128]{2,1,0:T(8,128)(2,1)S(1)} %get-tuple-element.157), channel_id=1, source_target_pairs={{0,4},{1,9},{2,6},{3,11},{4,0},{5,13},{6,2},{7,15},{8,12},{9,1},{1... | collective-permute-start | bytes 1572872 | tf_op jit(solution)/shard_map/ppermute | solution.py:906
  92.9 8.5 %collective-permute-start.15 = (bf16[4,256,128]{2,1,0:T(8,128)(2,1)S(1)}, bf16[4,256,128]{2,1,0:T(8,128)(2,1)S(1)}, u32[]{:S(2)}, u32[]{:S(2)}) collective-permute-start(bf16[4,256,128]{2,1,0:T(8,128)(2,1)S(1)} %get-tuple-element.163), channel_id=1, source_target_pairs={{0,8},{1,17},{2,10},{3,19},{4,12},{5,21},{6,14},{7,23},{8,0},{9,25... | collective-permute-start | bytes 786440 | tf_op jit(solution)/shard_map/ppermute | solution.py:906
  93.0 10.7 %collective-permute-start.17 = (bf16[8,5,64,128]{3,2,1,0:T(8,128)(2,1)S(1)}, bf16[8,5,64,128]{3,2,1,0:T(8,128)(2,1)S(1)}, u32[]{:S(2)}, u32[]{:S(2)}) collective-permute-start(bf16[8,5,64,128]{3,2,1,0:T(8,128)(2,1)S(1)} %get-tuple-element.155), channel_id=1, source_target_pairs={{0,2},{1,5},{2,0},{3,7},{4,6},{5,1},{6,4},{7,3},{8,10},{9,13},{10,... | collective-permute-start | bytes 1966088 | tf_op jit(solution)/shard_map/ppermute | solution.py:906
  101.6 13.2 %collective-permute-start.21 = (bf16[8,272,128]{2,1,0:T(8,128)(2,1)S(1)}, bf16[8,272,128]{2,1,0:T(8,128)(2,1)S(1)}, u32[]{:S(2)}, u32[]{:S(2)}) collective-permute-start(bf16[8,272,128]{2,1,0:T(8,128)(2,1)S(1)} %get-tuple-element.165), channel_id=1, source_target_pairs={{0,1},{1,0},{2,3},{3,2},{4,5},{5,4},{6,7},{7,6},{8,9},{9,8},{10,11... | collective-permute-start | bytes 1671176 | tf_op jit(solution)/shard_map/ppermute | solution.py:906
  103.7 11.0 %collective-permute-start.18 = (bf16[8,272,128]{2,1,0:T(8,128)(2,1)S(1)}, bf16[8,272,128]{2,1,0:T(8,128)(2,1)S(1)}, u32[]{:S(2)}, u32[]{:S(2)}) collective-permute-start(bf16[8,272,128]{2,1,0:T(8,128)(2,1)S(1)} %add_convert_fusion.1), channel_id=1, source_target_pairs={{0,2},{1,5},{2,0},{3,7},{4,6},{5,1},{6,4},{7,3},{8,10},{9,13},{10,... | collective-permute-start | bytes 1671176 | tf_op jit(solution)/shard_map/ppermute | solution.py:906
  104.7 10.0 %collective-permute-start.19 = (bf16[4,5,64,128]{3,2,1,0:T(8,128)(2,1)S(1)}, bf16[4,5,64,128]{3,2,1,0:T(8,128)(2,1)S(1)}, u32[]{:S(2)}, u32[]{:S(2)}) collective-permute-start(bf16[4,5,64,128]{3,2,1,0:T(8,128)(2,1)S(1)} %get-tuple-element.160), channel_id=1, source_target_pairs={{0,8},{1,17},{2,10},{3,19},{4,12},{5,21},{6,14},{7,23},{8,0},{9,25... | collective-permute-start | bytes 983048 | tf_op jit(solution)/shard_map/ppermute | solution.py:906
  106.8 8.0 %collective-permute-start.20 = (bf16[2,256,128]{2,1,0:T(8,128)(2,1)S(1)}, bf16[2,256,128]{2,1,0:T(8,128)(2,1)S(1)}, u32[]{:S(2)}, u32[]{:S(2)}) collective-permute-start(bf16[2,256,128]{2,1,0:T(8,128)(2,1)S(1)} %get-tuple-element.174), channel_id=1, source_target_pairs={{0,2},{1,5},{2,0},{3,7},{4,6},{5,1},{6,4},{7,3},{8,10},{9,13},{10,... | collective-permute-start | bytes 393224 | tf_op jit(solution)/shard_map/ppermute | solution.py:906
  115.0 9.4 %collective-permute-start.23 = (bf16[2,5,64,128]{3,2,1,0:T(8,128)(2,1)S(1)}, bf16[2,5,64,128]{3,2,1,0:T(8,128)(2,1)S(1)}, u32[]{:S(2)}, u32[]{:S(2)}) collective-permute-start(bf16[2,5,64,128]{3,2,1,0:T(8,128)(2,1)S(1)} %get-tuple-element.168), channel_id=1, source_target_pairs={{0,16},{1,9},{2,18},{3,11},{4,20},{5,13},{6,22},{7,15},{8,24},{9,1... | collective-permute-start | bytes 491528 | tf_op jit(solution)/shard_map/ppermute | solution.py:906
  117.6 6.8 %collective-permute-start.22 = (bf16[4,272,128]{2,1,0:T(8,128)(2,1)S(1)}, bf16[4,272,128]{2,1,0:T(8,128)(2,1)S(1)}, u32[]{:S(2)}, u32[]{:S(2)}) collective-permute-start(bf16[4,272,128]{2,1,0:T(8,128)(2,1)S(1)} %get-tuple-element.161), channel_id=1, source_target_pairs={{0,4},{1,3},{2,6},{3,1},{4,0},{5,7},{6,2},{7,5},{8,12},{9,11},{10,... | collective-permute-start | bytes 835592 | tf_op jit(solution)/shard_map/ppermute | solution.py:906
  118.6 5.8 %collective-permute-start.24 = (bf16[1,256,128]{2,1,0:T(8,128)(2,1)S(1)}, bf16[1,256,128]{2,1,0:T(8,128)(2,1)S(1)}, u32[]{:S(2)}, u32[]{:S(2)}) collective-permute-start(bf16[1,256,128]{2,1,0:T(8,128)(2,1)S(1)} %get-tuple-element.178), channel_id=1, source_target_pairs={{0,16},{1,3},{2,18},{3,1},{4,20},{5,7},{6,22},{7,5},{8,24},{9,11},... | collective-permute-start | bytes 196616 | tf_op jit(solution)/shard_map/ppermute | solution.py:906
  124.5 8.8 %collective-permute-start.28 = (bf16[1,5,64,128]{3,2,1,0:T(8,128)(2,1)S(1)}, bf16[1,5,64,128]{3,2,1,0:T(8,128)(2,1)S(1)}, u32[]{:S(2)}, u32[]{:S(2)}) collective-permute-start(bf16[1,5,64,128]{3,2,1,0:T(8,128)(2,1)S(1)} %get-tuple-element.175), channel_id=1, source_target_pairs={{0,4},{1,3},{2,6},{3,1},{4,0},{5,7},{6,2},{7,5},{8,12},{9,11},{10,... | collective-permute-start | bytes 245768 | tf_op jit(solution)/shard_map/ppermute | solution.py:906
  125.6 6.2 %collective-permute-start.27 = (bf16[1,272,128]{2,1,0:T(8,128)(2,1)S(1)}, bf16[1,272,128]{2,1,0:T(8,128)(2,1)S(1)}, u32[]{:S(2)}, u32[]{:S(2)}) collective-permute-start(bf16[1,272,128]{2,1,0:T(8,128)(2,1)S(1)} %get-tuple-element.169), channel_id=1, source_target_pairs={{0,24},{1,25},{2,26},{3,27},{4,28},{5,29},{6,30},{7,31},{8,16},{9,... | collective-permute-start | bytes 208904 | tf_op jit(solution)/shard_map/ppermute | solution.py:936
  127.6 5.6 %collective-permute-start.26 = (bf16[1,272,128]{2,1,0:T(8,128)(2,1)S(1)}, bf16[1,272,128]{2,1,0:T(8,128)(2,1)S(1)}, u32[]{:S(2)}, u32[]{:S(2)}) collective-permute-start(bf16[1,272,128]{2,1,0:T(8,128)(2,1)S(1)} %get-tuple-element.170), channel_id=1, source_target_pairs={{0,8},{1,17},{2,10},{3,19},{4,12},{5,21},{6,14},{7,23},{8,0},{9,25... | collective-permute-start | bytes 208904 | tf_op jit(solution)/shard_map/ppermute | solution.py:936
  (8 other events, 87.7 us)

commit v7 on v6

--- a/solution.py
+++ b/solution.py
@@ -274,24 +274,32 @@
     return value, half + value * bend
 
 
-def load_second(me, blocks, w_out, w_in, w_back, sems):
+def load_second(me, blocks, w_in, w_back, sems):
     for block in range(HALF):
         for half in range(2):
             source = blocks[half * 2 + block // 8].at[block % 8]
             wide, narrow = place_of(ORDER_SECOND, me, half, block)
             rows = pl.ds(pl.multiple_of(wide * 64, 64), 64)
             columns = pl.ds(pl.multiple_of(narrow * 128, 128), 128)
-            pltpu.make_async_copy(source.at[0], w_out.at[rows, columns], sems.at[0]).start()
             pltpu.make_async_copy(
-                source.at[pl.ds(1, 4)], w_in.at[pl.ds(narrow * 4, 4), rows, :], sems.at[1]
+                source.at[pl.ds(0, 5)], w_in.at[pl.ds(narrow * 5, 5), rows, :], sems.at[1]
             ).start()
             pltpu.make_async_copy(
                 source.at[pl.ds(5, 4)], w_back.at[pl.ds(wide * 4, 4), :, columns], sems.at[2]
             ).start()
 
 
+def w_in_tile(tile):
+    return tile // 4 * 5 + tile % 4 + 1
+
+
 def w_in_columns(w_in, chunk):
-    return jnp.concatenate([w_in[chunk * 2], w_in[chunk * 2 + 1]], axis=1)
+    tiles = [w_in[w_in_tile(chunk * 2 + side)] for side in range(2)]
+    return jnp.concatenate(tiles, axis=1)
+
+
+def w_out_whole(w_in):
+    return jnp.concatenate([w_in[narrow * 5] for narrow in range(NARROW)], axis=1)
 
 
 def rows_at(step, rows):
@@ -317,7 +325,6 @@
     keep_ref,
     send_ref,
     sums_ref,
-    w_out,
     w_in,
     w_back,
     active,
@@ -326,15 +333,14 @@
 ):
     rows = ROWS
     me = my_place() if direct else jnp.int32(0)
-    load_second(me, (p0_ref, p1_ref, p2_ref, p3_ref), w_out, w_in, w_back, sems)
+    load_second(me, (p0_ref, p1_ref, p2_ref, p3_ref), w_in, w_back, sems)
     sums_ref[...] = jnp.zeros_like(sums_ref)
-    wait_whole(w_out, sems.at[0])
     wait_whole(w_in, sems.at[1])
     wait_whole(w_back, sems.at[2])
 
     def per_rows(step, unused):
         here = rows_at(step, rows)
-        first_sum = passed_ref[here, :] + nn(attended_ref[here, :], w_out[...]) + vec_row(vec_ref, 2)
+        first_sum = passed_ref[here, :] + nn(attended_ref[here, :], w_out_whole(w_in)) + vec_row(vec_ref, 2)
         first_ref[here, :] = first_sum
         hat, unused_scale = norm_parts(first_sum)
         hidden = hat * vec_row(vec_ref, 4) + vec_row(vec_ref, 5)
@@ -394,7 +400,6 @@
     low_t,
     attended_ref,
     vec_ref,
-    w_out,
     w_in,
     w_back,
     grad_first_ref,
@@ -429,7 +434,7 @@
                 row = 2 * (chunk % 4) + part
                 bin_sums_ref[chunk // 4, row : row + 1, :] += sums[:, part * 128 : part * 128 + 128]
         grad_hidden += nt(
-            grad_pre[here, :], jnp.concatenate([w_in[tile] for tile in range(16)], axis=1)
+            grad_pre[here, :], jnp.concatenate([w_in[w_in_tile(tile)] for tile in range(16)], axis=1)
         )
         hat, scale = norm_parts(first_ref[here, :])
         gains = vec_row(vec_ref, 4)
@@ -440,7 +445,7 @@
         sums_ref[0:1, :] += column_sum(branch.astype(F32))
         sums_ref[1:2, :] += column_sum(grad_hidden * hat)
         sums_ref[2:3, :] += column_sum(grad_hidden)
-        grad_attended_ref[here, :] = nt(branch, w_out[...]).astype(BF16)
+        grad_attended_ref[here, :] = nt(branch, w_out_whole(w_in)).astype(BF16)
         return unused
 
     total_rows = attended_ref.shape[0]
@@ -763,12 +768,11 @@
             near((HALF, 256, 128), F32),
             near((HALF, 256, 128), BF16),
             shape((8, 512), F32),
-            near((512, 512), BF16),
-            near((16, 512, 128), BF16),
+            near((20, 512, 128), BF16),
             near((32, 64, 512), BF16),
         ),
         in_specs=[vmem()] * 5 + [hbm()] * 4,
-        out_specs=tuple([vmem()] * 11),
+        out_specs=tuple([vmem()] * 10),
         scratch_shapes=[
             pltpu.VMEM((total, 2048), BF16),
             pltpu.VMEM((NARROW, 128, total), BF16),
@@ -793,7 +797,7 @@
             shape((8, 512), F32),
             shape((2, 8, 128), F32),
         ),
-        in_specs=[vmem()] * 9,
+        in_specs=[vmem()] * 8,
         out_specs=tuple([vmem()] * 6),
         scratch_shapes=[
             pltpu.VMEM((total, 2048), BF16),

time: 134 us -> 134 us (level)
  no operation moved by 1% of the time
where the time goes in v7:
time: 134 us
  waiting for transfers between devices  55.2 us (41%)
  Pallas kernels  46.1 us (34%)
  starting transfers between devices  29.9 us (22%)
  other arithmetic  1.67 us (1%)
    ppermute x26, waiting for transfers between devices, swap(): return lax.ppermute(array, AXES, pairs(order, step))  52 us
    ppermute x26, starting transfers between devices, swap(): return lax.ppermute(array, AXES, pairs(order, step))  25.5 us
    pallas_call x1, Pallas kernels, forward_call(): pl.pallas_call(partial(forward_kernel, direct), out_shape=(shape((total,...  12.9 us
    pallas_call x1, Pallas kernels, backward_call(): pl.pallas_call(partial(backward_kernel, direct), out_shape=(shape((total,...  9.96 us
    pallas_call x1, Pallas kernels, attend_back_call(): pl.pallas_call(partial(attend_back_kernel, direct), out_shape=(shape((tot...  8.04 us
    pallas_call x1, Pallas kernels, attend_call(): pl.pallas_call(partial(attend_kernel, direct), out_shape=(near((total, 15...  7.83 us
    pallas_call x1, Pallas kernels, project_back_call(): pl.pallas_call(partial(project_back_kernel, direct, windows), out_shape=(...  5.29 us
    ppermute x3, starting transfers between devices, scatter_rest(): others.append(lax.ppermute(total, AXES, partners))  4.45 us
  transfers between devices with their start and end apart: 29, of which 13 were waited for; matrix products, arithmetic and copies ran while one was open for 1% of the time, Pallas kernels for 23%

profile of v7, /device:TPU:0, one launch (start us, length us, event | category | flops | bytes accessed | tf_op | source)
XLA Modules:
  0.0 133.9 jit_solution(8761151648437485284)
XLA Ops:
  1.7 4.1 %collective-permute-start.1 = (bf16[1,9,64,128]{3,2,1,0:T(8,128)(2,1)S(1)}, bf16[1,9,64,128]{3,2,1,0:T(8,128)(2,1)S(1)}, u32[]{:S(2)}, u32[]{:S(2)}) collective-permute-start(bf16[1,9,64,128]{3,2,1,0:T(8,128)(2,1)S(1)} %bitcast.8), channel_id=1, source_target_pairs={{0,16},{1,9},{2,18},{3,11},{4,20},{5,13},{6,22},{7,15},{8,24},{9,1... | collective-permute-start | bytes 442376 | tf_op jit(solution)/shard_map/ppermute | solution.py:910
  7.3 2.8 %collective-permute-done.second_ref = bf16[1,272,128]{2,1,0:T(8,128)(2,1)S(1)} collective-permute-done((bf16[1,272,128]{2,1,0:T(8,128)(2,1)S(1)}, bf16[1,272,128]{2,1,0:T(8,128)(2,1)S(1)}, u32[]{:S(2)}, u32[]{:S(2)}) %collective-permute-start) | collective-permute-done | bytes 69664 | tf_op jit(solution)/shard_map/ppermute | solution.py:910
  10.1 1.6 %collective-permute-start.3 = (bf16[2,9,64,128]{3,2,1,0:T(8,128)(2,1)S(1)}, bf16[2,9,64,128]{3,2,1,0:T(8,128)(2,1)S(1)}, u32[]{:S(2)}, u32[]{:S(2)}) collective-permute-start(bf16[2,9,64,128]{3,2,1,0:T(8,128)(2,1)S(1)} %join.6.first_ref), channel_id=1, source_target_pairs={{0,8},{1,17},{2,10},{3,19},{4,12},{5,21},{6,14},{7,23},{8,0},{9,25... | collective-permute-start | bytes 884744 | tf_op jit(solution)/shard_map/ppermute | solution.py:910
  11.8 1.6 %collective-permute-start.2 = (bf16[2,272,128]{2,1,0:T(8,128)(2,1)S(1)}, bf16[2,272,128]{2,1,0:T(8,128)(2,1)S(1)}, u32[]{:S(2)}, u32[]{:S(2)}) collective-permute-start(bf16[2,272,128]{2,1,0:T(8,128)(2,1)S(1)} %join.7.first_ref), channel_id=1, source_target_pairs={{0,2},{1,3},{2,0},{3,1},{4,6},{5,7},{6,4},{7,5},{8,10},{9,11},{10,... | collective-permute-start | bytes 417800 | tf_op jit(solution)/shard_map/ppermute | solution.py:910
  13.3 3.5 %collective-permute-done.2.second_ref = bf16[2,272,128]{2,1,0:T(8,128)(2,1)S(1)} collective-permute-done((bf16[2,272,128]{2,1,0:T(8,128)(2,1)S(1)}, bf16[2,272,128]{2,1,0:T(8,128)(2,1)S(1)}, u32[]{:S(2)}, u32[]{:S(2)}) %collective-permute-start.2) | collective-permute-done | bytes 139296 | tf_op jit(solution)/shard_map/ppermute | solution.py:910
  16.9 3.1 %collective-permute-done.3.second_ref = bf16[2,9,64,128]{3,2,1,0:T(8,128)(2,1)S(1)} collective-permute-done((bf16[2,9,64,128]{3,2,1,0:T(8,128)(2,1)S(1)}, bf16[2,9,64,128]{3,2,1,0:T(8,128)(2,1)S(1)}, u32[]{:S(2)}, u32[]{:S(2)}) %collective-permute-start.3) | collective-permute-done | bytes 294944 | tf_op jit(solution)/shard_map/ppermute | solution.py:910
  20.0 1.6 %collective-permute-start.5 = (bf16[4,9,64,128]{3,2,1,0:T(8,128)(2,1)S(1)}, bf16[4,9,64,128]{3,2,1,0:T(8,128)(2,1)S(1)}, u32[]{:S(2)}, u32[]{:S(2)}) collective-permute-start(bf16[4,9,64,128]{3,2,1,0:T(8,128)(2,1)S(1)} %join.8.first_ref), channel_id=1, source_target_pairs={{0,4},{1,3},{2,6},{3,1},{4,0},{5,7},{6,2},{7,5},{8,12},{9,11},{10,... | collective-permute-start | bytes 1769480 | tf_op jit(solution)/shard_map/ppermute | solution.py:910
  22.7 9.4 %collective-permute-done.4.second_ref = bf16[4,272,128]{2,1,0:T(8,128)(2,1)S(1)} collective-permute-done((bf16[4,272,128]{2,1,0:T(8,128)(2,1)S(1)}, bf16[4,272,128]{2,1,0:T(8,128)(2,1)S(1)}, u32[]{:S(2)}, u32[]{:S(2)}) %collective-permute-start.4) | collective-permute-done | bytes 278560 | tf_op jit(solution)/shard_map/ppermute | solution.py:910
  32.2 1.6 %collective-permute-start.7 = (bf16[8,9,64,128]{3,2,1,0:T(8,128)(2,1)S(1)}, bf16[8,9,64,128]{3,2,1,0:T(8,128)(2,1)S(1)}, u32[]{:S(2)}, u32[]{:S(2)}) collective-permute-start(bf16[8,9,64,128]{3,2,1,0:T(8,128)(2,1)S(1)} %join.10.p0_ref), channel_id=1, source_target_pairs={{0,2},{1,5},{2,0},{3,7},{4,6},{5,1},{6,4},{7,3},{8,10},{9,13},{10,... | collective-permute-start | bytes 3538952 | tf_op jit(solution)/shard_map/ppermute | solution.py:910
  34.0 15.3 %collective-permute-done.6.p1_ref = bf16[8,272,128]{2,1,0:T(8,128)(2,1)S(1)} collective-permute-done((bf16[8,272,128]{2,1,0:T(8,128)(2,1)S(1)}, bf16[8,272,128]{2,1,0:T(8,128)(2,1)S(1)}, u32[]{:S(2)}, u32[]{:S(2)}) %collective-permute-start.6) | collective-permute-done | bytes 557088 | tf_op jit(solution)/shard_map/ppermute | solution.py:910
  51.2 7.8 %attend.1 = (bf16[1024,1536]{1,0:T(8,128)(2,1)S(1)}, bf16[1024,512]{1,0:T(8,128)(2,1)S(1)}, f32[4,2,4,256]{3,2,1,0:T(4,128)S(1)}, f32[1024,512]{1,0:T(8,128)S(1)...) custom-call(s32[2,512]{1,0:T(2,128)S(1)} %copy-done.2, ...), custom_call_target="tpu_custom_call" | custom-call | flops 12582912000 | bytes 12582912 | tf_op jit(solution)/shard_map/attend/pallas_call | solution.py:724
  59.1 12.9 %forward.1 = (bf16[1024,512]{1,0:T(8,128)(2,1)}, f32[1024,2048]{1,0:T(8,128)S(1)}, f32[1024,512]{1,0:T(8,128)S(1)}, f32[1024,512]{1,0:T(8,128)S(1)}, bf16[8,64,1...) custom-call(bf16[1024,512]{1,0:T(8,128)(2,1)S(1)} %get-tuple-element, ...), custom_call_target="tpu_custom_call", output_to_operand_aliasing={{3}: (1, {})} | custom-call | flops 12582912000 | bytes 25165824 | tf_op jit(solution)/shard_map/forward/pallas_call | solution.py:760
  72.2 10.0 %backward.1 = (f32[1024,512]{1,0:T(8,128)S(1)}, bf16[1024,512]{1,0:T(8,128)(2,1)S(1)}, f32[16,5,64,128]{3,2,1,0:T(8,128)S(1)}, bf16[16,5,64,128]{3,2,1,0:T(8,128...) custom-call(f32[1024,2048]{1,0:T(8,128)S(1)} %get-tuple-element.104.slop, ...), custom_call_target="tpu_custom_call", output_to_operand_aliasing={{0}: (1, {}), {1}: (4, {})} | custom-call | flops 14680064000 | bytes 25165824 | tf_op jit(solution)/shard_map/backward/pallas_call | solution.py:790
  83.4 8.0 %attend_back.1 = (bf16[1024,1536]{1,0:T(8,128)(2,1)S(1)}, f32[4,8,128]{2,1,0:T(8,128)S(1)}) custom-call(s32[2,512]{1,0:T(2,128)S(1)} %copy-done.2, bf16[1024,1536]{1,0:T(8,128)(2,1)S(1)} %get-tuple-element.103.qkv_ref, bf16[1024,512]{1,0:T(8,128)(2,1)S(1)} %get-tuple-element.113.grad_attended_ref, f32[4,2,4,256]{3,2,1,0:T(4,128)S(1)} %get-tuple-element.114.lse_ref), custom_call_target="tpu_custom_call" | custom-call | flops 8388608000 | bytes 8388608 | tf_op jit(solution)/shard_map/attend_back/pallas_call | solution.py:825
  93.5 5.3 %project_back.1 = (bf16[1024,512]{1,0:T(8,128)(2,1)}, f32[16,272,128]{2,1,0:T(8,128)S(1)}, bf16[16,272,128]{2,1,0:T(8,128)(2,1)S(1)}) custom-call(bf16[1024,1536]{1,0:T(8,128)(2,1)S(1)} %get-tuple-element.121.grads, bf16[1024,512]{1,0:T(8,128)(2,1)S(1)} %get-tuple-element.122.mixed_ref, f32[1024,512]{1,0:T(8,128)S(1)} %get-tuple-element.123.grad_first_ref, ...), custom_call_target="tpu_custom_call" | custom-call | flops 6291456000 | bytes 8388608 | tf_op jit(solution)/shard_map/project_back/pallas_call | solution.py:839
  98.8 2.4 %collective-permute-done.15 = bf16[4,256,128]{2,1,0:T(8,128)(2,1)S(1)} collective-permute-done((bf16[4,256,128]{2,1,0:T(8,128)(2,1)S(1)}, bf16[4,256,128]{2,1,0:T(8,128)(2,1)S(1)}, u32[]{:S(2)}, u32[]{:S(2)}) %collective-permute-start.15) | collective-permute-done | bytes 262176 | tf_op jit(solution)/shard_map/ppermute | solution.py:910
  101.9 1.5 %collective-permute-done.17 = bf16[8,5,64,128]{3,2,1,0:T(8,128)(2,1)S(1)} collective-permute-done((bf16[8,5,64,128]{3,2,1,0:T(8,128)(2,1)S(1)}, bf16[8,5,64,128]{3,2,1,0:T(8,128)(2,1)S(1)}, u32[]{:S(2)}, u32[]{:S(2)}) %collective-permute-start.17) | collective-permute-done | bytes 655392 | tf_op jit(solution)/shard_map/ppermute | solution.py:910
  104.5 2.0 %collective-permute-start.19 = (bf16[4,5,64,128]{3,2,1,0:T(8,128)(2,1)S(1)}, bf16[4,5,64,128]{3,2,1,0:T(8,128)(2,1)S(1)}, u32[]{:S(2)}, u32[]{:S(2)}) collective-permute-start(bf16[4,5,64,128]{3,2,1,0:T(8,128)(2,1)S(1)} %get-tuple-element.158), channel_id=1, source_target_pairs={{0,8},{1,17},{2,10},{3,19},{4,12},{5,21},{6,14},{7,23},{8,0},{9,25... | collective-permute-start | bytes 983048 | tf_op jit(solution)/shard_map/ppermute | solution.py:910
  108.0 6.6 %collective-permute-done.20 = bf16[2,256,128]{2,1,0:T(8,128)(2,1)S(1)} collective-permute-done((bf16[2,256,128]{2,1,0:T(8,128)(2,1)S(1)}, bf16[2,256,128]{2,1,0:T(8,128)(2,1)S(1)}, u32[]{:S(2)}, u32[]{:S(2)}) %collective-permute-start.20) | collective-permute-done | bytes 131104 | tf_op jit(solution)/shard_map/ppermute | solution.py:910
  114.8 2.5 %collective-permute-start.23 = (bf16[2,5,64,128]{3,2,1,0:T(8,128)(2,1)S(1)}, bf16[2,5,64,128]{3,2,1,0:T(8,128)(2,1)S(1)}, u32[]{:S(2)}, u32[]{:S(2)}) collective-permute-start(bf16[2,5,64,128]{3,2,1,0:T(8,128)(2,1)S(1)} %get-tuple-element.166), channel_id=1, source_target_pairs={{0,16},{1,9},{2,18},{3,11},{4,20},{5,13},{6,22},{7,15},{8,24},{9,1... | collective-permute-start | bytes 491528 | tf_op jit(solution)/shard_map/ppermute | solution.py:910
  118.9 5.3 %collective-permute-done.24.back_came_ref = bf16[1,256,128]{2,1,0:T(8,128)(2,1)S(1)} collective-permute-done((bf16[1,256,128]{2,1,0:T(8,128)(2,1)S(1)}, bf16[1,256,128]{2,1,0:T(8,128)(2,1)S(1)}, u32[]{:S(2)}, u32[]{:S(2)}) %collective-permute-start.24) | collective-permute-done | bytes 65568 | tf_op jit(solution)/shard_map/ppermute | solution.py:910
  125.4 2.1 %collective-permute-start.27 = (bf16[1,272,128]{2,1,0:T(8,128)(2,1)S(1)}, bf16[1,272,128]{2,1,0:T(8,128)(2,1)S(1)}, u32[]{:S(2)}, u32[]{:S(2)}) collective-permute-start(bf16[1,272,128]{2,1,0:T(8,128)(2,1)S(1)} %get-tuple-element.167), channel_id=1, source_target_pairs={{0,24},{1,25},{2,26},{3,27},{4,28},{5,29},{6,30},{7,31},{8,16},{9,... | collective-permute-start | bytes 208904 | tf_op jit(solution)/shard_map/ppermute | solution.py:940
  127.4 2.4 %collective-permute-start.25 = (bf16[1,272,128]{2,1,0:T(8,128)(2,1)S(1)}, bf16[1,272,128]{2,1,0:T(8,128)(2,1)S(1)}, u32[]{:S(2)}, u32[]{:S(2)}) collective-permute-start(bf16[1,272,128]{2,1,0:T(8,128)(2,1)S(1)} %get-tuple-element.169), channel_id=1, source_target_pairs={{0,16},{1,9},{2,18},{3,11},{4,20},{5,13},{6,22},{7,15},{8,24},{9,1... | collective-permute-start | bytes 208904 | tf_op jit(solution)/shard_map/ppermute | solution.py:940
  129.8 1.8 %collective-permute-done.27.outer_third_ref = bf16[1,272,128]{2,1,0:T(8,128)(2,1)S(1)} collective-permute-done((bf16[1,272,128]{2,1,0:T(8,128)(2,1)S(1)}, bf16[1,272,128]{2,1,0:T(8,128)(2,1)S(1)}, u32[]{:S(2)}, u32[]{:S(2)}) %collective-permute-start.27) | collective-permute-done | bytes 69664 | tf_op jit(solution)/shard_map/ppermute | solution.py:940
  (66 shorter events, 17.8 us)
Async XLA Ops:
  1.7 8.4 %collective-permute-start.1 = (bf16[1,9,64,128]{3,2,1,0:T(8,128)(2,1)S(1)}, bf16[1,9,64,128]{3,2,1,0:T(8,128)(2,1)S(1)}, u32[]{:S(2)}, u32[]{:S(2)}) collective-permute-start(bf16[1,9,64,128]{3,2,1,0:T(8,128)(2,1)S(1)} %bitcast.8), channel_id=1, source_target_pairs={{0,16},{1,9},{2,18},{3,11},{4,20},{5,13},{6,22},{7,15},{8,24},{9,1... | collective-permute-start | bytes 442376 | tf_op jit(solution)/shard_map/ppermute | solution.py:910
  10.1 9.8 %collective-permute-start.3 = (bf16[2,9,64,128]{3,2,1,0:T(8,128)(2,1)S(1)}, bf16[2,9,64,128]{3,2,1,0:T(8,128)(2,1)S(1)}, u32[]{:S(2)}, u32[]{:S(2)}) collective-permute-start(bf16[2,9,64,128]{3,2,1,0:T(8,128)(2,1)S(1)} %join.6.first_ref), channel_id=1, source_target_pairs={{0,8},{1,17},{2,10},{3,19},{4,12},{5,21},{6,14},{7,23},{8,0},{9,25... | collective-permute-start | bytes 884744 | tf_op jit(solution)/shard_map/ppermute | solution.py:910
  20.0 12.1 %collective-permute-start.5 = (bf16[4,9,64,128]{3,2,1,0:T(8,128)(2,1)S(1)}, bf16[4,9,64,128]{3,2,1,0:T(8,128)(2,1)S(1)}, u32[]{:S(2)}, u32[]{:S(2)}) collective-permute-start(bf16[4,9,64,128]{3,2,1,0:T(8,128)(2,1)S(1)} %join.8.first_ref), channel_id=1, source_target_pairs={{0,4},{1,3},{2,6},{3,1},{4,0},{5,7},{6,2},{7,5},{8,12},{9,11},{10,... | collective-permute-start | bytes 1769480 | tf_op jit(solution)/shard_map/ppermute | solution.py:910
  21.6 10.5 %collective-permute-start.4 = (bf16[4,272,128]{2,1,0:T(8,128)(2,1)S(1)}, bf16[4,272,128]{2,1,0:T(8,128)(2,1)S(1)}, u32[]{:S(2)}, u32[]{:S(2)}) collective-permute-start(bf16[4,272,128]{2,1,0:T(8,128)(2,1)S(1)} %join.9.first_ref), channel_id=1, source_target_pairs={{0,16},{1,9},{2,18},{3,11},{4,20},{5,13},{6,22},{7,15},{8,24},{9,1... | collective-permute-start | bytes 835592 | tf_op jit(solution)/shard_map/ppermute | solution.py:910
  32.2 17.1 %collective-permute-start.7 = (bf16[8,9,64,128]{3,2,1,0:T(8,128)(2,1)S(1)}, bf16[8,9,64,128]{3,2,1,0:T(8,128)(2,1)S(1)}, u32[]{:S(2)}, u32[]{:S(2)}) collective-permute-start(bf16[8,9,64,128]{3,2,1,0:T(8,128)(2,1)S(1)} %join.10.p0_ref), channel_id=1, source_target_pairs={{0,2},{1,5},{2,0},{3,7},{4,6},{5,1},{6,4},{7,3},{8,10},{9,13},{10,... | collective-permute-start | bytes 3538952 | tf_op jit(solution)/shard_map/ppermute | solution.py:910
  33.8 15.5 %collective-permute-start.6 = (bf16[8,272,128]{2,1,0:T(8,128)(2,1)S(1)}, bf16[8,272,128]{2,1,0:T(8,128)(2,1)S(1)}, u32[]{:S(2)}, u32[]{:S(2)}) collective-permute-start(bf16[8,272,128]{2,1,0:T(8,128)(2,1)S(1)} %join.11.p0_ref), channel_id=1, source_target_pairs={{0,8},{1,17},{2,10},{3,19},{4,12},{5,21},{6,14},{7,23},{8,0},{9,25... | collective-permute-start | bytes 1671176 | tf_op jit(solution)/shard_map/ppermute | solution.py:910
  33.9 15.9 %collective-permute-start.10 = (bf16[8,272,128]{2,1,0:T(8,128)(2,1)S(1)}, bf16[8,272,128]{2,1,0:T(8,128)(2,1)S(1)}, u32[]{:S(2)}, u32[]{:S(2)}) collective-permute-start(bf16[8,272,128]{2,1,0:T(8,128)(2,1)S(1)} %join.11.p0_ref), channel_id=1, source_target_pairs={{0,1},{1,0},{2,3},{3,2},{4,5},{5,4},{6,7},{7,6},{8,9},{9,8},{10,11... | collective-permute-start | bytes 1671176 | tf_op jit(solution)/shard_map/ppermute | solution.py:910
  49.3 9.8 %collective-permute-start.8 = (bf16[8,9,64,128]{3,2,1,0:T(8,128)(2,1)S(1)}, bf16[8,9,64,128]{3,2,1,0:T(8,128)(2,1)S(1)}, u32[]{:S(2)}, u32[]{:S(2)}) collective-permute-start(bf16[8,9,64,128]{3,2,1,0:T(8,128)(2,1)S(1)} %join.10.p0_ref), channel_id=1, source_target_pairs={{0,1},{1,0},{2,3},{3,2},{4,5},{5,4},{6,7},{7,6},{8,9},{9,8},{10,11... | collective-permute-start | bytes 3538952 | tf_op jit(solution)/shard_map/ppermute | solution.py:910
  49.8 9.3 %collective-permute-start.9 = (bf16[8,9,64,128]{3,2,1,0:T(8,128)(2,1)S(1)}, bf16[8,9,64,128]{3,2,1,0:T(8,128)(2,1)S(1)}, u32[]{:S(2)}, u32[]{:S(2)}) collective-permute-start(bf16[8,9,64,128]{3,2,1,0:T(8,128)(2,1)S(1)} %collective-permute-done.7.p1_ref), channel_id=1, source_target_pairs={{0,1},{1,0},{2,3},{3,2},{4,5},{5,4},{6,7},{7,6},{8,9},{9,8},{10,11... | collective-permute-start | bytes 3538952 | tf_op jit(solution)/shard_map/ppermute | solution.py:910
  72.0 10.5 %collective-permute-start.12 = (bf16[16,256,128]{2,1,0:T(8,128)(2,1)S(1)}, bf16[16,256,128]{2,1,0:T(8,128)(2,1)S(1)}, u32[]{:S(2)}, u32[]{:S(2)}) collective-permute-start(bf16[16,256,128]{2,1,0:T(8,128)(2,1)S(1)} %get-tuple-element.112), channel_id=1, source_target_pairs={{0,1},{1,0},{2,3},{3,2},{4,5},{5,4},{6,7},{7,6},{8,9},{9,8},{10,11... | collective-permute-start | bytes 3145736 | tf_op jit(solution)/shard_map/ppermute | solution.py:910
  82.2 9.3 %collective-permute-start.14 = (bf16[16,5,64,128]{3,2,1,0:T(8,128)(2,1)S(1)}, bf16[16,5,64,128]{3,2,1,0:T(8,128)(2,1)S(1)}, u32[]{:S(2)}, u32[]{:S(2)}) collective-permute-start(bf16[16,5,64,128]{3,2,1,0:T(8,128)(2,1)S(1)} %get-tuple-element.116), channel_id=1, source_target_pairs={{0,1},{1,0},{2,3},{3,2},{4,5},{5,4},{6,7},{7,6},{8,9},{9,8},{10,11... | collective-permute-start | bytes 3932168 | tf_op jit(solution)/shard_map/ppermute | solution.py:910
  82.8 9.2 %collective-permute-start.13 = (bf16[8,256,128]{2,1,0:T(8,128)(2,1)S(1)}, bf16[8,256,128]{2,1,0:T(8,128)(2,1)S(1)}, u32[]{:S(2)}, u32[]{:S(2)}) collective-permute-start(bf16[8,256,128]{2,1,0:T(8,128)(2,1)S(1)} %get-tuple-element.155), channel_id=1, source_target_pairs={{0,4},{1,9},{2,6},{3,11},{4,0},{5,13},{6,2},{7,15},{8,12},{9,1},{1... | collective-permute-start | bytes 1572872 | tf_op jit(solution)/shard_map/ppermute | solution.py:910
  92.7 8.5 %collective-permute-start.15 = (bf16[4,256,128]{2,1,0:T(8,128)(2,1)S(1)}, bf16[4,256,128]{2,1,0:T(8,128)(2,1)S(1)}, u32[]{:S(2)}, u32[]{:S(2)}) collective-permute-start(bf16[4,256,128]{2,1,0:T(8,128)(2,1)S(1)} %get-tuple-element.161), channel_id=1, source_target_pairs={{0,8},{1,17},{2,10},{3,19},{4,12},{5,21},{6,14},{7,23},{8,0},{9,25... | collective-permute-start | bytes 786440 | tf_op jit(solution)/shard_map/ppermute | solution.py:910
  92.8 10.7 %collective-permute-start.17 = (bf16[8,5,64,128]{3,2,1,0:T(8,128)(2,1)S(1)}, bf16[8,5,64,128]{3,2,1,0:T(8,128)(2,1)S(1)}, u32[]{:S(2)}, u32[]{:S(2)}) collective-permute-start(bf16[8,5,64,128]{3,2,1,0:T(8,128)(2,1)S(1)} %get-tuple-element.153), channel_id=1, source_target_pairs={{0,2},{1,5},{2,0},{3,7},{4,6},{5,1},{6,4},{7,3},{8,10},{9,13},{10,... | collective-permute-start | bytes 1966088 | tf_op jit(solution)/shard_map/ppermute | solution.py:910
  101.4 13.2 %collective-permute-start.21 = (bf16[8,272,128]{2,1,0:T(8,128)(2,1)S(1)}, bf16[8,272,128]{2,1,0:T(8,128)(2,1)S(1)}, u32[]{:S(2)}, u32[]{:S(2)}) collective-permute-start(bf16[8,272,128]{2,1,0:T(8,128)(2,1)S(1)} %get-tuple-element.163), channel_id=1, source_target_pairs={{0,1},{1,0},{2,3},{3,2},{4,5},{5,4},{6,7},{7,6},{8,9},{9,8},{10,11... | collective-permute-start | bytes 1671176 | tf_op jit(solution)/shard_map/ppermute | solution.py:910
  103.5 11.0 %collective-permute-start.18 = (bf16[8,272,128]{2,1,0:T(8,128)(2,1)S(1)}, bf16[8,272,128]{2,1,0:T(8,128)(2,1)S(1)}, u32[]{:S(2)}, u32[]{:S(2)}) collective-permute-start(bf16[8,272,128]{2,1,0:T(8,128)(2,1)S(1)} %add_convert_fusion.1), channel_id=1, source_target_pairs={{0,2},{1,5},{2,0},{3,7},{4,6},{5,1},{6,4},{7,3},{8,10},{9,13},{10,... | collective-permute-start | bytes 1671176 | tf_op jit(solution)/shard_map/ppermute | solution.py:910
  104.5 10.1 %collective-permute-start.19 = (bf16[4,5,64,128]{3,2,1,0:T(8,128)(2,1)S(1)}, bf16[4,5,64,128]{3,2,1,0:T(8,128)(2,1)S(1)}, u32[]{:S(2)}, u32[]{:S(2)}) collective-permute-start(bf16[4,5,64,128]{3,2,1,0:T(8,128)(2,1)S(1)} %get-tuple-element.158), channel_id=1, source_target_pairs={{0,8},{1,17},{2,10},{3,19},{4,12},{5,21},{6,14},{7,23},{8,0},{9,25... | collective-permute-start | bytes 983048 | tf_op jit(solution)/shard_map/ppermute | solution.py:910
  106.6 8.0 %collective-permute-start.20 = (bf16[2,256,128]{2,1,0:T(8,128)(2,1)S(1)}, bf16[2,256,128]{2,1,0:T(8,128)(2,1)S(1)}, u32[]{:S(2)}, u32[]{:S(2)}) collective-permute-start(bf16[2,256,128]{2,1,0:T(8,128)(2,1)S(1)} %get-tuple-element.172), channel_id=1, source_target_pairs={{0,2},{1,5},{2,0},{3,7},{4,6},{5,1},{6,4},{7,3},{8,10},{9,13},{10,... | collective-permute-start | bytes 393224 | tf_op jit(solution)/shard_map/ppermute | solution.py:910
  114.8 9.4 %collective-permute-start.23 = (bf16[2,5,64,128]{3,2,1,0:T(8,128)(2,1)S(1)}, bf16[2,5,64,128]{3,2,1,0:T(8,128)(2,1)S(1)}, u32[]{:S(2)}, u32[]{:S(2)}) collective-permute-start(bf16[2,5,64,128]{3,2,1,0:T(8,128)(2,1)S(1)} %get-tuple-element.166), channel_id=1, source_target_pairs={{0,16},{1,9},{2,18},{3,11},{4,20},{5,13},{6,22},{7,15},{8,24},{9,1... | collective-permute-start | bytes 491528 | tf_op jit(solution)/shard_map/ppermute | solution.py:910
  117.4 6.8 %collective-permute-start.22 = (bf16[4,272,128]{2,1,0:T(8,128)(2,1)S(1)}, bf16[4,272,128]{2,1,0:T(8,128)(2,1)S(1)}, u32[]{:S(2)}, u32[]{:S(2)}) collective-permute-start(bf16[4,272,128]{2,1,0:T(8,128)(2,1)S(1)} %get-tuple-element.159), channel_id=1, source_target_pairs={{0,4},{1,3},{2,6},{3,1},{4,0},{5,7},{6,2},{7,5},{8,12},{9,11},{10,... | collective-permute-start | bytes 835592 | tf_op jit(solution)/shard_map/ppermute | solution.py:910
  118.4 5.8 %collective-permute-start.24 = (bf16[1,256,128]{2,1,0:T(8,128)(2,1)S(1)}, bf16[1,256,128]{2,1,0:T(8,128)(2,1)S(1)}, u32[]{:S(2)}, u32[]{:S(2)}) collective-permute-start(bf16[1,256,128]{2,1,0:T(8,128)(2,1)S(1)} %get-tuple-element.176), channel_id=1, source_target_pairs={{0,16},{1,3},{2,18},{3,1},{4,20},{5,7},{6,22},{7,5},{8,24},{9,11},... | collective-permute-start | bytes 196616 | tf_op jit(solution)/shard_map/ppermute | solution.py:910
  124.3 8.8 %collective-permute-start.28 = (bf16[1,5,64,128]{3,2,1,0:T(8,128)(2,1)S(1)}, bf16[1,5,64,128]{3,2,1,0:T(8,128)(2,1)S(1)}, u32[]{:S(2)}, u32[]{:S(2)}) collective-permute-start(bf16[1,5,64,128]{3,2,1,0:T(8,128)(2,1)S(1)} %get-tuple-element.173), channel_id=1, source_target_pairs={{0,4},{1,3},{2,6},{3,1},{4,0},{5,7},{6,2},{7,5},{8,12},{9,11},{10,... | collective-permute-start | bytes 245768 | tf_op jit(solution)/shard_map/ppermute | solution.py:910
  125.4 6.2 %collective-permute-start.27 = (bf16[1,272,128]{2,1,0:T(8,128)(2,1)S(1)}, bf16[1,272,128]{2,1,0:T(8,128)(2,1)S(1)}, u32[]{:S(2)}, u32[]{:S(2)}) collective-permute-start(bf16[1,272,128]{2,1,0:T(8,128)(2,1)S(1)} %get-tuple-element.167), channel_id=1, source_target_pairs={{0,24},{1,25},{2,26},{3,27},{4,28},{5,29},{6,30},{7,31},{8,16},{9,... | collective-permute-start | bytes 208904 | tf_op jit(solution)/shard_map/ppermute | solution.py:940
  127.4 5.6 %collective-permute-start.26 = (bf16[1,272,128]{2,1,0:T(8,128)(2,1)S(1)}, bf16[1,272,128]{2,1,0:T(8,128)(2,1)S(1)}, u32[]{:S(2)}, u32[]{:S(2)}) collective-permute-start(bf16[1,272,128]{2,1,0:T(8,128)(2,1)S(1)} %get-tuple-element.168), channel_id=1, source_target_pairs={{0,8},{1,17},{2,10},{3,19},{4,12},{5,21},{6,14},{7,23},{8,0},{9,25... | collective-permute-start | bytes 208904 | tf_op jit(solution)/shard_map/ppermute | solution.py:940
  (8 other events, 87.7 us)
